TPU v7x, 32 devices: a whole 2x2x4 slice. The times are simulated.
32 devices in a mesh: scene: 2 (over y), row: 4 (over z), col: 2 (over x), mode: 2 (over core).
Axes of the slice: x: 2, y: 2, z: 4, core: 2. Of those that a mesh axis runs over, the one named last changes fastest.
Arguments:
- object_field: float32 [4, 2048, 1024], P('scene', 'row', 'col'), parts along dimension 0, may hold values from -4 to 4
- probe_modes: float32 [16, 2, 256, 256], P(('scene', 'mode')), parts along dimension 0, may hold values from -1 to 1
- amplitudes: float32 [8, 2, 2, 256, 256], P(('scene', 'row'), 'col'), parts along dimension 0, may hold values from 0.2 to 2
- positions: int32 [8, 2, 2, 2], P(('scene', 'row'), 'col'), parts along dimension 0, may hold values from 0 to 512, as said below
- counts: int32 [8, 2], P(('scene', 'row'), 'col'), parts along dimension 0, may hold values from 1 to 2, as said below
Outputs:
- object_grad: float32 [4, 2048, 1024], P(('scene', 'mode'), 'row', 'col'), parts along dimension 0
- probe_grad: float32 [16, 2, 256, 256], P(('scene', 'mode')), parts along dimension 0
There are 2 independent parts, one for each index of `scene`. A program takes and returns all parts, laid end to end along the dimension named above; each array names one. Nothing has to cross between parts.
Inputs may be any that keep to these rules, and one draw needn't show every extreme that they name: `positions`: row and column offset of a slot's 256 x 256 patch in its tile's frame widened by 128 cells on every side; slots at or beyond the tile's count are ignored. Slots 0 to counts - 1 of a tile are live.
All inputs are finite; a program needn't handle non-finite values.
Results may differ from a plain program's by a relative error of at most 0.0075.
Values sent between devices are 32-bit elements; how exact they have to be, the bound alone decides.
No kernel may reach another device: no remote copies, remote signals or barrier semaphores. Data moves between devices by JAX's collectives and lax.ppermute only.
A program may use at most 128 MiB of HBM per device.

v0:
```python
import math

import jax
import jax.numpy as jnp
from jax import lax
from jax.sharding import PartitionSpec as P

damping = 0.1


def extended(cells, sides, width):
    for axis, dim in sides:
        count = lax.axis_size(axis)
        ends = count - 1
        head = lax.slice_in_dim(cells, 0, width, axis=dim)
        tail = lax.slice_in_dim(cells, cells.shape[dim] - width, cells.shape[dim], axis=dim)
        cells = jnp.concatenate(
            [
                lax.ppermute(tail, axis, [(i, (i + 1) % count) for i in range(ends)]),
                cells,
                lax.ppermute(head, axis, [((i + 1) % count, i) for i in range(ends)]),
            ],
            axis=dim,
        )
    return cells


def dft_tables(patch_size, direction):
    indices = jnp.arange(patch_size, dtype=jnp.int32)
    product = indices[:, None] * indices[None, :] % patch_size
    angles = 2.0 * math.pi / patch_size * product.astype(jnp.float32)
    norm_scale = 1.0 / math.sqrt(patch_size)
    real_part = (jnp.cos(angles) * norm_scale).astype(jnp.bfloat16)
    imag_part = (-direction * jnp.sin(angles) * norm_scale).astype(jnp.bfloat16)
    upper_rows = jnp.stack([real_part, -imag_part], axis=1)
    lower_rows = jnp.stack([imag_part, real_part], axis=1)
    left_table = jnp.stack([upper_rows, lower_rows], axis=0)
    right_table = jnp.transpose(left_table, (2, 3, 0, 1))
    return (left_table, right_table)


def transform(wave_field, left_table, right_table):
    halfway = jnp.einsum(
        "dick,mckj->mdij", left_table, wave_field, preferred_element_type=jnp.float32
    ).astype(jnp.bfloat16)
    return jnp.einsum("mcij,cjdl->mdil", halfway, right_table, preferred_element_type=jnp.float32)


def complex_product(left_term, right_term):
    left_real, left_imag = (left_term[..., 0, :, :], left_term[..., 1, :, :])
    right_real, right_imag = (right_term[..., 0, :, :], right_term[..., 1, :, :])
    return jnp.stack(
        [
            left_real * right_real - left_imag * right_imag,
            left_real * right_imag + left_imag * right_real,
        ],
        axis=-3,
    )


def conj_product(left_term, right_term):
    left_real, left_imag = (left_term[..., 0, :, :], left_term[..., 1, :, :])
    right_real, right_imag = (right_term[..., 0, :, :], right_term[..., 1, :, :])
    return jnp.stack(
        [
            left_real * right_real + left_imag * right_imag,
            left_real * right_imag - left_imag * right_real,
        ],
        axis=-3,
    )


def forward_pass(patches, probe_modes, left_table, right_table):
    exit_wave = complex_product(probe_modes[None], patches[:, None]).astype(jnp.bfloat16)
    shape_all = exit_wave.shape
    flattened = exit_wave.reshape((-1,) + shape_all[2:])
    return transform(flattened, left_table, right_table).reshape(shape_all)


def backward_pass(spectrum, weight, patches, probe_modes, left_table, right_table):
    back_hat = (weight[:, None, None] * spectrum).astype(jnp.bfloat16)
    shape_all = back_hat.shape
    flattened = back_hat.reshape((-1,) + shape_all[2:])
    back_wave = transform(flattened, left_table, right_table).reshape(shape_all)
    object_terms = jnp.sum(conj_product(probe_modes[None], back_wave), axis=1)
    probe_term = jnp.sum(conj_product(patches[:, None], back_wave), axis=0)
    return (object_terms, probe_term)


def fold_edges(outer_grid, dimension, margin, interior):
    extent = outer_grid.shape[dimension]
    middle = lax.slice_in_dim(outer_grid, 2 * margin, 2 * margin + interior, axis=dimension)
    leading = lax.slice_in_dim(outer_grid, 0, margin, axis=dimension)
    trailing = lax.slice_in_dim(outer_grid, extent - margin, extent, axis=dimension)
    pad_leading = [(0, 0)] * outer_grid.ndim
    pad_leading[dimension] = (0, interior - margin)
    pad_trailing = [(0, 0)] * outer_grid.ndim
    pad_trailing[dimension] = (interior - margin, 0)
    return middle + jnp.pad(leading, pad_leading) + jnp.pad(trailing, pad_trailing)


def shards(object_field, probe_modes, amplitudes, positions, counts):
    patch_size = probe_modes.shape[-1]
    margin = patch_size // 2
    tile_size = object_field.shape[-1]
    slot_count = positions.shape[2]
    forward_left, forward_right = dft_tables(patch_size, 1.0)
    inverse_left, inverse_right = dft_tables(patch_size, -1.0)
    padded = extended(object_field, (("row", 1), ("col", 2)), margin)
    anchor = jnp.zeros((), jnp.int32)
    my_count = counts[0, 0]
    empty_grid = jnp.zeros(padded.shape, jnp.float32)

    def cut_patch(offset):
        return lax.dynamic_slice(
            padded, (anchor, offset[0], offset[1]), (2, patch_size, patch_size)
        )

    def visit_slot(slot_index, running):
        gradient_grid, probe_total = running
        offset = positions[0, 0, slot_index]
        patches = cut_patch(offset)[None]
        active = (slot_index < my_count).astype(jnp.float32)
        spectrum = forward_pass(patches, probe_modes, forward_left, forward_right)
        local_power = jnp.sum(spectrum * spectrum, axis=(1, 2))
        total_power = lax.psum(local_power, "mode")
        weight = active * (
            1.0 - amplitudes[0, 0, slot_index][None] / jnp.sqrt(total_power + damping)
        )
        object_terms, probe_term = backward_pass(
            spectrum, weight, patches, probe_modes, inverse_left, inverse_right
        )
        current = lax.dynamic_slice(
            gradient_grid, (anchor, offset[0], offset[1]), (2, patch_size, patch_size)
        )
        gradient_grid = lax.dynamic_update_slice(
            gradient_grid, current + object_terms[0], (anchor, offset[0], offset[1])
        )
        return (gradient_grid, probe_total + probe_term)

    start_state = (empty_grid, jnp.zeros(probe_modes.shape, jnp.float32))
    gradient_grid, probe_total = lax.fori_loop(0, slot_count, visit_slot, start_state)
    outer_grid = extended(gradient_grid, (("row", 1), ("col", 2)), margin)
    folded = fold_edges(fold_edges(outer_grid, 1, margin, tile_size), 2, margin, tile_size)
    object_grad = lax.psum_scatter(folded, "mode", scatter_dimension=0, tiled=True)
    probe_sum = lax.psum(probe_total, ("row", "col"))
    probe_grad = probe_sum * (1.0 / math.sqrt(lax.axis_size("row") * lax.axis_size("col")))
    return (object_grad, probe_grad)


def solution(mesh):
    return jax.shard_map(
        shards,
        mesh=mesh,
        in_specs=(
            P("scene", "row", "col"),
            P(("scene", "mode"), None, None, None),
            P(("scene", "row"), "col", None, None, None),
            P(("scene", "row"), "col", None, None),
            P(("scene", "row"), "col"),
        ),
        out_specs=(P(("scene", "mode"), "row", "col"), P(("scene", "mode"), None, None, None)),
        check_vma=False,
    )
```

profile of v0, /device:TPU:0, one launch (start us, length us, event | category | flops | bytes accessed | tf_op | source)
XLA Modules:
  0.0 319.3 jit_solution(6419787103646912841)
XLA Ops:
  8.0 1.4 fusion.58
  9.4 5.0 %collective-permute-start = (f32[2,128,512]{2,1,0:T(8,128)S(1)}, f32[2,128,512]{2,1,0:T(8,128)S(1)}, u32[]{:S(2)}, u32[]{:S(2)}) collective-permute-start(f32[2,128,512]{2,1,0:T(8,128)S(1)} %get-tuple-element.308), channel_id=1, source_target_pairs={{0,4},{4,8},{8,12},{1,5},{5,9},{9,13},{2,6},{6,10},{10,14},{3,7},{... | collective-permute-start | bytes 1572872 | tf_op jit(solution)/shard_map/ppermute | solution.py:19
  14.4 1.3 collective-permute-start.1
  15.7 9.8 %collective-permute-done = f32[2,128,512]{2,1,0:T(8,128)S(1)} collective-permute-done((f32[2,128,512]{2,1,0:T(8,128)S(1)}, f32[2,128,512]{2,1,0:T(8,128)S(1)}, u32[]{:S(2)}, u32[]{:S(2)}) %collective-permute-start) | collective-permute-done | bytes 524320 | tf_op jit(solution)/shard_map/ppermute | solution.py:19
  25.8 3.9 %collective-permute-done.1 = f32[2,128,512]{2,1,0:T(8,128)S(1)} collective-permute-done((f32[2,128,512]{2,1,0:T(8,128)S(1)}, f32[2,128,512]{2,1,0:T(8,128)S(1)}, u32[]{:S(2)}, u32[]{:S(2)}) %collective-permute-start.1) | collective-permute-done | bytes 524320 | tf_op jit(solution)/shard_map/ppermute | solution.py:21
  29.7 1.6 copy-done.5
  31.4 1.2 fusion.57
  32.6 3.4 %collective-permute-start.2 = (f32[2,768,128]{2,1,0:T(8,128)}, f32[2,768,128]{2,1,0:T(8,128)S(1)}, u32[]{:S(2)}, u32[]{:S(2)}) collective-permute-start(f32[2,768,128]{2,1,0:T(8,128)} %get-tuple-element.305), channel_id=1, source_target_pairs={{0,2},{1,3},{4,6},{5,7},{8,10},{9,11},{12,14},{13,15},{16,18},{17,... | collective-permute-start | bytes 2359304 | tf_op jit(solution)/shard_map/ppermute | solution.py:19
  36.1 1.3 collective-permute-start.3
  37.4 1.0 fusion.47
  38.4 1.0 fusion.46
  39.4 1.0 multiply_convert_fusion.2
  40.3 1.0 multiply_convert_fusion.1
  41.3 1.0 multiply_convert_fusion
  42.6 1.0 copy.32
  43.6 1.3 copy.31
  44.9 1.3 copy.29
  46.3 1.0 copy.30
  47.3 1.8 copy.28
  49.1 2.8 collective-permute-done.2
  51.9 4.2 %collective-permute-done.3 = f32[2,768,128]{2,1,0:T(8,128)} collective-permute-done((f32[2,768,128]{2,1,0:T(8,128)}, f32[2,768,128]{2,1,0:T(8,128)}, u32[]{:S(2)}, u32[]{:S(2)}) %collective-permute-start.3) | collective-permute-done | bytes 786464 | tf_op jit(solution)/shard_map/ppermute | solution.py:21
  56.1 4.6 %pad_maximum_fusion.1 = f32[2,768,768]{2,1,0:T(8,128)} fusion(f32[2,768,128]{2,1,0:T(8,128)} %collective-permute-done.3, f32[2,768,512]{2,1,0:T(8,128)} %copy-done.5, f32[2,768,128]{2,1,0:T(8,128)S(1)} %collective-permute-done.2), kind=kLoop, calls=%fused_computation.50 | loop fusion | flops 2359296 | bytes 9437184 | tf_op jit(solution)/shard_map/concatenate | solution.py:17
  60.7 2.5 broadcast_in_dim.29
  63.2 103.7 %while.16 = (s32[]{:T(128)}, f32[2,768,768]{2,1,0:T(8,128)}, f32[4,2,256,256]{3,2,1,0:T(8,128)}, s32[1,1,2,2]{3,2,1,0:T(2,128)S(1)}, f32[4,2,256,256]{3,2,0,1:T(...) while((s32[]{:T(128)}, f32[2,768,768]{2,1,0:T(8,128)}, ...), condition=%wide.region_4.5_spmd.clone, body=%wide.region_0.4_spmd.clone.sunk | while | flops 2159280128 | bytes 55837072 | solution.py:142
  63.2 0.6 fusion.76
  67.5 1.4 dynamic-slice_bitcast_fusion.2
  69.1 1.0 fusion.77
  70.1 4.7 %fusion.79 = (f32[256,256]{1,0:T(8,128)}, f32[4,256,2,256,1]{3,1,4,2,0:T(8,128)}) fusion(bf16[2,256,2,256]{3,1,0,2:T(8,128)(2,1)} %get-tuple-element.451, bf16[2,256,2,256,1]{3,2,1,0,4:T(2,128)(2,1)} %bitcast.238, bf16[4,1,256,256]{3,2,0,1:T(8,128)(2,1)} %fusion.77, bf16[4,1,256,256]{3,2,0,1:T(8,128)(2,1)S(1)} %fusion.78), kind=kOutput, calls=%fused_computation.6.clone.1 | convolution fusion | flops 1075773440 | bytes 4456448 | tf_op jit(solution)/shard_map/while/body/eval_jaxpr/mcij,cjdl->mdil/dot_general | solution.py:46
  75.5 17.0 %all-reduce.7.cloned.1.call-done = f32[1,256,256]{2,1,0:T(8,128)} async-done(((f32[1,256,256]{2,1,0:T(8,128)}), f32[1,256,256]{2,1,0:T(8,128)}) %all-reduce.7.cloned.1.call-update) | async-done | bytes 262160 | tf_op jit(solution)/shard_map/while/body/eval_jaxpr/psum | solution.py:126
  92.5 1.1 fusion.80
  93.6 4.6 %convolution_bitcast_fusion.2 = f32[1,4,2,256,256]{4,3,2,1,0:T(8,128)} fusion(f32[4,256,2,256,1]{3,1,4,2,0:T(8,128)} %get-tuple-element.406, f32[256,256]{1,0:T(8,128)S(1)} %fusion.80, bf16[2,256,2,256]{3,1,0,2:T(8,128)(2,1)} %get-tuple-element.453, bf16[2,256,2,256,1]{3,2,1,0,4:T(2,128)(2,1)} %bitcast.237), kind=kOutput, calls=%fused_computation.9.clone.1 | convolution fusion | flops 1075314688 | bytes 5505024 | tf_op jit(solution)/shard_map/while/body/eval_jaxpr/mcij,cjdl->mdil/dot_general | solution.py:46
  98.1 3.3 %multiply_add_fusion.2 = (f32[1,4,1,256,256]{4,3,2,1,0:T(8,128)}, f32[1,4,1,256,256]{4,3,2,1,0:T(8,128)}) fusion(f32[1,4,2,256,256]{4,3,2,1,0:T(8,128)} %convolution_bitcast_fusion.2, f32[256,256]{1,0:T(8,128)S(1)} %get-tuple-element.404, f32[256,256]{1,0:T(8,128)S(1)} %get-tuple-element.405), kind=kLoop, calls=%fused_computation.32.clone.1 | loop fusion | flops 1572864 | bytes 4718592 | tf_op jit(solution)/shard_map/while/body/eval_jaxpr/add | solution.py:66
  101.9 2.3 dynamic-slice_add_fusion.2
  104.2 6.7 %dynamic_update_slice.9 = f32[2,768,768]{2,1,0:T(8,128)} dynamic-update-slice(f32[2,768,768]{2,1,0:T(8,128)} %get-tuple-element.428, f32[2,256,256]{2,1,0:T(8,128)} %dynamic-slice_add_fusion.2, s32[]{:T(128)} %constant.72.clone.1..sunk, s32[]{:T(128)S(6)} %select_n.92, s32[]{:T(128)S(6)} %select_n.93) | dynamic-update-slice | bytes 1048580 | tf_op jit(solution)/shard_map/while/body/eval_jaxpr/dynamic_update_slice | solution.py:136
  110.9 2.8 fusion.82
  113.7 0.6 fusion.76
  118.0 1.4 dynamic-slice_bitcast_fusion.2
  119.6 1.0 fusion.77
  120.6 4.7 %fusion.79 = (f32[256,256]{1,0:T(8,128)}, f32[4,256,2,256,1]{3,1,4,2,0:T(8,128)}) fusion(bf16[2,256,2,256]{3,1,0,2:T(8,128)(2,1)} %get-tuple-element.451, bf16[2,256,2,256,1]{3,2,1,0,4:T(2,128)(2,1)} %bitcast.238, bf16[4,1,256,256]{3,2,0,1:T(8,128)(2,1)} %fusion.77, bf16[4,1,256,256]{3,2,0,1:T(8,128)(2,1)S(1)} %fusion.78), kind=kOutput, calls=%fused_computation.6.clone.1 | convolution fusion | flops 1075773440 | bytes 4456448 | tf_op jit(solution)/shard_map/while/body/eval_jaxpr/mcij,cjdl->mdil/dot_general | solution.py:46
  126.0 19.0 %all-reduce.7.cloned.1.call-done = f32[1,256,256]{2,1,0:T(8,128)} async-done(((f32[1,256,256]{2,1,0:T(8,128)}), f32[1,256,256]{2,1,0:T(8,128)}) %all-reduce.7.cloned.1.call-update) | async-done | bytes 262160 | tf_op jit(solution)/shard_map/while/body/eval_jaxpr/psum | solution.py:126
  145.0 1.1 fusion.80
  146.1 4.6 %convolution_bitcast_fusion.2 = f32[1,4,2,256,256]{4,3,2,1,0:T(8,128)} fusion(f32[4,256,2,256,1]{3,1,4,2,0:T(8,128)} %get-tuple-element.406, f32[256,256]{1,0:T(8,128)S(1)} %fusion.80, bf16[2,256,2,256]{3,1,0,2:T(8,128)(2,1)} %get-tuple-element.453, bf16[2,256,2,256,1]{3,2,1,0,4:T(2,128)(2,1)} %bitcast.237), kind=kOutput, calls=%fused_computation.9.clone.1 | convolution fusion | flops 1075314688 | bytes 5505024 | tf_op jit(solution)/shard_map/while/body/eval_jaxpr/mcij,cjdl->mdil/dot_general | solution.py:46
  150.6 3.3 %multiply_add_fusion.2 = (f32[1,4,1,256,256]{4,3,2,1,0:T(8,128)}, f32[1,4,1,256,256]{4,3,2,1,0:T(8,128)}) fusion(f32[1,4,2,256,256]{4,3,2,1,0:T(8,128)} %convolution_bitcast_fusion.2, f32[256,256]{1,0:T(8,128)S(1)} %get-tuple-element.404, f32[256,256]{1,0:T(8,128)S(1)} %get-tuple-element.405), kind=kLoop, calls=%fused_computation.32.clone.1 | loop fusion | flops 1572864 | bytes 4718592 | tf_op jit(solution)/shard_map/while/body/eval_jaxpr/add | solution.py:66
  154.4 2.3 dynamic-slice_add_fusion.2
  156.7 6.7 %dynamic_update_slice.9 = f32[2,768,768]{2,1,0:T(8,128)} dynamic-update-slice(f32[2,768,768]{2,1,0:T(8,128)} %get-tuple-element.428, f32[2,256,256]{2,1,0:T(8,128)} %dynamic-slice_add_fusion.2, s32[]{:T(128)} %constant.72.clone.1..sunk, s32[]{:T(128)S(6)} %select_n.92, s32[]{:T(128)S(6)} %select_n.93) | dynamic-update-slice | bytes 1048580 | tf_op jit(solution)/shard_map/while/body/eval_jaxpr/dynamic_update_slice | solution.py:136
  163.4 3.5 %fusion.82 = f32[4,2,256,256]{3,2,1,0:T(8,128)} fusion(f32[1,4,1,256,256]{4,3,2,1,0:T(8,128)} %get-tuple-element.410, f32[1,4,1,256,256]{4,3,2,1,0:T(8,128)S(1)} %copy-done.1, f32[4,2,256,256]{3,2,1,0:T(8,128)} %get-tuple-element.429, pred[]{:T(512)S(6)} %compare.30), kind=kLoop, calls=%fused_computation.2.clone.1 | loop fusion | flops 1572864 | bytes 6291457 | tf_op jit(solution)/shard_map/while/body/eval_jaxpr/add | solution.py:139
  166.9 1.7 fusion.56
  168.6 3.8 %collective-permute-start.4 = (f32[2,128,768]{2,1,0:T(8,128)S(1)}, f32[2,128,768]{2,1,0:T(8,128)S(1)}, u32[]{:S(2)}, u32[]{:S(2)}) collective-permute-start(f32[2,128,768]{2,1,0:T(8,128)S(1)} %get-tuple-element.304), channel_id=1, source_target_pairs={{0,4},{4,8},{8,12},{1,5},{5,9},{9,13},{2,6},{6,10},{10,14},{3,7},{... | collective-permute-start | bytes 2359304 | tf_op jit(solution)/shard_map/ppermute | solution.py:19
  172.4 1.3 collective-permute-start.5
  173.7 15.9 %collective-permute-done.4 = f32[2,128,768]{2,1,0:T(8,128)S(1)} collective-permute-done((f32[2,128,768]{2,1,0:T(8,128)S(1)}, f32[2,128,768]{2,1,0:T(8,128)S(1)}, u32[]{:S(2)}, u32[]{:S(2)}) %collective-permute-start.4) | collective-permute-done | bytes 786464 | tf_op jit(solution)/shard_map/ppermute | solution.py:19
  189.7 0.3 constant_dynamic-update-slice_fusion.4
  190.0 3.8 %collective-permute-done.5 = f32[2,128,768]{2,1,0:T(8,128)S(1)} collective-permute-done((f32[2,128,768]{2,1,0:T(8,128)S(1)}, f32[2,128,768]{2,1,0:T(8,128)S(1)}, u32[]{:S(2)}, u32[]{:S(2)}) %collective-permute-start.5) | collective-permute-done | bytes 786464 | tf_op jit(solution)/shard_map/ppermute | solution.py:21
  193.8 2.6 copy-done.3
  196.5 1.1 fusion.55
  197.6 3.4 %collective-permute-start.6 = (f32[2,1024,128]{2,1,0:T(8,128)}, f32[2,1024,128]{2,1,0:T(8,128)S(1)}, u32[]{:S(2)}, u32[]{:S(2)}) collective-permute-start(f32[2,1024,128]{2,1,0:T(8,128)} %get-tuple-element.301), channel_id=1, source_target_pairs={{0,2},{1,3},{4,6},{5,7},{8,10},{9,11},{12,14},{13,15},{16,18},{17,... | collective-permute-start | bytes 3145736 | tf_op jit(solution)/shard_map/ppermute | solution.py:19
  201.0 1.3 collective-permute-start.7
  202.4 28.0 %collective-permute-done.6 = f32[2,1024,128]{2,1,0:T(8,128)S(1)} collective-permute-done((f32[2,1024,128]{2,1,0:T(8,128)}, f32[2,1024,128]{2,1,0:T(8,128)S(1)}, u32[]{:S(2)}, u32[]{:S(2)}) %collective-permute-start.6) | collective-permute-done | bytes 1048608 | tf_op jit(solution)/shard_map/ppermute | solution.py:19
  230.5 4.0 %collective-permute-done.7 = f32[2,1024,128]{2,1,0:T(8,128)S(1)} collective-permute-done((f32[2,1024,128]{2,1,0:T(8,128)S(1)}, f32[2,1024,128]{2,1,0:T(8,128)S(1)}, u32[]{:S(2)}, u32[]{:S(2)}) %collective-permute-start.7) | collective-permute-done | bytes 1048608 | tf_op jit(solution)/shard_map/ppermute | solution.py:21
  234.4 3.5 %pad_maximum_fusion = f32[2,1024,1024]{2,1,0:T(8,128)S(1)} fusion(f32[2,1024,128]{2,1,0:T(8,128)S(1)} %collective-permute-done.7, f32[2,1024,768]{2,1,0:T(8,128)} %copy-done.3, f32[2,1024,128]{2,1,0:T(8,128)S(1)} %collective-permute-done.6), kind=kLoop, calls=%fused_computation.49 | loop fusion | flops 4194304 | bytes 16777216 | tf_op jit(solution)/shard_map/concatenate | solution.py:17
  238.0 1.1 copy-done.4
  239.1 1.8 fusion.31
  241.0 1.7 fusion.34
  242.8 66.2 %all-reduce.5.cloned.1.call-done = f32[4,2,256,256]{3,2,1,0:T(8,128)} async-done(((f32[4,2,256,256]{3,2,1,0:T(8,128)}), f32[4,2,256,256]{3,2,1,0:T(8,128)}) %all-reduce.5.cloned.1.call-update) | async-done | bytes 2097168 | tf_op jit(solution)/shard_map/psum | solution.py:146
  309.0 3.1 broadcast_multiply_fusion
  (47 shorter events, 2.2 us)
Async XLA Ops:
  8.0 17.6 %copy-start.6 = (f32[2,512,512]{2,1,0:T(8,128)S(1)}, f32[2,512,512]{2,1,0:T(8,128)}, u32[]{:S(2)}) copy-start(f32[2,512,512]{2,1,0:T(8,128)} %param.7) | copy-start | bytes 6291460
  9.4 16.1 %collective-permute-start = (f32[2,128,512]{2,1,0:T(8,128)S(1)}, f32[2,128,512]{2,1,0:T(8,128)S(1)}, u32[]{:S(2)}, u32[]{:S(2)}) collective-permute-start(f32[2,128,512]{2,1,0:T(8,128)S(1)} %get-tuple-element.308), channel_id=1, source_target_pairs={{0,4},{4,8},{8,12},{1,5},{5,9},{9,13},{2,6},{6,10},{10,14},{3,7},{... | collective-permute-start | bytes 1572872 | tf_op jit(solution)/shard_map/ppermute | solution.py:19
  14.4 15.3 %collective-permute-start.1 = (f32[2,128,512]{2,1,0:T(8,128)S(1)}, f32[2,128,512]{2,1,0:T(8,128)S(1)}, u32[]{:S(2)}, u32[]{:S(2)}) collective-permute-start(f32[2,128,512]{2,1,0:T(8,128)S(1)} %get-tuple-element.307), channel_id=1, source_target_pairs={{4,0},{8,4},{12,8},{5,1},{9,5},{13,9},{6,2},{10,6},{14,10},{7,3},{... | collective-permute-start | bytes 1572872 | tf_op jit(solution)/shard_map/ppermute | solution.py:21
  29.7 1.6 copy-start.5
  32.6 19.3 %collective-permute-start.2 = (f32[2,768,128]{2,1,0:T(8,128)}, f32[2,768,128]{2,1,0:T(8,128)S(1)}, u32[]{:S(2)}, u32[]{:S(2)}) collective-permute-start(f32[2,768,128]{2,1,0:T(8,128)} %get-tuple-element.305), channel_id=1, source_target_pairs={{0,2},{1,3},{4,6},{5,7},{8,10},{9,11},{12,14},{13,15},{16,18},{17,... | collective-permute-start | bytes 2359304 | tf_op jit(solution)/shard_map/ppermute | solution.py:19
  36.1 20.0 %collective-permute-start.3 = (f32[2,768,128]{2,1,0:T(8,128)}, f32[2,768,128]{2,1,0:T(8,128)}, u32[]{:S(2)}, u32[]{:S(2)}) collective-permute-start(f32[2,768,128]{2,1,0:T(8,128)} %get-tuple-element.306), channel_id=1, source_target_pairs={{2,0},{3,1},{6,4},{7,5},{10,8},{11,9},{14,12},{15,13},{18,16},{19,... | collective-permute-start | bytes 2359304 | tf_op jit(solution)/shard_map/ppermute | solution.py:21
  60.7 2.5 copy-start.8
  63.2 29.3 %all-reduce.7.cloned.1.call-start = ((), (), s32[]{:S(2)}) async-start(), calls=%async_computation.3 | async-start | bytes 524288 | tf_op jit(solution)/shard_map/while/body/eval_jaxpr/psum | solution.py:126
  98.1 3.3 %copy-start = (f32[1,4,2,256,256]{4,3,2,1,0:T(8,128)S(1)}, f32[1,4,2,256,256]{4,3,2,1,0:T(8,128)}, u32[]{:S(2)}) copy-start(f32[1,4,2,256,256]{4,3,2,1,0:T(8,128)} %convolution_bitcast_fusion.2) | copy-start | bytes 6291460 | tf_op jit(solution)/shard_map/while
  101.8 9.1 %copy-start.1 = (f32[1,4,1,256,256]{4,3,2,1,0:T(8,128)S(1)}, f32[1,4,1,256,256]{4,3,2,1,0:T(8,128)}, u32[]{:S(2)}) copy-start(f32[1,4,1,256,256]{4,3,2,1,0:T(8,128)} %get-tuple-element.411) | copy-start | bytes 3145732 | tf_op jit(solution)/shard_map/while
  113.7 31.3 %all-reduce.7.cloned.1.call-start = ((), (), s32[]{:S(2)}) async-start(), calls=%async_computation.3 | async-start | bytes 524288 | tf_op jit(solution)/shard_map/while/body/eval_jaxpr/psum | solution.py:126
  150.6 3.3 %copy-start = (f32[1,4,2,256,256]{4,3,2,1,0:T(8,128)S(1)}, f32[1,4,2,256,256]{4,3,2,1,0:T(8,128)}, u32[]{:S(2)}) copy-start(f32[1,4,2,256,256]{4,3,2,1,0:T(8,128)} %convolution_bitcast_fusion.2) | copy-start | bytes 6291460 | tf_op jit(solution)/shard_map/while
  154.3 9.1 %copy-start.1 = (f32[1,4,1,256,256]{4,3,2,1,0:T(8,128)S(1)}, f32[1,4,1,256,256]{4,3,2,1,0:T(8,128)}, u32[]{:S(2)}) copy-start(f32[1,4,1,256,256]{4,3,2,1,0:T(8,128)} %get-tuple-element.411) | copy-start | bytes 3145732 | tf_op jit(solution)/shard_map/while
  166.9 142.1 %all-reduce.5.cloned.1.call-start = ((), (), s32[]{:S(2)}) async-start(), calls=%async_computation.2 | async-start | bytes 4194304 | tf_op jit(solution)/shard_map/psum | solution.py:146
  166.9 22.8 %copy-start.2 = (f32[2,768,768]{2,1,0:T(8,128)S(1)}, f32[2,768,768]{2,1,0:T(8,128)}, u32[]{:S(2)}) copy-start(f32[2,768,768]{2,1,0:T(8,128)} %get-tuple-element.202) | copy-start | bytes 14155780
  168.6 21.0 %collective-permute-start.4 = (f32[2,128,768]{2,1,0:T(8,128)S(1)}, f32[2,128,768]{2,1,0:T(8,128)S(1)}, u32[]{:S(2)}, u32[]{:S(2)}) collective-permute-start(f32[2,128,768]{2,1,0:T(8,128)S(1)} %get-tuple-element.304), channel_id=1, source_target_pairs={{0,4},{4,8},{8,12},{1,5},{5,9},{9,13},{2,6},{6,10},{10,14},{3,7},{... | collective-permute-start | bytes 2359304 | tf_op jit(solution)/shard_map/ppermute | solution.py:19
  172.4 21.4 %collective-permute-start.5 = (f32[2,128,768]{2,1,0:T(8,128)S(1)}, f32[2,128,768]{2,1,0:T(8,128)S(1)}, u32[]{:S(2)}, u32[]{:S(2)}) collective-permute-start(f32[2,128,768]{2,1,0:T(8,128)S(1)} %get-tuple-element.303), channel_id=1, source_target_pairs={{4,0},{8,4},{12,8},{5,1},{9,5},{13,9},{6,2},{10,6},{14,10},{7,3},{... | collective-permute-start | bytes 2359304 | tf_op jit(solution)/shard_map/ppermute | solution.py:21
  193.8 2.7 copy-start.3
  197.6 32.9 %collective-permute-start.6 = (f32[2,1024,128]{2,1,0:T(8,128)}, f32[2,1024,128]{2,1,0:T(8,128)S(1)}, u32[]{:S(2)}, u32[]{:S(2)}) collective-permute-start(f32[2,1024,128]{2,1,0:T(8,128)} %get-tuple-element.301), channel_id=1, source_target_pairs={{0,2},{1,3},{4,6},{5,7},{8,10},{9,11},{12,14},{13,15},{16,18},{17,... | collective-permute-start | bytes 3145736 | tf_op jit(solution)/shard_map/ppermute | solution.py:19
  201.0 33.4 %collective-permute-start.7 = (f32[2,1024,128]{2,1,0:T(8,128)S(1)}, f32[2,1024,128]{2,1,0:T(8,128)S(1)}, u32[]{:S(2)}, u32[]{:S(2)}) collective-permute-start(f32[2,1024,128]{2,1,0:T(8,128)S(1)} %get-tuple-element.302), channel_id=1, source_target_pairs={{2,0},{3,1},{6,4},{7,5},{10,8},{11,9},{14,12},{15,13},{18,16},{19,... | collective-permute-start | bytes 3145736 | tf_op jit(solution)/shard_map/ppermute | solution.py:21
  202.3 35.6 %copy-start.7 = (pred[512]{0:T(512)(128)(4,1)S(1)}, pred[512]{0:T(512)(128)(4,1)}, u32[]{:S(2)}) copy-start(pred[512]{0:T(512)(128)(4,1)} %constant.79.clone.1) | copy-start | bytes 1540
  202.4 109.8 %reduce-scatter.2.cloned.1.call-start = ((), (), s32[]{:S(2)}) async-start(), calls=%async_computation.1 | async-start | bytes 3145728 | tf_op jit(solution)/shard_map/reduce_scatter | solution.py:145
  234.4 4.7 %copy-start.4 = (f32[2,1024,768]{2,1,0:T(8,128)S(1)}, f32[2,1024,768]{2,1,0:T(8,128)}, u32[]{:S(2)}) copy-start(f32[2,1024,768]{2,1,0:T(8,128)} %copy-done.3) | copy-start | bytes 18874372
Sparse Core Ops, SparseCore 0:
  74.9 17.5 all-reduce.6
  125.4 19.5 all-reduce.6
  242.9 8.0 reduce-scatter.1
Sparse Core Ops, SparseCore 1:
  202.4 106.5 all-reduce.4
where the time goes:
time: 321 us; the launch traced here: 319 us
  waiting for transfers between devices  175 us (55%)
  other arithmetic  42.8 us (13%)
  local copies, waits for them, and re-layouts  38.1 us (12%)
  starting transfers between devices  20.9 us (7%)
  matrix products  18.5 us (6%)
  between operations  15.4 us (5%)
  loops' own time  8.78 us (3%)
    psum x1, waiting for transfers between devices, shards(): probe_sum = lax.psum(probe_total, ('row', 'col'))  66.2 us
    ppermute x4, waiting for transfers between devices, extended(): lax.ppermute(tail, axis, [(i, (i + 1) % count) for i in range(ends)])  56.6 us
    psum x2, waiting for transfers between devices, visit_slot(): total_power = lax.psum(local_power, 'mode')  36.1 us
    dot_general x4, matrix products, transform(): jnp.einsum('mcij,cjdl->mdil', halfway, right_table, preferred_element_typ...  18.5 us
    ppermute x4, waiting for transfers between devices, extended(): lax.ppermute(head, axis, [((i + 1) % count, i) for i in range(ends)])  15.8 us
    ppermute x4, starting transfers between devices, extended(): lax.ppermute(tail, axis, [(i, (i + 1) % count) for i in range(ends)])  15.6 us
    dynamic_update_slice x2, local copies, waits for them, and re-layouts, visit_slot(): lax.dynamic_update_slice(gradient_grid, current + object_terms[0], (ancho...  13.4 us
    unnamed x23, local copies, waits for them, and re-layouts  12.5 us
  transfers between devices with their start and end apart: 12, of which 11 were waited for; matrix products, arithmetic and copies ran while one was open for 7% of the time, Pallas kernels for 0%

commit v1 on v0

v1 whole, which is shorter than its diff:
```python
import functools
import math

import jax
import jax.numpy as jnp
import numpy as np
from jax import lax
from jax.experimental import pallas as pl
from jax.experimental.pallas import tpu as pltpu
from jax.sharding import PartitionSpec as P

damping = 0.1
LANES = 128
SUBLANES = 8
VMEM_BYTES = 32 * 1024 * 1024

f32 = jnp.float32
bf16 = jnp.bfloat16


def dft_blocks(size):
    index = np.arange(size, dtype=np.int64)
    angles = 2.0 * np.pi / size * (index[:, None] * index[None, :] % size)
    real = (np.cos(angles) / np.sqrt(size)).astype(np.float32).astype(bf16)
    imag = (-np.sin(angles) / np.sqrt(size)).astype(np.float32).astype(bf16)
    left = np.block([[real, -imag], [imag, real]])
    return left, np.ascontiguousarray(left.T)


def params():
    return pltpu.CompilerParams(vmem_limit_bytes=VMEM_BYTES)


def whole(shape):
    return pl.BlockSpec(shape, lambda *_: (0,) * len(shape))


def window_of(offset):
    base_row = pl.multiple_of(offset[0] // SUBLANES * SUBLANES, SUBLANES)
    base_col = pl.multiple_of(offset[1] // LANES * LANES, LANES)
    return base_row, base_col, offset[0] - base_row, offset[1] - base_col


def cut_kernel(size, margin, tile, slots, info, own, up, down, left, right, ul, ur, dl, dr, out, frame):
    low, high = slice(0, margin), slice(margin + tile, 2 * margin + tile)
    mid = slice(margin, margin + tile)
    has_left = info[1].astype(f32)
    has_right = info[2].astype(f32)
    frame[low, mid] = up[...]
    frame[high, mid] = down[...]
    frame[mid, mid] = own[...]
    frame[mid, low] = left[...] * has_left
    frame[mid, high] = right[...] * has_right
    frame[low, low] = ul[...] * has_left
    frame[low, high] = ur[...] * has_right
    frame[high, low] = dl[...] * has_left
    frame[high, high] = dr[...] * has_right
    rows, cols = size + SUBLANES, size + LANES
    for slot in range(slots):
        base_row, base_col, row, col = window_of((info[3 + 2 * slot], info[4 + 2 * slot]))
        window = frame[pl.ds(base_row, rows), pl.ds(base_col, cols)]
        window = pltpu.roll(window, rows - row, 0)[:size]
        window = pltpu.roll(window, cols - col, 1)[:, :size]
        out[slot] = window


def cut_patches(info, field, strips, size, slots):
    tile = field.shape[-1]
    margin = size // 2
    span = tile + 2 * margin
    kernel = functools.partial(cut_kernel, size, margin, tile, slots)
    return pl.pallas_call(
        kernel,
        grid_spec=pltpu.PrefetchScalarGridSpec(
            num_scalar_prefetch=1,
            grid=(1,),
            in_specs=[pl.BlockSpec((None, tile, tile), lambda i, info: (info[0], 0, 0))]
            + [whole(s.shape) for s in strips],
            out_specs=whole((slots, size, size)),
            scratch_shapes=[pltpu.VMEM((span + SUBLANES, span + LANES), f32)],
        ),
        out_shape=jax.ShapeDtypeStruct((slots, size, size), f32),
        compiler_params=params(),
        name="cut",
    )(info, field, *strips)


def as_slot_rows(wave, size, slots):
    return jnp.concatenate(
        [
            jnp.concatenate(
                [wave[c * size : (c + 1) * size, s * size : (s + 1) * size] for c in range(2)], axis=1
            )
            for s in range(slots)
        ],
        axis=0,
    )


def forward_kernel(size, slots, info, probe, mine, other, left, right, spectrum, power):
    first = info[0] == 0
    pr, pi = probe[0], probe[1]
    real, imag = [], []
    for s in range(slots):
        a, b = mine[s], other[s]
        qr, qi = jnp.where(first, a, b), jnp.where(first, b, a)
        real.append((pr * qr - pi * qi).astype(bf16))
        imag.append((pr * qi + pi * qr).astype(bf16))
    wave = jnp.concatenate([jnp.concatenate(real, axis=1), jnp.concatenate(imag, axis=1)], axis=0)
    half = jnp.dot(left[...], wave, preferred_element_type=f32).astype(bf16)
    full = jnp.dot(as_slot_rows(half, size, slots), right[...], preferred_element_type=f32)

    @pl.when(pl.program_id(0) == 0)
    def _():
        power[...] = jnp.zeros_like(power)

    for s in range(slots):
        rows = full[s * size : (s + 1) * size]
        spectrum[s] = rows
        power[s] += rows[:, :size] * rows[:, :size] + rows[:, size:] * rows[:, size:]


def forward(info, probes, mine, other, left, right):
    modes, _, size, _ = probes.shape
    slots = mine.shape[0]
    return pl.pallas_call(
        functools.partial(forward_kernel, size, slots),
        grid_spec=pltpu.PrefetchScalarGridSpec(
            num_scalar_prefetch=1,
            grid=(modes,),
            in_specs=[
                pl.BlockSpec((None, 2, size, size), lambda m, info: (m, 0, 0, 0)),
                whole(mine.shape),
                whole(other.shape),
                whole(left.shape),
                whole(right.shape),
            ],
            out_specs=[
                pl.BlockSpec((None, slots, size, 2 * size), lambda m, info: (m, 0, 0, 0)),
                whole((slots, size, size)),
            ],
        ),
        out_shape=[
            jax.ShapeDtypeStruct((modes, slots, size, 2 * size), f32),
            jax.ShapeDtypeStruct((slots, size, size), f32),
        ],
        compiler_params=params(),
        name="forward",
    )(info, probes, mine, other, left, right)


def backward_kernel(
    size, slots, scale, info, probe, mine, other, amplitudes, power, power_other, spectrum, left, right,
    probe_keep, probe_send, object_keep, object_send, weight,
):
    step = pl.program_id(0)
    first = info[0] == 0
    low = info[1] == 0

    @pl.when(step == 0)
    def _():
        for s in range(slots):
            active = (s < info[2]).astype(f32)
            total = power[s] + power_other[s]
            weight[s] = active * (1.0 - amplitudes[s] / jnp.sqrt(total + damping))
        object_keep[...] = jnp.zeros_like(object_keep)
        object_send[...] = jnp.zeros_like(object_send)

    real, imag = [], []
    for s in range(slots):
        w = weight[s]
        real.append((w * spectrum[s, :, :size]).astype(bf16))
        imag.append((w * spectrum[s, :, size:]).astype(bf16))
    hat = jnp.concatenate([jnp.concatenate(real, axis=1), jnp.concatenate(imag, axis=1)], axis=0)
    half = jnp.dot(right[...], hat, preferred_element_type=f32).astype(bf16)
    back = jnp.dot(as_slot_rows(half, size, slots), left[...], preferred_element_type=f32)

    pr, pi = probe[0], probe[1]
    sum_real = jnp.zeros((size, size), f32)
    sum_imag = jnp.zeros((size, size), f32)
    for s in range(slots):
        br = back[s * size : (s + 1) * size, :size]
        bi = back[s * size : (s + 1) * size, size:]
        a, b = mine[s], other[s]
        qr, qi = jnp.where(first, a, b), jnp.where(first, b, a)
        sum_real += qr * br + qi * bi
        sum_imag += qr * bi - qi * br
        term_real = pr * br + pi * bi
        term_imag = pr * bi - pi * br
        object_keep[s] += jnp.where(first, term_real, term_imag)
        object_send[s] += jnp.where(first, term_imag, term_real)
    sum_real *= scale
    sum_imag *= scale
    probe_keep[...] = jnp.where(low, sum_real, sum_imag)
    probe_send[...] = jnp.where(low, sum_imag, sum_real)


def backward(info, probes, mine, other, amplitudes, power, power_other, spectrum, left, right, scale):
    modes, _, size, _ = probes.shape
    slots = mine.shape[0]
    plane = pl.BlockSpec((None, size, size), lambda m, info: (m, 0, 0))
    return pl.pallas_call(
        functools.partial(backward_kernel, size, slots, scale),
        grid_spec=pltpu.PrefetchScalarGridSpec(
            num_scalar_prefetch=1,
            grid=(modes,),
            in_specs=[
                pl.BlockSpec((None, 2, size, size), lambda m, info: (m, 0, 0, 0)),
                whole(mine.shape),
                whole(other.shape),
                whole(mine.shape),
                whole(power.shape),
                whole(power.shape),
                pl.BlockSpec((None, slots, size, 2 * size), lambda m, info: (m, 0, 0, 0)),
                whole(left.shape),
                whole(right.shape),
            ],
            out_specs=[plane, plane, whole(mine.shape), whole(mine.shape)],
            scratch_shapes=[pltpu.VMEM(mine.shape, f32)],
        ),
        out_shape=[jax.ShapeDtypeStruct((modes, size, size), f32)] * 2
        + [jax.ShapeDtypeStruct(mine.shape, f32)] * 2,
        compiler_params=params(),
        name="backward",
    )(info, probes, mine, other, amplitudes, power, power_other, spectrum, left, right)


def place_kernel(size, margin, tile, slots, groups, info, mine, other, columns, strips, frame):
    span = tile + 2 * margin
    frame[...] = jnp.zeros_like(frame)
    rows, cols = size + SUBLANES, size + LANES
    for slot in range(slots):
        base_row, base_col, row, col = window_of((info[2 * slot], info[2 * slot + 1]))
        patch = mine[slot] + other[slot]
        window = jnp.concatenate([patch, jnp.zeros((SUBLANES, size), f32)], axis=0)
        window = pltpu.roll(window, row, 0)
        window = jnp.concatenate([window, jnp.zeros((rows, LANES), f32)], axis=1)
        window = pltpu.roll(window, col, 1)
        at = (pl.ds(base_row, rows), pl.ds(base_col, cols))
        frame[at] = frame[at] + window
    columns[...] = frame[0:span, margin : margin + tile]
    for g in range(groups):
        start = pl.multiple_of(info[2 * slots + g], LANES)
        strips[g] = frame[0:span, pl.ds(start, margin)]


def place(info, mine, other, tile, groups):
    slots, size, _ = mine.shape
    margin = size // 2
    span = tile + 2 * margin
    return pl.pallas_call(
        functools.partial(place_kernel, size, margin, tile, slots, groups),
        grid_spec=pltpu.PrefetchScalarGridSpec(
            num_scalar_prefetch=1,
            grid=(1,),
            in_specs=[whole(mine.shape), whole(other.shape)],
            out_specs=[whole((span, tile)), whole((groups, span, margin))],
            scratch_shapes=[pltpu.VMEM((span + SUBLANES, span + LANES), f32)],
        ),
        out_shape=[
            jax.ShapeDtypeStruct((span, tile), f32),
            jax.ShapeDtypeStruct((groups, span, margin), f32),
        ],
        compiler_params=params(),
        name="place",
    )(info, mine, other)


def merge_kernel(margin, tile, groups, info, columns, *refs):
    arrived, (top, middle, bottom) = refs[:groups], refs[groups:]
    top[...] = columns[0:margin]
    middle[...] = columns[margin : margin + tile]
    bottom[...] = columns[margin + tile :]
    for g in range(groups):
        at = pl.ds(pl.multiple_of(info[g], LANES), margin)
        top[:, at] = top[:, at] + arrived[g][0:margin]
        middle[:, at] = middle[:, at] + arrived[g][margin : margin + tile]
        bottom[:, at] = bottom[:, at] + arrived[g][margin + tile :]


def merge(info, columns, arrived):
    span, tile = columns.shape
    margin = (span - tile) // 2
    shapes = [(margin, tile), (tile, tile), (margin, tile)]
    return pl.pallas_call(
        functools.partial(merge_kernel, margin, tile, len(arrived)),
        grid_spec=pltpu.PrefetchScalarGridSpec(
            num_scalar_prefetch=1,
            grid=(1,),
            in_specs=[whole(columns.shape)] + [whole(a.shape) for a in arrived],
            out_specs=[whole(s) for s in shapes],
        ),
        out_shape=[jax.ShapeDtypeStruct(s, f32) for s in shapes],
        compiler_params=params(),
        name="merge",
    )(info, columns, *arrived)


def finish_kernel(margin, tile, middle, above, below, out):
    out[0, 0:margin] = middle[0:margin] + above[...]
    out[0, margin : tile - margin] = middle[margin : tile - margin]
    out[0, tile - margin :] = middle[tile - margin :] + below[...]


def finish(middle, above, below):
    tile = middle.shape[0]
    margin = above.shape[0]
    return pl.pallas_call(
        functools.partial(finish_kernel, margin, tile),
        out_shape=jax.ShapeDtypeStruct((1, tile, tile), f32),
        compiler_params=params(),
        name="finish",
    )(middle, above, below)


def pairs(axis, bit):
    return [(i, i ^ (1 << bit)) for i in range(lax.axis_size(axis))]


def swap(value, dim):
    axis, bit = dim
    return lax.ppermute(value, axis, pairs(axis, bit))


def side_of(dim):
    axis, bit = dim
    return (lax.axis_index(axis) >> bit) & 1


def halves(value, side):
    count = value.shape[0] // 2
    keep = lax.dynamic_slice_in_dim(value, side * count, count, 0)
    send = lax.dynamic_slice_in_dim(value, (1 - side) * count, count, 0)
    return keep, send


def joined(mine, back, side):
    low = jnp.where(side == 0, mine, back)
    high = jnp.where(side == 0, back, mine)
    return jnp.concatenate([low, high], axis=0)


def total(value, dims):
    if not dims:
        return value
    if len(dims) == 1:
        return value + swap(value, dims[0])
    side = side_of(dims[0])
    keep, send = halves(value, side)
    mine = total(keep + swap(send, dims[0]), dims[1:])
    return joined(mine, swap(mine, dims[0]), side)


def shards(object_field, probe_modes, amplitudes, positions, counts):
    modes, _, size, _ = probe_modes.shape
    margin = size // 2
    tile = object_field.shape[-1]
    slots = positions.shape[2]
    rows, cols = lax.axis_size("row"), lax.axis_size("col")
    row, col, core = lax.axis_index("row"), lax.axis_index("col"), lax.axis_index("mode")
    left, right = (jnp.asarray(t) for t in dft_blocks(size))
    offsets = positions[0, 0].reshape(-1)

    field = lax.dynamic_index_in_dim(object_field, core, 0, keepdims=False)
    downward = [(i, i + 1) for i in range(rows - 1)]
    upward = [(i + 1, i) for i in range(rows - 1)]
    from_above = lax.ppermute(field[tile - margin :], "row", downward)
    from_below = lax.ppermute(field[:margin], "row", upward)
    if cols == 2:
        shifts = [[(0, 1), (1, 0)]]
        starts = [jnp.where(col == 0, tile - margin, 0)]
    else:
        shifts = [[(i, i + 1) for i in range(cols - 1)], [(i + 1, i) for i in range(cols - 1)]]
        starts = [jnp.int32(tile - margin), jnp.int32(0)]
    sides, uppers, lowers = [], [], []
    for shift, start in zip(shifts, starts):
        edge = lax.dynamic_slice(field, (0, start), (tile, margin))
        sides.append(lax.ppermute(edge, "col", shift))
        both = ("row", "col")
        uppers.append(
            lax.ppermute(
                edge[tile - margin :], both, [(a * cols + c, b * cols + d) for a, b in downward for c, d in shift]
            )
        )
        lowers.append(
            lax.ppermute(
                edge[:margin], both, [(a * cols + c, b * cols + d) for a, b in upward for c, d in shift]
            )
        )
    strips = [
        from_above, from_below, sides[0], sides[-1], uppers[0], uppers[-1], lowers[0], lowers[-1],
    ]
    flags = jnp.stack([core, (col > 0).astype(jnp.int32), (col < cols - 1).astype(jnp.int32)])
    mine = cut_patches(jnp.concatenate([flags, offsets]), object_field, strips, size, slots)
    core_dim = ("mode", 0)
    other = swap(mine, core_dim)

    spectrum, power = forward(core[None], probe_modes, mine, other, left, right)
    power_other = swap(power, core_dim)
    dims = [("col", b) for b in range(cols.bit_length() - 1)] + [
        ("row", b) for b in range(rows.bit_length() - 1)
    ]
    side = side_of(dims[0])
    probe_keep, probe_send, object_keep, object_send = backward(
        jnp.stack([core, side, counts[0, 0]]), probe_modes, mine, other, amplitudes[0, 0], power, power_other,
        spectrum, left, right, 1.0 / math.sqrt(rows * cols),
    )

    planes = []
    for m in range(modes):
        part = total(probe_keep[m] + swap(probe_send[m], dims[0]), dims[1:])
        planes.append(joined(part[None], swap(part, dims[0])[None], side))
    probe_grad = jnp.stack(planes)

    object_other = swap(object_send, core_dim)
    if cols == 2:
        out_starts = [jnp.where(col == 0, tile + margin, 0)]
        in_starts = [jnp.where(col == 0, tile - margin, 0)]
    else:
        out_starts = [jnp.int32(tile + margin), jnp.int32(0)]
        in_starts = [jnp.int32(0), jnp.int32(tile - margin)]
    columns, outgoing = place(
        jnp.concatenate([offsets, jnp.stack(out_starts)]), object_keep, object_other, tile, len(shifts)
    )
    arrived = [lax.ppermute(outgoing[g], "col", shift) for g, shift in enumerate(shifts)]
    top, middle, bottom = merge(jnp.stack(in_starts), columns, arrived)
    below = lax.ppermute(top, "row", upward)
    above = lax.ppermute(bottom, "row", downward)
    object_grad = finish(middle, above, below)
    return (object_grad, probe_grad)


def solution(mesh):
    return jax.shard_map(
        shards,
        mesh=mesh,
        in_specs=(
            P("scene", "row", "col"),
            P(("scene", "mode"), None, None, None),
            P(("scene", "row"), "col", None, None, None),
            P(("scene", "row"), "col", None, None),
            P(("scene", "row"), "col"),
        ),
        out_specs=(P(("scene", "mode"), "row", "col"), P(("scene", "mode"), None, None, None)),
        check_vma=False,
    )
```

time: 321 us -> 143 us (0.45)
  waiting for transfers between devices: 175 us -> 64.1 us
  other arithmetic: 42.8 us -> 2.43 us
  matrix products: 18.5 us -> 0 us
  starting transfers between devices: 20.9 us -> 38.6 us
  local copies, waits for them, and re-layouts: 38.1 us -> 21.4 us
  Pallas kernels: 0 us -> 14.2 us
  between operations: 15.4 us -> 1.63 us
  loops' own time: 8.78 us -> 0 us
    psum x3 -> x0, waiting for transfers between devices: 102 us -> none  [the longest x1 66.2 us: shards(): probe_sum = lax.psum(probe_total, ('row', 'col'))]
    add x10 -> x9, other arithmetic: 21.6 us -> 0.27 us  [the longest x1 0.14 us: shards(): part = total(probe_keep[m] + swap(probe_send[m], dims[0]), dims[1:])]
    dot_general x4 -> x0, matrix products: 18.5 us -> none  [transform(): jnp.einsum('mcij,cjdl->mdil', halfway, right_table, preferred_element_typ...]
    ppermute x8 -> x31, starting transfers between devices: 20.8 us -> 38.6 us  [the longest x23 20.8 us: swap(): return lax.ppermute(value, axis, pairs(axis, bit))]
    pallas_call x0 -> x6, Pallas kernels: none -> 14.2 us  [the longest x1 6.08 us: backward(): pl.pallas_call(functools.partial(backward_kernel, size, slots, scale), gr...]
    dynamic_update_slice x2 -> x0, local copies, waits for them, and re-layouts: 13.4 us -> none  [visit_slot(): lax.dynamic_update_slice(gradient_grid, current + object_terms[0], (ancho...]
    another operation x1 -> x0, loops' own time: 8.78 us -> none  [shards(): lax.fori_loop(0, slot_count, visit_slot, start_state)]
    ppermute x8 -> x31, waiting for transfers between devices: 72.4 us -> 64.1 us  [the longest x23 59 us: swap(): return lax.ppermute(value, axis, pairs(axis, bit))]
  transfers between devices with their start and end apart: 12 -> 31, of which waited for: 11 -> 20; matrix products, arithmetic and copies ran while one was open for 7% -> 5% of each run, Pallas kernels for 0% -> 1%
where the time goes in v1:
time: 143 us; the launch traced here: 142 us
  waiting for transfers between devices  64.1 us (45%)
  starting transfers between devices  38.6 us (27%)
  local copies, waits for them, and re-layouts  21.4 us (15%)
  Pallas kernels  14.2 us (10%)
  other arithmetic  2.43 us (2%)
  between operations  1.63 us (1%)
    ppermute x23, waiting for transfers between devices, swap(): return lax.ppermute(value, axis, pairs(axis, bit))  59 us
    ppermute x23, starting transfers between devices, swap(): return lax.ppermute(value, axis, pairs(axis, bit))  20.8 us
    unnamed x38, local copies, waits for them, and re-layouts  14.5 us
    pallas_call x1, Pallas kernels, backward(): pl.pallas_call(functools.partial(backward_kernel, size, slots, scale), gr...  6.08 us
    ppermute x1, waiting for transfers between devices, shards(): lax.ppermute(edge[:margin], both, [(a * cols + c, b * cols + d) for a, b...  5.07 us
    ppermute x1, starting transfers between devices, shards(): from_above = lax.ppermute(field[tile - margin:], 'row', downward)  4.93 us
    ppermute x1, starting transfers between devices, shards(): lax.ppermute(edge[tile - margin:], both, [(a * cols + c, b * cols + d) fo...  4.69 us
    pallas_call x1, Pallas kernels, forward(): pl.pallas_call(functools.partial(forward_kernel, size, slots), grid_spec=...  4.64 us
  transfers between devices with their start and end apart: 31, of which 20 were waited for; matrix products, arithmetic and copies ran while one was open for 5% of the time, Pallas kernels for 1%

profile of v1, /device:TPU:0, one launch (start us, length us, event | category | flops | bytes accessed | tf_op | source)
XLA Modules:
  0.0 142.4 jit_solution(12949073243459647304)
XLA Ops:
  0.6 1.9 %dynamic-slice_bitcast_fusion = (f32[128,512]{1,0:T(8,128)}, f32[128,512]{1,0:T(8,128)}) fusion(f32[2,512,512]{2,1,0:T(8,128)} %own.1, s32[]{:T(128)S(6)} %select_n.127, s32[]{:T(128)S(6)} %add.77), kind=kLoop, calls=%fused_computation.5 | loop fusion | bytes 1048584 | tf_op jit(solution)/shard_map/slice | solution.py:368
  2.5 4.9 %collective-permute-start = (f32[128,512]{1,0:T(8,128)}, f32[128,512]{1,0:T(8,128)S(1)}, u32[]{:S(2)}, u32[]{:S(2)}) collective-permute-start(f32[128,512]{1,0:T(8,128)} %get-tuple-element.27), channel_id=1, source_target_pairs={{0,4},{4,8},{8,12},{1,5},{5,9},{9,13},{2,6},{6,10},{10,14},{3,7},{... | collective-permute-start | bytes 786440 | tf_op jit(solution)/shard_map/ppermute | solution.py:367
  7.4 1.3 collective-permute-start.1
  8.8 1.8 %dynamic-slice_bitcast_fusion.2 = f32[512,128]{1,0:T(8,128)} fusion(f32[2,512,512]{2,1,0:T(8,128)} %own.1, s32[]{:T(128)S(6)} %select_n.128, s32[]{:T(128)S(6)} %select_n.129), kind=kLoop, calls=%fused_computation.27 | loop fusion | bytes 524296 | tf_op jit(solution)/shard_map/dynamic_slice | solution.py:377
  10.6 1.6 %collective-permute-start.2 = (f32[512,128]{1,0:T(8,128)}, f32[512,128]{1,0:T(8,128)S(1)}, u32[]{:S(2)}, u32[]{:S(2)}) collective-permute-start(f32[512,128]{1,0:T(8,128)} %dynamic-slice_bitcast_fusion.2), channel_id=1, source_target_pairs={{0,2},{2,0},{1,3},{3,1},{4,6},{6,4},{5,7},{7,5},{8,10},{10,8},{9,1... | collective-permute-start | bytes 786440 | tf_op jit(solution)/shard_map/ppermute | solution.py:378
  12.2 1.6 %dynamic-slice_bitcast_fusion.3 = (f32[128,128]{1,0:T(8,128)}, f32[128,128]{1,0:T(8,128)}) fusion(f32[2,512,512]{2,1,0:T(8,128)} %own.1, s32[]{:T(128)S(6)} %select_n.128, s32[]{:T(128)S(6)} %select_n.129, s32[]{:T(128)S(6)} %add.77), kind=kLoop, calls=%fused_computation.32 | loop fusion | bytes 262156 | tf_op jit(solution)/shard_map/slice | solution.py:387
  13.8 4.7 %collective-permute-start.3 = (f32[128,128]{1,0:T(8,128)}, f32[128,128]{1,0:T(8,128)S(1)}, u32[]{:S(2)}, u32[]{:S(2)}) collective-permute-start(f32[128,128]{1,0:T(8,128)} %get-tuple-element.25), channel_id=1, source_target_pairs={{0,6},{2,4},{4,10},{6,8},{8,14},{10,12},{1,7},{3,5},{5,11},{7,9},{... | collective-permute-start | bytes 196616 | tf_op jit(solution)/shard_map/ppermute | solution.py:381
  18.5 1.3 collective-permute-start.4
  19.8 0.8 reshape_squeeze.3
  20.7 5.1 %collective-permute-done.4.dl.dr = f32[128,128]{1,0:T(8,128)S(1)} collective-permute-done((f32[128,128]{1,0:T(8,128)}, f32[128,128]{1,0:T(8,128)S(1)}, u32[]{:S(2)}, u32[]{:S(2)}) %collective-permute-start.4) | collective-permute-done | bytes 65568 | tf_op jit(solution)/shard_map/ppermute | solution.py:386
  25.8 0.7 copy-done.14
  26.5 0.7 copy-done.16
  27.2 1.6 %copy-done.1 = f32[2,512,512]{2,1,0:T(8,128)S(1)} copy-done((f32[2,512,512]{2,1,0:T(8,128)S(1)}, f32[2,512,512]{2,1,0:T(8,128)}, u32[]{:S(2)}) %copy-start.1) | copy-done | bytes 2097176
  28.8 0.9 copy-done.15
  29.8 0.9 copy-done.17
  30.7 1.0 cut.1.mine
  31.8 1.9 %collective-permute-done.5.other = f32[2,256,256]{2,1,0:T(8,128)S(1)} collective-permute-done((f32[2,256,256]{2,1,0:T(8,128)S(1)}, f32[2,256,256]{2,1,0:T(8,128)S(1)}, u32[]{:S(2)}, u32[]{:S(2)}) %collective-permute-start.5) | collective-permute-done | bytes 524320 | tf_op jit(solution)/shard_map/ppermute | solution.py:322
  33.7 1.0 copy-done.5
  34.8 4.6 %forward.1 = (f32[4,2,256,512]{3,2,1,0:T(8,128)S(1)}, f32[2,256,256]{2,1,0:T(8,128)}) custom-call(s32[1]{0:T(128)} %bitcast.2.info, f32[4,2,256,256]{3,2,1,0:T(8,128)S(1)} %copy-done, f32[2,256,256]{2,1,0:T(8,128)S(1)} %cut.1.mine, f32[2,256,256]{2,1,0:T(8,128)S(1)} %collective-permute-done.5.other, bf16[512,512]{1,0:T(8,128)(2,1)S(1)} %copy-done.4, ...), custom_call_target="tpu_custom_call" | custom-call | tf_op jit(solution)/shard_map/forward/pallas_call | solution.py:126
  39.4 2.0 %copy-done.2 = f32[4,2,256,512]{3,2,1,0:T(8,128)} copy-done((f32[4,2,256,512]{3,2,1,0:T(8,128)}, f32[4,2,256,512]{3,2,1,0:T(8,128)S(1)}, u32[]{:S(2)}) %copy-start.2) | copy-done | bytes 4194328
  42.3 1.4 collective-permute-done.6.power_other
  43.7 2.2 %copy-done.3 = f32[4,2,256,512]{3,2,1,0:T(8,128)S(1)} copy-done((f32[4,2,256,512]{3,2,1,0:T(8,128)S(1)}, f32[4,2,256,512]{3,2,1,0:T(8,128)}, u32[]{:S(2)}) %copy-start.3) | copy-done | bytes 4194328
  45.9 1.0 copy-done.6
  46.9 1.0 copy-done.8
  47.9 1.0 copy-done.11
  49.0 6.1 %backward.1 = (f32[4,256,256]{2,1,0:T(8,128)S(1)}, f32[4,256,256]{2,1,0:T(8,128)S(1)}, f32[2,256,256]{2,1,0:T(8,128)S(1)}, f32[2,256,256]{2,1,0:T(8,128)S(1)}) custom-call(s32[3]{0:T(128)S(1)} %pad_add_fusion.1.info, f32[4,2,256,256]{3,2,1,0:T(8,128)S(1)} %copy-done, f32[2,256,256]{2,1,0:T(8,128)S(1)} %cut.1.mine, f32[2,256,256]{2,1,0:T(8,128)S(1)} %copy-done.8, ...), custom_call_target="tpu_custom_call" | custom-call | tf_op jit(solution)/shard_map/backward/pallas_call | solution.py:202
  55.1 1.0 copy-done.9
  56.1 0.8 slice_bitcast_fusion.3
  57.1 1.3 collective-permute-start.11
  58.4 0.7 collective-permute-start.26
  59.1 1.3 collective-permute-start.21
  60.4 0.7 collective-permute-start.16
  61.2 5.3 %collective-permute-done.11 = f32[256,256]{1,0:T(8,128)S(1)} collective-permute-done((f32[256,256]{1,0:T(8,128)}, f32[256,256]{1,0:T(8,128)S(1)}, u32[]{:S(2)}, u32[]{:S(2)}) %collective-permute-start.11) | collective-permute-done | bytes 262176 | tf_op jit(solution)/shard_map/ppermute | solution.py:322
  66.5 5.6 %collective-permute-done.26 = f32[256,256]{1,0:T(8,128)S(1)} collective-permute-done((f32[256,256]{1,0:T(8,128)S(1)}, f32[256,256]{1,0:T(8,128)S(1)}, u32[]{:S(2)}, u32[]{:S(2)}) %collective-permute-start.26) | collective-permute-done | bytes 262176 | tf_op jit(solution)/shard_map/ppermute | solution.py:322
  72.1 5.6 %collective-permute-done.21 = f32[256,256]{1,0:T(8,128)S(1)} collective-permute-done((f32[256,256]{1,0:T(8,128)S(1)}, f32[256,256]{1,0:T(8,128)S(1)}, u32[]{:S(2)}, u32[]{:S(2)}) %collective-permute-start.21) | collective-permute-done | bytes 262176 | tf_op jit(solution)/shard_map/ppermute | solution.py:322
  77.7 4.8 %collective-permute-done.16 = f32[256,256]{1,0:T(8,128)S(1)} collective-permute-done((f32[256,256]{1,0:T(8,128)S(1)}, f32[256,256]{1,0:T(8,128)S(1)}, u32[]{:S(2)}, u32[]{:S(2)}) %collective-permute-start.16) | collective-permute-done | bytes 262176 | tf_op jit(solution)/shard_map/ppermute | solution.py:322
  82.7 1.6 %collective-permute-start.22 = (f32[128,256]{1,0:T(8,128)S(1)}, f32[128,256]{1,0:T(8,128)S(1)}, u32[]{:S(2)}, u32[]{:S(2)}) collective-permute-start(f32[128,256]{1,0:T(8,128)S(1)} %constant_dynamic-slice_fusion.1), channel_id=1, source_target_pairs={{0,4},{4,0},{8,12},{12,8},{1,5},{5,1},{9,13},{13,9},{2,6},{6,2},{1... | collective-permute-start | bytes 393224 | tf_op jit(solution)/shard_map/ppermute | solution.py:322
  84.9 1.6 %collective-permute-start.12 = (f32[128,256]{1,0:T(8,128)S(1)}, f32[128,256]{1,0:T(8,128)S(1)}, u32[]{:S(2)}, u32[]{:S(2)}) collective-permute-start(f32[128,256]{1,0:T(8,128)S(1)} %constant_dynamic-slice_fusion.3), channel_id=1, source_target_pairs={{0,4},{4,0},{8,12},{12,8},{1,5},{5,1},{9,13},{13,9},{2,6},{6,2},{1... | collective-permute-start | bytes 393224 | tf_op jit(solution)/shard_map/ppermute | solution.py:322
  87.1 2.1 %collective-permute-done.22 = f32[128,256]{1,0:T(8,128)S(1)} collective-permute-done((f32[128,256]{1,0:T(8,128)S(1)}, f32[128,256]{1,0:T(8,128)S(1)}, u32[]{:S(2)}, u32[]{:S(2)}) %collective-permute-start.22) | collective-permute-done | bytes 131104 | tf_op jit(solution)/shard_map/ppermute | solution.py:322
  89.2 2.7 %collective-permute-start.23 = (f32[128,256]{1,0:T(8,128)S(1)}, f32[128,256]{1,0:T(8,128)S(1)}, u32[]{:S(2)}, u32[]{:S(2)}) collective-permute-start(f32[128,256]{1,0:T(8,128)S(1)} %dynamic-slice_add_fusion.1), channel_id=1, source_target_pairs={{0,8},{4,12},{8,0},{12,4},{1,9},{5,13},{9,1},{13,5},{2,10},{6,14},... | collective-permute-start | bytes 393224 | tf_op jit(solution)/shard_map/ppermute | solution.py:322
  91.9 4.3 %collective-permute-done.27 = f32[128,256]{1,0:T(8,128)S(1)} collective-permute-done((f32[128,256]{1,0:T(8,128)S(1)}, f32[128,256]{1,0:T(8,128)S(1)}, u32[]{:S(2)}, u32[]{:S(2)}) %collective-permute-start.27) | collective-permute-done | bytes 131104 | tf_op jit(solution)/shard_map/ppermute | solution.py:322
  96.3 2.4 %collective-permute-done.12 = f32[128,256]{1,0:T(8,128)S(1)} collective-permute-done((f32[128,256]{1,0:T(8,128)S(1)}, f32[128,256]{1,0:T(8,128)S(1)}, u32[]{:S(2)}, u32[]{:S(2)}) %collective-permute-start.12) | collective-permute-done | bytes 131104 | tf_op jit(solution)/shard_map/ppermute | solution.py:322
  99.3 1.1 collective-permute-done.17
  100.4 1.4 collective-permute-start.18
  101.9 1.4 collective-permute-start.24
  103.3 1.2 place.1
  104.5 1.4 collective-permute-start.8
  105.9 6.2 %collective-permute-done.28 = f32[128,256]{1,0:T(8,128)S(1)} collective-permute-done((f32[128,256]{1,0:T(8,128)S(1)}, f32[128,256]{1,0:T(8,128)S(1)}, u32[]{:S(2)}, u32[]{:S(2)}) %collective-permute-start.28) | collective-permute-done | bytes 131104 | tf_op jit(solution)/shard_map/ppermute | solution.py:322
  112.2 2.5 %collective-permute-done.13 = f32[128,256]{1,0:T(8,128)S(1)} collective-permute-done((f32[128,256]{1,0:T(8,128)S(1)}, f32[128,256]{1,0:T(8,128)S(1)}, u32[]{:S(2)}, u32[]{:S(2)}) %collective-permute-start.13) | collective-permute-done | bytes 131104 | tf_op jit(solution)/shard_map/ppermute | solution.py:322
  114.8 1.4 collective-permute-done.18
  116.2 0.7 collective-permute-start.19
  116.9 1.3 collective-permute-start.25
  118.2 0.7 collective-permute-done.29
  119.0 1.3 collective-permute-start.30
  120.3 1.3 collective-permute-done.14
  121.7 1.3 collective-permute-start.15
  123.1 1.3 collective-permute-start.20
  124.6 1.5 %collective-permute-start.9 = (f32[128,512]{1,0:T(8,128)S(1)}, f32[128,512]{1,0:T(8,128)S(1)}, u32[]{:S(2)}, u32[]{:S(2)}) collective-permute-start(f32[128,512]{1,0:T(8,128)S(1)} %get-tuple-element.20), channel_id=1, source_target_pairs={{0,4},{4,8},{8,12},{1,5},{5,9},{9,13},{2,6},{6,10},{10,14},{3,7},{... | collective-permute-start | bytes 786440 | tf_op jit(solution)/shard_map/ppermute | solution.py:428
  126.2 1.3 collective-permute-start.10
  127.6 4.3 %collective-permute-done.30 = f32[256,256]{1,0:T(8,128)S(1)} collective-permute-done((f32[256,256]{1,0:T(8,128)S(1)}, f32[256,256]{1,0:T(8,128)S(1)}, u32[]{:S(2)}, u32[]{:S(2)}) %collective-permute-start.30) | collective-permute-done | bytes 262176 | tf_op jit(solution)/shard_map/ppermute | solution.py:322
  132.0 5.0 %collective-permute-done.15 = f32[256,256]{1,0:T(8,128)S(1)} collective-permute-done((f32[256,256]{1,0:T(8,128)S(1)}, f32[256,256]{1,0:T(8,128)S(1)}, u32[]{:S(2)}, u32[]{:S(2)}) %collective-permute-start.15) | collective-permute-done | bytes 262176 | tf_op jit(solution)/shard_map/ppermute | solution.py:322
  137.0 2.8 %collective-permute-done.20 = f32[256,256]{1,0:T(8,128)S(1)} collective-permute-done((f32[256,256]{1,0:T(8,128)S(1)}, f32[256,256]{1,0:T(8,128)S(1)}, u32[]{:S(2)}, u32[]{:S(2)}) %collective-permute-start.20) | collective-permute-done | bytes 262176 | tf_op jit(solution)/shard_map/ppermute | solution.py:322
  139.9 1.5 %pad_maximum_fusion = f32[4,2,256,256]{3,2,1,0:T(8,128)} fusion(f32[1,2,256,256]{3,2,1,0:T(8,128)S(1)} %get-tuple-element.55, f32[1,2,256,256]{3,2,1,0:T(8,128)S(1)} %get-tuple-element.54, f32[1,2,256,256]{3,2,1,0:T(8,128)S(1)} %get-tuple-element.53, f32[1,2,256,256]{3,2,1,0:T(8,128)S(1)} %get-tuple-element.52), kind=kLoop, calls=%fused_computation | loop fusion | flops 1572864 | bytes 4194304 | tf_op jit(solution)/shard_map/stack | solution.py:413
  141.4 1.1 finish.1
  (78 shorter events, 3.8 us)
Async XLA Ops:
  2.5 23.3 %collective-permute-start = (f32[128,512]{1,0:T(8,128)}, f32[128,512]{1,0:T(8,128)S(1)}, u32[]{:S(2)}, u32[]{:S(2)}) collective-permute-start(f32[128,512]{1,0:T(8,128)} %get-tuple-element.27), channel_id=1, source_target_pairs={{0,4},{4,8},{8,12},{1,5},{5,9},{9,13},{2,6},{6,10},{10,14},{3,7},{... | collective-permute-start | bytes 786440 | tf_op jit(solution)/shard_map/ppermute | solution.py:367
  7.4 19.1 %collective-permute-start.1 = (f32[128,512]{1,0:T(8,128)}, f32[128,512]{1,0:T(8,128)S(1)}, u32[]{:S(2)}, u32[]{:S(2)}) collective-permute-start(f32[128,512]{1,0:T(8,128)} %get-tuple-element.26), channel_id=1, source_target_pairs={{4,0},{8,4},{12,8},{5,1},{9,5},{13,9},{6,2},{10,6},{14,10},{7,3},{... | collective-permute-start | bytes 786440 | tf_op jit(solution)/shard_map/ppermute | solution.py:368
  8.8 25.0 %copy-start.4 = (bf16[512,512]{1,0:T(8,128)(2,1)S(1)}, bf16[512,512]{1,0:T(8,128)(2,1)}, u32[]{:S(2)}) copy-start(bf16[512,512]{1,0:T(8,128)(2,1)} %constant.50.clone.left) | copy-start | bytes 1572868
  10.6 23.1 %copy-start = (f32[4,2,256,256]{3,2,1,0:T(8,128)S(1)}, f32[4,2,256,256]{3,2,1,0:T(8,128)}, u32[]{:S(2)}) copy-start(f32[4,2,256,256]{3,2,1,0:T(8,128)} %probe.3) | copy-start | bytes 6291460
  10.6 16.6 %collective-permute-start.2 = (f32[512,128]{1,0:T(8,128)}, f32[512,128]{1,0:T(8,128)S(1)}, u32[]{:S(2)}, u32[]{:S(2)}) collective-permute-start(f32[512,128]{1,0:T(8,128)} %dynamic-slice_bitcast_fusion.2), channel_id=1, source_target_pairs={{0,2},{2,0},{1,3},{3,1},{4,6},{6,4},{5,7},{7,5},{8,10},{10,8},{9,1... | collective-permute-start | bytes 786440 | tf_op jit(solution)/shard_map/ppermute | solution.py:378
  13.8 6.9 %collective-permute-start.3 = (f32[128,128]{1,0:T(8,128)}, f32[128,128]{1,0:T(8,128)S(1)}, u32[]{:S(2)}, u32[]{:S(2)}) collective-permute-start(f32[128,128]{1,0:T(8,128)} %get-tuple-element.25), channel_id=1, source_target_pairs={{0,6},{2,4},{4,10},{6,8},{8,14},{10,12},{1,7},{3,5},{5,11},{7,9},{... | collective-permute-start | bytes 196616 | tf_op jit(solution)/shard_map/ppermute | solution.py:381
  18.5 7.3 %collective-permute-start.4 = (f32[128,128]{1,0:T(8,128)}, f32[128,128]{1,0:T(8,128)S(1)}, u32[]{:S(2)}, u32[]{:S(2)}) collective-permute-start(f32[128,128]{1,0:T(8,128)} %get-tuple-element.24), channel_id=1, source_target_pairs={{4,2},{6,0},{8,6},{10,4},{12,10},{14,8},{5,3},{7,1},{9,7},{11,5},{... | collective-permute-start | bytes 196616 | tf_op jit(solution)/shard_map/ppermute | solution.py:386
  25.8 0.7 copy-start.14
  26.5 0.7 copy-start.16
  27.2 1.6 %copy-start.1 = (f32[2,512,512]{2,1,0:T(8,128)S(1)}, f32[2,512,512]{2,1,0:T(8,128)}, u32[]{:S(2)}) copy-start(f32[2,512,512]{2,1,0:T(8,128)} %own.1) | copy-start | bytes 6291460
  28.8 0.9 copy-start.15
  29.8 0.9 copy-start.17
  31.8 2.0 %collective-permute-start.5 = (f32[2,256,256]{2,1,0:T(8,128)S(1)}, f32[2,256,256]{2,1,0:T(8,128)S(1)}, u32[]{:S(2)}, u32[]{:S(2)}) collective-permute-start(f32[2,256,256]{2,1,0:T(8,128)S(1)} %cut.1.mine), channel_id=1, source_target_pairs={{0,1},{1,0},{2,3},{3,2},{4,5},{5,4},{6,7},{7,6},{8,9},{9,8},{10,11... | collective-permute-start | bytes 1572872 | tf_op jit(solution)/shard_map/ppermute | solution.py:322
  33.7 1.0 copy-start.5
  34.8 4.6 %copy-start.7 = (f32[2,256,256]{2,1,0:T(8,128)}, f32[2,256,256]{2,1,0:T(8,128)S(1)}, u32[]{:S(2)}) copy-start(f32[2,256,256]{2,1,0:T(8,128)S(1)} %collective-permute-done.5.other) | copy-start | bytes 1572868
  39.4 2.0 %copy-start.2 = (f32[4,2,256,512]{3,2,1,0:T(8,128)}, f32[4,2,256,512]{3,2,1,0:T(8,128)S(1)}, u32[]{:S(2)}) copy-start(f32[4,2,256,512]{3,2,1,0:T(8,128)S(1)} %get-tuple-element.14.spectrum) | copy-start | bytes 12582916
  41.4 2.3 %collective-permute-start.6 = (f32[2,256,256]{2,1,0:T(8,128)}, f32[2,256,256]{2,1,0:T(8,128)}, u32[]{:S(2)}, u32[]{:S(2)}) collective-permute-start(f32[2,256,256]{2,1,0:T(8,128)} %get-tuple-element.13.power), channel_id=1, source_target_pairs={{0,1},{1,0},{2,3},{3,2},{4,5},{5,4},{6,7},{7,6},{8,9},{9,8},{10,11... | collective-permute-start | bytes 1572872 | tf_op jit(solution)/shard_map/ppermute | solution.py:322
  43.7 2.2 %copy-start.3 = (f32[4,2,256,512]{3,2,1,0:T(8,128)S(1)}, f32[4,2,256,512]{3,2,1,0:T(8,128)}, u32[]{:S(2)}) copy-start(f32[4,2,256,512]{3,2,1,0:T(8,128)} %copy-done.2) | copy-start | bytes 12582916
  45.9 1.0 copy-start.6
  46.9 1.0 copy-start.8
  47.9 1.0 copy-start.11
  55.1 1.0 copy-start.9
  56.0 0.9 copy-start.12
  56.0 1.1 copy-start.18
  56.1 26.5 %copy-start.10 = (f32[4,256,256]{2,1,0:T(8,128)S(1)}, f32[4,256,256]{2,1,0:T(8,128)}, u32[]{:S(2)}) copy-start(f32[4,256,256]{2,1,0:T(8,128)} %copy-done.9) | copy-start | bytes 3145732
  57.1 9.4 %collective-permute-start.11 = (f32[256,256]{1,0:T(8,128)}, f32[256,256]{1,0:T(8,128)S(1)}, u32[]{:S(2)}, u32[]{:S(2)}) collective-permute-start(f32[256,256]{1,0:T(8,128)} %get-tuple-element.32), channel_id=1, source_target_pairs={{0,2},{2,0},{1,3},{3,1},{4,6},{6,4},{5,7},{7,5},{8,10},{10,8},{9,1... | collective-permute-start | bytes 786440 | tf_op jit(solution)/shard_map/ppermute | solution.py:322
  58.4 13.7 %collective-permute-start.26 = (f32[256,256]{1,0:T(8,128)S(1)}, f32[256,256]{1,0:T(8,128)S(1)}, u32[]{:S(2)}, u32[]{:S(2)}) collective-permute-start(f32[256,256]{1,0:T(8,128)S(1)} %get-tuple-element.33), channel_id=1, source_target_pairs={{0,2},{2,0},{1,3},{3,1},{4,6},{6,4},{5,7},{7,5},{8,10},{10,8},{9,1... | collective-permute-start | bytes 786440 | tf_op jit(solution)/shard_map/ppermute | solution.py:322
  59.1 18.6 %collective-permute-start.21 = (f32[256,256]{1,0:T(8,128)S(1)}, f32[256,256]{1,0:T(8,128)S(1)}, u32[]{:S(2)}, u32[]{:S(2)}) collective-permute-start(f32[256,256]{1,0:T(8,128)S(1)} %get-tuple-element.34), channel_id=1, source_target_pairs={{0,2},{2,0},{1,3},{3,1},{4,6},{6,4},{5,7},{7,5},{8,10},{10,8},{9,1... | collective-permute-start | bytes 786440 | tf_op jit(solution)/shard_map/ppermute | solution.py:322
  60.4 22.1 %collective-permute-start.16 = (f32[256,256]{1,0:T(8,128)S(1)}, f32[256,256]{1,0:T(8,128)S(1)}, u32[]{:S(2)}, u32[]{:S(2)}) collective-permute-start(f32[256,256]{1,0:T(8,128)S(1)} %get-tuple-element.35), channel_id=1, source_target_pairs={{0,2},{2,0},{1,3},{3,1},{4,6},{6,4},{5,7},{7,5},{8,10},{10,8},{9,1... | collective-permute-start | bytes 786440 | tf_op jit(solution)/shard_map/ppermute | solution.py:322
  61.2 42.1 %collective-permute-start.7 = (f32[2,256,256]{2,1,0:T(8,128)}, f32[2,256,256]{2,1,0:T(8,128)S(1)}, u32[]{:S(2)}, u32[]{:S(2)}) collective-permute-start(f32[2,256,256]{2,1,0:T(8,128)} %copy-done.18), channel_id=1, source_target_pairs={{0,1},{1,0},{2,3},{3,2},{4,5},{5,4},{6,7},{7,6},{8,9},{9,8},{10,11... | collective-permute-start | bytes 1572872 | tf_op jit(solution)/shard_map/ppermute | solution.py:322
  82.7 20.6 %copy-start.13 = (f32[2,256,256]{2,1,0:T(8,128)S(1)}, f32[2,256,256]{2,1,0:T(8,128)}, u32[]{:S(2)}) copy-start(f32[2,256,256]{2,1,0:T(8,128)} %copy-done.12) | copy-start | bytes 1572868
  82.7 6.5 %collective-permute-start.22 = (f32[128,256]{1,0:T(8,128)S(1)}, f32[128,256]{1,0:T(8,128)S(1)}, u32[]{:S(2)}, u32[]{:S(2)}) collective-permute-start(f32[128,256]{1,0:T(8,128)S(1)} %constant_dynamic-slice_fusion.1), channel_id=1, source_target_pairs={{0,4},{4,0},{8,12},{12,8},{1,5},{5,1},{9,13},{13,9},{2,6},{6,2},{1... | collective-permute-start | bytes 393224 | tf_op jit(solution)/shard_map/ppermute | solution.py:322
  84.4 11.9 %collective-permute-start.27 = (f32[128,256]{1,0:T(8,128)S(1)}, f32[128,256]{1,0:T(8,128)S(1)}, u32[]{:S(2)}, u32[]{:S(2)}) collective-permute-start(f32[128,256]{1,0:T(8,128)S(1)} %constant_dynamic-slice_fusion), channel_id=1, source_target_pairs={{0,4},{4,0},{8,12},{12,8},{1,5},{5,1},{9,13},{13,9},{2,6},{6,2},{1... | collective-permute-start | bytes 393224 | tf_op jit(solution)/shard_map/ppermute | solution.py:322
  84.9 13.8 %collective-permute-start.12 = (f32[128,256]{1,0:T(8,128)S(1)}, f32[128,256]{1,0:T(8,128)S(1)}, u32[]{:S(2)}, u32[]{:S(2)}) collective-permute-start(f32[128,256]{1,0:T(8,128)S(1)} %constant_dynamic-slice_fusion.3), channel_id=1, source_target_pairs={{0,4},{4,0},{8,12},{12,8},{1,5},{5,1},{9,13},{13,9},{2,6},{6,2},{1... | collective-permute-start | bytes 393224 | tf_op jit(solution)/shard_map/ppermute | solution.py:322
  86.5 13.9 %collective-permute-start.17 = (f32[128,256]{1,0:T(8,128)S(1)}, f32[128,256]{1,0:T(8,128)S(1)}, u32[]{:S(2)}, u32[]{:S(2)}) collective-permute-start(f32[128,256]{1,0:T(8,128)S(1)} %constant_dynamic-slice_fusion.2), channel_id=1, source_target_pairs={{0,4},{4,0},{8,12},{12,8},{1,5},{5,1},{9,13},{13,9},{2,6},{6,2},{1... | collective-permute-start | bytes 393224 | tf_op jit(solution)/shard_map/ppermute | solution.py:322
  89.2 12.6 %collective-permute-start.23 = (f32[128,256]{1,0:T(8,128)S(1)}, f32[128,256]{1,0:T(8,128)S(1)}, u32[]{:S(2)}, u32[]{:S(2)}) collective-permute-start(f32[128,256]{1,0:T(8,128)S(1)} %dynamic-slice_add_fusion.1), channel_id=1, source_target_pairs={{0,8},{4,12},{8,0},{12,4},{1,9},{5,13},{9,1},{13,5},{2,10},{6,14},... | collective-permute-start | bytes 393224 | tf_op jit(solution)/shard_map/ppermute | solution.py:322
  96.3 15.8 %collective-permute-start.28 = (f32[128,256]{1,0:T(8,128)S(1)}, f32[128,256]{1,0:T(8,128)S(1)}, u32[]{:S(2)}, u32[]{:S(2)}) collective-permute-start(f32[128,256]{1,0:T(8,128)S(1)} %dynamic-slice_add_fusion), channel_id=1, source_target_pairs={{0,8},{4,12},{8,0},{12,4},{1,9},{5,13},{9,1},{13,5},{2,10},{6,14},... | collective-permute-start | bytes 393224 | tf_op jit(solution)/shard_map/ppermute | solution.py:322
  98.8 15.9 %collective-permute-start.13 = (f32[128,256]{1,0:T(8,128)S(1)}, f32[128,256]{1,0:T(8,128)S(1)}, u32[]{:S(2)}, u32[]{:S(2)}) collective-permute-start(f32[128,256]{1,0:T(8,128)S(1)} %dynamic-slice_add_fusion.3), channel_id=1, source_target_pairs={{0,8},{4,12},{8,0},{12,4},{1,9},{5,13},{9,1},{13,5},{2,10},{6,14},... | collective-permute-start | bytes 393224 | tf_op jit(solution)/shard_map/ppermute | solution.py:322
  100.4 15.7 %collective-permute-start.18 = (f32[128,256]{1,0:T(8,128)S(1)}, f32[128,256]{1,0:T(8,128)S(1)}, u32[]{:S(2)}, u32[]{:S(2)}) collective-permute-start(f32[128,256]{1,0:T(8,128)S(1)} %dynamic-slice_add_fusion.2), channel_id=1, source_target_pairs={{0,8},{4,12},{8,0},{12,4},{1,9},{5,13},{9,1},{13,5},{2,10},{6,14},... | collective-permute-start | bytes 393224 | tf_op jit(solution)/shard_map/ppermute | solution.py:322
  101.9 15.0 %collective-permute-start.24 = (f32[128,256]{1,0:T(8,128)S(1)}, f32[128,256]{1,0:T(8,128)S(1)}, u32[]{:S(2)}, u32[]{:S(2)}) collective-permute-start(f32[128,256]{1,0:T(8,128)S(1)} %add.67), channel_id=1, source_target_pairs={{0,4},{4,0},{8,12},{12,8},{1,5},{5,1},{9,13},{13,9},{2,6},{6,2},{1... | collective-permute-start | bytes 393224 | tf_op jit(solution)/shard_map/ppermute | solution.py:322
  104.5 19.9 %collective-permute-start.8 = (f32[768,128]{1,0:T(8,128)S(1)}, f32[768,128]{1,0:T(8,128)S(1)}, u32[]{:S(2)}, u32[]{:S(2)}) collective-permute-start(f32[768,128]{1,0:T(8,128)S(1)} %bitcast.61), channel_id=1, source_target_pairs={{0,2},{2,0},{1,3},{3,1},{4,6},{6,4},{5,7},{7,5},{8,10},{10,8},{9,1... | collective-permute-start | bytes 1179656 | tf_op jit(solution)/shard_map/ppermute | solution.py:425
  112.1 6.8 %collective-permute-start.29 = (f32[128,256]{1,0:T(8,128)S(1)}, f32[128,256]{1,0:T(8,128)S(1)}, u32[]{:S(2)}, u32[]{:S(2)}) collective-permute-start(f32[128,256]{1,0:T(8,128)S(1)} %add.70), channel_id=1, source_target_pairs={{0,4},{4,0},{8,12},{12,8},{1,5},{5,1},{9,13},{13,9},{2,6},{6,2},{1... | collective-permute-start | bytes 393224 | tf_op jit(solution)/shard_map/ppermute | solution.py:322
  114.7 7.0 %collective-permute-start.14 = (f32[128,256]{1,0:T(8,128)S(1)}, f32[128,256]{1,0:T(8,128)S(1)}, u32[]{:S(2)}, u32[]{:S(2)}) collective-permute-start(f32[128,256]{1,0:T(8,128)S(1)} %add.61), channel_id=1, source_target_pairs={{0,4},{4,0},{8,12},{12,8},{1,5},{5,1},{9,13},{13,9},{2,6},{6,2},{1... | collective-permute-start | bytes 393224 | tf_op jit(solution)/shard_map/ppermute | solution.py:322
  116.2 6.9 %collective-permute-start.19 = (f32[128,256]{1,0:T(8,128)S(1)}, f32[128,256]{1,0:T(8,128)S(1)}, u32[]{:S(2)}, u32[]{:S(2)}) collective-permute-start(f32[128,256]{1,0:T(8,128)S(1)} %add.64), channel_id=1, source_target_pairs={{0,4},{4,0},{8,12},{12,8},{1,5},{5,1},{9,13},{13,9},{2,6},{6,2},{1... | collective-permute-start | bytes 393224 | tf_op jit(solution)/shard_map/ppermute | solution.py:322
  116.9 9.3 %collective-permute-start.25 = (f32[256,256]{1,0:T(8,128)S(1)}, f32[256,256]{1,0:T(8,128)S(1)}, u32[]{:S(2)}, u32[]{:S(2)}) collective-permute-start(f32[256,256]{1,0:T(8,128)S(1)} %pad_maximum_fusion.3), channel_id=1, source_target_pairs={{0,2},{2,0},{1,3},{3,1},{4,6},{6,4},{5,7},{7,5},{8,10},{10,8},{9,1... | collective-permute-start | bytes 786440 | tf_op jit(solution)/shard_map/ppermute | solution.py:322
  119.0 12.9 %collective-permute-start.30 = (f32[256,256]{1,0:T(8,128)S(1)}, f32[256,256]{1,0:T(8,128)S(1)}, u32[]{:S(2)}, u32[]{:S(2)}) collective-permute-start(f32[256,256]{1,0:T(8,128)S(1)} %pad_maximum_fusion.4), channel_id=1, source_target_pairs={{0,2},{2,0},{1,3},{3,1},{4,6},{6,4},{5,7},{7,5},{8,10},{10,8},{9,1... | collective-permute-start | bytes 786440 | tf_op jit(solution)/shard_map/ppermute | solution.py:322
  121.7 15.2 %collective-permute-start.15 = (f32[256,256]{1,0:T(8,128)S(1)}, f32[256,256]{1,0:T(8,128)S(1)}, u32[]{:S(2)}, u32[]{:S(2)}) collective-permute-start(f32[256,256]{1,0:T(8,128)S(1)} %pad_maximum_fusion.1), channel_id=1, source_target_pairs={{0,2},{2,0},{1,3},{3,1},{4,6},{6,4},{5,7},{7,5},{8,10},{10,8},{9,1... | collective-permute-start | bytes 786440 | tf_op jit(solution)/shard_map/ppermute | solution.py:322
  123.1 16.7 %collective-permute-start.20 = (f32[256,256]{1,0:T(8,128)S(1)}, f32[256,256]{1,0:T(8,128)S(1)}, u32[]{:S(2)}, u32[]{:S(2)}) collective-permute-start(f32[256,256]{1,0:T(8,128)S(1)} %pad_maximum_fusion.2), channel_id=1, source_target_pairs={{0,2},{2,0},{1,3},{3,1},{4,6},{6,4},{5,7},{7,5},{8,10},{10,8},{9,1... | collective-permute-start | bytes 786440 | tf_op jit(solution)/shard_map/ppermute | solution.py:322
  124.6 16.7 %collective-permute-start.9 = (f32[128,512]{1,0:T(8,128)S(1)}, f32[128,512]{1,0:T(8,128)S(1)}, u32[]{:S(2)}, u32[]{:S(2)}) collective-permute-start(f32[128,512]{1,0:T(8,128)S(1)} %get-tuple-element.20), channel_id=1, source_target_pairs={{0,4},{4,8},{8,12},{1,5},{5,9},{9,13},{2,6},{6,10},{10,14},{3,7},{... | collective-permute-start | bytes 786440 | tf_op jit(solution)/shard_map/ppermute | solution.py:428
  126.2 15.1 %collective-permute-start.10 = (f32[128,512]{1,0:T(8,128)S(1)}, f32[128,512]{1,0:T(8,128)S(1)}, u32[]{:S(2)}, u32[]{:S(2)}) collective-permute-start(f32[128,512]{1,0:T(8,128)S(1)} %get-tuple-element.21), channel_id=1, source_target_pairs={{4,0},{8,4},{12,8},{5,1},{9,5},{13,9},{6,2},{10,6},{14,10},{7,3},{... | collective-permute-start | bytes 786440 | tf_op jit(solution)/shard_map/ppermute | solution.py:427

commit v2 on v1

v2 whole, which is shorter than its diff:
```python
import functools
import math

import jax
import jax.numpy as jnp
import numpy as np
from jax import lax
from jax.experimental import pallas as pl
from jax.experimental.pallas import tpu as pltpu
from jax.sharding import PartitionSpec as P

damping = 0.1
LANES = 128
SUBLANES = 8
MIB = 1024 * 1024

CHUNKS = (("C", (0,)), ("A", (1,)), ("A", (2,)), ("A", (3,)))
ORDER = "0123410142321032140234023103"

f32 = jnp.float32
bf16 = jnp.bfloat16


def dft_blocks(size):
    index = np.arange(size, dtype=np.int64)
    angles = 2.0 * np.pi / size * (index[:, None] * index[None, :] % size)
    real = (np.cos(angles) / np.sqrt(size)).astype(np.float32).astype(bf16)
    imag = (-np.sin(angles) / np.sqrt(size)).astype(np.float32).astype(bf16)
    left = np.block([[real, -imag], [imag, real]])
    return left, np.ascontiguousarray(left.T)


def params(mebibytes):
    return pltpu.CompilerParams(vmem_limit_bytes=mebibytes * MIB)


def whole(shape):
    return pl.BlockSpec(shape, lambda *_: (0,) * len(shape))


ANYWHERE = pl.BlockSpec(memory_space=pl.ANY)
RESIDENT = pl.BlockSpec(memory_space=pltpu.VMEM)


def resident(value):
    return pltpu.with_memory_space_constraint(value, pltpu.VMEM)


def in_hbm(value):
    return pltpu.with_memory_space_constraint(value, pltpu.HBM)


def copies(sems):
    taken = iter(range(sems.shape[0]))

    def start(source, target):
        copy = pltpu.make_async_copy(source, target, sems.at[next(taken)])
        copy.start()
        return copy

    return start


def window_of(offset):
    base_row = pl.multiple_of(offset[0] // SUBLANES * SUBLANES, SUBLANES)
    base_col = pl.multiple_of(offset[1] // LANES * LANES, LANES)
    return base_row, base_col, offset[0] - base_row, offset[1] - base_col


def edges_kernel(margin, tile, groups, field, *refs):
    outs, sems = refs[:-1], refs[-1]
    start = copies(sems)
    own = field.at[lax.axis_index("mode")]
    moves = []
    for g in range(groups):
        if groups == 1:
            column = jnp.where(lax.axis_index("col") == 0, tile - margin, 0)
        else:
            column = (tile - margin, 0)[g]
        at = pl.ds(pl.multiple_of(column, LANES), margin)
        moves.append(start(own.at[:, at], outs[2 + g]))
    moves.append(start(own.at[pl.ds(0, margin)], outs[0]))
    moves.append(start(own.at[pl.ds(tile - margin, margin)], outs[1]))
    for move in moves:
        move.wait()


def edges(field, margin, groups):
    tile = field.shape[-1]
    shapes = [(margin, tile)] * 2 + [(tile, margin)] * groups
    return pl.pallas_call(
        functools.partial(edges_kernel, margin, tile, groups),
        in_specs=[ANYWHERE],
        out_specs=[RESIDENT] * len(shapes),
        out_shape=[pltpu.VMEM(s, f32) for s in shapes],
        scratch_shapes=[pltpu.SemaphoreType.DMA((len(shapes),))],
        compiler_params=params(1),
        name="edges",
    )(in_hbm(field))


def cut_kernel(
    size, margin, tile, slots, offsets, field, up, down, left, right, corners_left, corners_right, out, frame, sems
):
    start = copies(sems)
    low, high = pl.ds(0, margin), pl.ds(margin + tile, margin)
    mid = pl.ds(margin, tile)
    col = lax.axis_index("col")
    moves = [
        start(field.at[lax.axis_index("mode")], frame.at[mid, mid]),
        start(up, frame.at[low, mid]),
        start(down, frame.at[high, mid]),
        start(left, frame.at[mid, low]),
        start(right, frame.at[mid, high]),
        start(corners_left.at[0], frame.at[low, low]),
        start(corners_right.at[0], frame.at[low, high]),
        start(corners_left.at[1], frame.at[high, low]),
        start(corners_right.at[1], frame.at[high, high]),
    ]
    for move in moves:
        move.wait()
    span = tile + 2 * margin

    @pl.when(col == 0)
    def _():
        frame[0:span, 0:margin] = jnp.zeros((span, margin), f32)

    @pl.when(col == lax.axis_size("col") - 1)
    def _():
        frame[0:span, margin + tile : span] = jnp.zeros((span, margin), f32)

    rows, cols = size + SUBLANES, size + LANES
    for slot in range(slots):
        base_row, base_col, row, col = window_of((offsets[2 * slot], offsets[2 * slot + 1]))
        window = frame[pl.ds(base_row, rows), pl.ds(base_col, cols)]
        window = pltpu.roll(window, rows - row, 0)[:size]
        window = pltpu.roll(window, cols - col, 1)[:, :size]
        out[slot] = window


SMEM = pl.BlockSpec(memory_space=pltpu.SMEM)


def cut_patches(offsets, field, strips, size, slots):
    tile = field.shape[-1]
    margin = size // 2
    span = tile + 2 * margin
    return pl.pallas_call(
        functools.partial(cut_kernel, size, margin, tile, slots),
        in_specs=[SMEM, ANYWHERE] + [RESIDENT] * len(strips),
        out_specs=RESIDENT,
        out_shape=pltpu.VMEM((slots, size, size), f32),
        scratch_shapes=[
            pltpu.VMEM((span + SUBLANES, span + LANES), f32),
            pltpu.SemaphoreType.DMA((3 + len(strips),)),
        ],
        compiler_params=params(4),
        name="cut",
    )(offsets, in_hbm(field), *map(resident, strips))


def as_slot_rows(wave, size, slots):
    return jnp.concatenate(
        [
            jnp.concatenate(
                [wave[c * size : (c + 1) * size, s * size : (s + 1) * size] for c in range(2)], axis=1
            )
            for s in range(slots)
        ],
        axis=0,
    )


def staged(value):
    def kernel(source, target, sem):
        copy = pltpu.make_async_copy(source, target, sem)
        copy.start()
        copy.wait()

    return pl.pallas_call(
        kernel,
        in_specs=[ANYWHERE],
        out_specs=RESIDENT,
        out_shape=pltpu.VMEM(value.shape, value.dtype),
        scratch_shapes=[pltpu.SemaphoreType.DMA],
        compiler_params=params(1),
        name="stage",
    )(in_hbm(value))


def forward_kernel(size, slots, modes, mine, other, probes, tables, spectrum, power, spectrum_v, sems):
    start = copies(sems)
    leaving = []
    first = lax.axis_index("mode") == 0
    for m in range(modes):
        pr, pi = probes[m, 0], probes[m, 1]
        real, imag = [], []
        for s in range(slots):
            a, b = mine[s], other[s]
            qr, qi = jnp.where(first, a, b), jnp.where(first, b, a)
            real.append((pr * qr - pi * qi).astype(bf16))
            imag.append((pr * qi + pi * qr).astype(bf16))
        wave = jnp.concatenate([jnp.concatenate(real, axis=1), jnp.concatenate(imag, axis=1)], axis=0)
        half = jnp.dot(tables[0], wave, preferred_element_type=f32).astype(bf16)
        full = jnp.dot(as_slot_rows(half, size, slots), tables[1], preferred_element_type=f32)
        for s in range(slots):
            rows = full[s * size : (s + 1) * size]
            spectrum_v[m, s] = rows
            square = rows[:, :size] * rows[:, :size] + rows[:, size:] * rows[:, size:]
            power[s] = square if m == 0 else power[s] + square
        leaving.append(start(spectrum_v.at[m], spectrum.at[m]))
    for move in leaving:
        move.wait()


def forward(probes, mine, other, tables):
    modes, _, size, _ = probes.shape
    slots = mine.shape[0]
    spectra = (modes, slots, size, 2 * size)
    return pl.pallas_call(
        functools.partial(forward_kernel, size, slots, modes),
        in_specs=[RESIDENT] * 4,
        out_specs=[ANYWHERE, RESIDENT],
        out_shape=[pltpu.HBM(spectra, f32), pltpu.VMEM(mine.shape, f32)],
        scratch_shapes=[
            pltpu.VMEM(spectra, f32),
            pltpu.SemaphoreType.DMA((modes,)),
        ],
        compiler_params=params(8),
        name="forward",
    )(*map(resident, (mine, other, probes, tables)))


def backward_kernel(
    size, slots, chunks, scale, live, spectrum, amplitudes, tables, power, power_other, probes, mine, other, *refs
):
    outs, (spectrum_v, amplitudes_v, tables_v, planes_v, objects_v, weight, sems) = refs[:-7], refs[-7:]
    modes = probes.shape[0]
    start = copies(sems)
    fetched = start(amplitudes, amplitudes_v)
    arriving = [start(spectrum.at[0], spectrum_v.at[0])]
    needed = [start(tables.at[j], tables_v.at[j]) for j in (1, 0)]
    arriving += [start(spectrum.at[m], spectrum_v.at[m]) for m in range(1, modes)]
    leaving = []
    first = lax.axis_index("mode") == 0
    places = {m: (c, k) for c, chunk in enumerate(chunks) for k, m in enumerate(chunk)}
    fetched.wait()
    for s in range(slots):
        active = (s < live[0]).astype(f32)
        total = power[s] + power_other[s]
        weight[s] = active * (1.0 - amplitudes_v[s] / jnp.sqrt(total + damping))
    for m in range(modes):
        arriving[m].wait()
        real, imag = [], []
        for s in range(slots):
            w = weight[s]
            real.append((w * spectrum_v[m, s, :, :size]).astype(bf16))
            imag.append((w * spectrum_v[m, s, :, size:]).astype(bf16))
        hat = jnp.concatenate([jnp.concatenate(real, axis=1), jnp.concatenate(imag, axis=1)], axis=0)
        if m == 0:
            for move in needed:
                move.wait()
        half = jnp.dot(tables_v[1], hat, preferred_element_type=f32).astype(bf16)
        back = jnp.dot(as_slot_rows(half, size, slots), tables_v[0], preferred_element_type=f32)
        pr, pi = probes[m, 0], probes[m, 1]
        sum_real = sum_imag = None
        for s in range(slots):
            br = back[s * size : (s + 1) * size, :size]
            bi = back[s * size : (s + 1) * size, size:]
            a, b = mine[s], other[s]
            qr, qi = jnp.where(first, a, b), jnp.where(first, b, a)
            add_real, add_imag = qr * br + qi * bi, qr * bi - qi * br
            sum_real = add_real if s == 0 else sum_real + add_real
            sum_imag = add_imag if s == 0 else sum_imag + add_imag
            term_real = pr * br + pi * bi
            term_imag = pr * bi - pi * br
            terms = jnp.where(first, term_real, term_imag), jnp.where(first, term_imag, term_real)
            for j, term in enumerate(terms):
                objects_v[j, s] = term if m == 0 else objects_v[j, s] + term
        sum_real, sum_imag = sum_real * scale, sum_imag * scale
        if m > 1:
            for _ in range(2):
                leaving.pop(0).wait()
        c, k = places[m]
        low = live[1 + c] == 0
        planes_v[m % 2, 0] = jnp.where(low, sum_real, sum_imag)
        planes_v[m % 2, 1] = jnp.where(low, sum_imag, sum_real)
        rows = pl.ds(k * size, size)
        leaving += [start(planes_v.at[m % 2, j], outs[2 * c + j].at[rows]) for j in range(2)]
    leaving += [start(objects_v.at[j], outs[2 * len(chunks) + j]) for j in range(2)]
    for move in leaving:
        move.wait()


def backward(live, chunks, probes, mine, other, amplitudes, power, power_other, spectrum, tables, scale):
    modes, _, size, _ = probes.shape
    slots = mine.shape[0]
    operands = [power, power_other, probes, mine, other]
    planes = [pltpu.HBM((len(chunk) * size, size), f32) for chunk in chunks for _ in range(2)]
    return pl.pallas_call(
        functools.partial(backward_kernel, size, slots, chunks, scale),
        in_specs=[SMEM] + [ANYWHERE] * 3 + [RESIDENT] * len(operands),
        out_specs=[ANYWHERE] * (len(planes) + 2),
        out_shape=planes + [pltpu.HBM(mine.shape, f32)] * 2,
        scratch_shapes=[
            pltpu.VMEM(spectrum.shape, f32),
            pltpu.VMEM(mine.shape, f32),
            pltpu.VMEM(tables.shape, bf16),
            pltpu.VMEM((2, 2, size, size), f32),
            pltpu.VMEM((2,) + mine.shape, f32),
            pltpu.VMEM(mine.shape, f32),
            pltpu.SemaphoreType.DMA((3 * modes + 5,)),
        ],
        compiler_params=params(12),
        name="backward",
    )(live, *map(in_hbm, (spectrum, amplitudes, tables)), *map(resident, operands))


def place_kernel(size, margin, tile, slots, groups, info, mine, other, columns, strips, frame):
    span = tile + 2 * margin
    frame[...] = jnp.zeros_like(frame)
    rows, cols = size + SUBLANES, size + LANES
    for slot in range(slots):
        base_row, base_col, row, col = window_of((info[2 * slot], info[2 * slot + 1]))
        patch = mine[slot] + other[slot]
        window = jnp.concatenate([patch, jnp.zeros((SUBLANES, size), f32)], axis=0)
        window = pltpu.roll(window, row, 0)
        window = jnp.concatenate([window, jnp.zeros((rows, LANES), f32)], axis=1)
        window = pltpu.roll(window, col, 1)
        at = (pl.ds(base_row, rows), pl.ds(base_col, cols))
        frame[at] = frame[at] + window
    columns[...] = frame[0:span, margin : margin + tile]
    for g in range(groups):
        start = pl.multiple_of(info[2 * slots + g], LANES)
        strips[g] = frame[0:span, pl.ds(start, margin)]


def place(info, mine, other, tile, groups):
    slots, size, _ = mine.shape
    margin = size // 2
    span = tile + 2 * margin
    return pl.pallas_call(
        functools.partial(place_kernel, size, margin, tile, slots, groups),
        grid_spec=pltpu.PrefetchScalarGridSpec(
            num_scalar_prefetch=1,
            grid=(1,),
            in_specs=[whole(mine.shape), whole(other.shape)],
            out_specs=[whole((span, tile)), whole((groups, span, margin))],
            scratch_shapes=[pltpu.VMEM((span + SUBLANES, span + LANES), f32)],
        ),
        out_shape=[
            jax.ShapeDtypeStruct((span, tile), f32),
            jax.ShapeDtypeStruct((groups, span, margin), f32),
        ],
        compiler_params=params(5),
        name="place",
    )(info, mine, other)


def merge_kernel(margin, tile, groups, info, columns, *refs):
    arrived, (top, middle, bottom) = refs[:groups], refs[groups:]
    top[...] = columns[0:margin]
    middle[...] = columns[margin : margin + tile]
    bottom[...] = columns[margin + tile :]
    for g in range(groups):
        at = pl.ds(pl.multiple_of(info[g], LANES), margin)
        top[:, at] = top[:, at] + arrived[g][0:margin]
        middle[:, at] = middle[:, at] + arrived[g][margin : margin + tile]
        bottom[:, at] = bottom[:, at] + arrived[g][margin + tile :]


def merge(info, columns, arrived):
    span, tile = columns.shape
    margin = (span - tile) // 2
    shapes = [(margin, tile), (tile, tile), (margin, tile)]
    return pl.pallas_call(
        functools.partial(merge_kernel, margin, tile, len(arrived)),
        grid_spec=pltpu.PrefetchScalarGridSpec(
            num_scalar_prefetch=1,
            grid=(1,),
            in_specs=[whole(columns.shape)] + [whole(a.shape) for a in arrived],
            out_specs=[whole(s) for s in shapes],
        ),
        out_shape=[jax.ShapeDtypeStruct(s, f32) for s in shapes],
        compiler_params=params(2),
        name="merge",
    )(info, columns, *arrived)


def finish_kernel(margin, tile, middle, above, below, out):
    out[0, 0:margin] = middle[0:margin] + above[...]
    out[0, margin : tile - margin] = middle[margin : tile - margin]
    out[0, tile - margin :] = middle[tile - margin :] + below[...]


def finish(middle, above, below):
    tile = middle.shape[0]
    margin = above.shape[0]
    return pl.pallas_call(
        functools.partial(finish_kernel, margin, tile),
        out_shape=jax.ShapeDtypeStruct((1, tile, tile), f32),
        compiler_params=params(2),
        name="finish",
    )(middle, above, below)


AXES = ("row", "col", "mode")


def crossed(turn):
    sizes = [lax.axis_size(axis) for axis in AXES]
    perm = []
    for index in np.ndindex(*sizes):
        axis, bit = turn[index[2] % 2]
        partner = list(index)
        partner[AXES.index(axis)] ^= 1 << bit
        perm.append(tuple(int(np.ravel_multi_index(i, sizes)) for i in (index, partner)))
    sides = [(lax.axis_index(axis) >> bit) & 1 for axis, bit in turn]
    return perm, jnp.where(lax.axis_index("mode") == 0, sides[0], sides[1])


def swap(value, turn):
    return lax.ppermute(value, AXES, crossed(turn)[0])


def halves(value, side):
    count = value.shape[0] // 2
    keep = lax.dynamic_slice_in_dim(value, side * count, count, 0)
    send = lax.dynamic_slice_in_dim(value, (1 - side) * count, count, 0)
    return keep, send


def joined(mine, back, side):
    low = jnp.where(side == 0, mine, back)
    high = jnp.where(side == 0, back, mine)
    return jnp.concatenate([low, high], axis=0)


def summed(keep, send, turns):
    sides = [crossed(turn)[1] for turn in turns]
    send = yield send
    got = yield swap(send, turns[0])
    value = keep + got
    for turn, side in zip(turns[1:-1], sides[1:-1]):
        keep, send = halves(value, side)
        got = yield swap(send, turn)
        value = keep + got
    got = yield swap(value, turns[-1])
    value = value + got
    for turn, side in reversed(list(zip(turns[1:-1], sides[1:-1]))):
        back = yield swap(value, turn)
        value = joined(value, back, side)
    back = yield swap(value, turns[0])
    return (value, back)


def woven(jobs, order):
    waiting = [next(job) for job in jobs]
    results = [None] * len(jobs)
    token = None
    for j in order:
        got = waiting[j]
        if token is not None:
            got, _ = lax.optimization_barrier((got, token))
        try:
            waiting[j] = jobs[j].send(got)
            token = got
        except StopIteration as stop:
            results[j] = stop.value
            token = got
    return results


def order_of(lengths):
    order = [int(c) for c in ORDER]
    if [order.count(j) for j in range(len(lengths))] == lengths:
        return order
    steps = [(k + (j if j < len(lengths) - 1 else 1.5), j) for j, n in enumerate(lengths) for k in range(n)]
    return [j for _, j in sorted(steps)]


def shards(object_field, probe_modes, amplitudes, positions, counts):
    modes, _, size, _ = probe_modes.shape
    margin = size // 2
    tile = object_field.shape[-1]
    slots = positions.shape[2]
    rows, cols = lax.axis_size("row"), lax.axis_size("col")
    row, col, core = lax.axis_index("row"), lax.axis_index("col"), lax.axis_index("mode")
    tables = jnp.asarray(np.stack(dft_blocks(size)))
    offsets = positions[0, 0].reshape(-1)

    downward = [(i, i + 1) for i in range(rows - 1)]
    upward = [(i + 1, i) for i in range(rows - 1)]
    if cols == 2:
        shifts = [[(0, 1), (1, 0)]]
    else:
        shifts = [[(i, i + 1) for i in range(cols - 1)], [(i + 1, i) for i in range(cols - 1)]]
    top, bottom, *rest = edges(object_field, margin, len(shifts))
    from_above = lax.ppermute(bottom, "row", downward)
    from_below = lax.ppermute(top, "row", upward)
    sides, corners = [], []
    for g, shift in enumerate(shifts):
        sides.append(lax.ppermute(rest[g], "col", shift))
        at = jnp.where(col == 0, tile - margin, 0) if cols == 2 else (tile - margin, 0)[g]
        ends = [lax.dynamic_slice_in_dim(strip, at, margin, 1) for strip in (from_above, from_below)]
        corners.append(lax.ppermute(jnp.stack(ends), "col", shift))
    strips = [from_above, from_below, sides[0], sides[-1], corners[0], corners[-1]]
    mine = cut_patches(offsets, object_field, strips, size, slots)
    sibling = [("mode", 0)] * 2
    other = swap(mine, sibling)

    spectrum, power = forward(probe_modes, mine, other, staged(tables))
    power_other = swap(power, sibling)
    col_dims = [("col", b) for b in range(cols.bit_length() - 1)]
    row_dims = [("row", b) for b in range(rows.bit_length() - 1)]
    x, z = col_dims[0], row_dims[0]
    rest = [(dim, dim) for dim in col_dims[1:] + row_dims[1:]]
    turns = {"A": [(x, x), (z, z)] + rest, "C": [(z, z), (x, x)] + rest, "S": [(x, z), (z, x)] + rest}
    plans = [turns[kind] for kind, _ in CHUNKS]
    sides = [crossed(plan[0])[1] for plan in plans]
    *planes, object_keep, object_send = backward(
        jnp.stack([counts[0, 0]] + sides), [chunk for _, chunk in CHUNKS], probe_modes, mine, other,
        amplitudes[0, 0], power, power_other, spectrum, tables, 1.0 / math.sqrt(rows * cols),
    )

    def folded():
        if cols == 2:
            out_starts = [jnp.where(col == 0, tile + margin, 0)]
            in_starts = [jnp.where(col == 0, tile - margin, 0)]
        else:
            out_starts = [jnp.int32(tile + margin), jnp.int32(0)]
            in_starts = [jnp.int32(0), jnp.int32(tile - margin)]
        sent = yield object_send
        object_other = yield swap(sent, sibling)
        columns, outgoing = place(
            jnp.concatenate([offsets, jnp.stack(out_starts)]), object_keep, object_other, tile, len(shifts)
        )
        arrived = yield [lax.ppermute(outgoing[g], "col", shift) for g, shift in enumerate(shifts)]
        top, middle, bottom = merge(jnp.stack(in_starts), columns, arrived)
        above, below = yield (lax.ppermute(bottom, "row", downward), lax.ppermute(top, "row", upward))
        return finish(middle, above, below)

    jobs = [summed(*parts) for parts in zip(planes[0::2], planes[1::2], plans)] + [folded()]
    lengths = [2 * len(plan) for plan in plans] + [4]
    *sums, object_grad = woven(jobs, order_of(lengths))
    grads = {}
    for (own, back), side, (_, chunk) in zip(sums, sides, CHUNKS):
        low, high = jnp.where(side == 0, own, back), jnp.where(side == 0, back, own)
        for k, m in enumerate(chunk):
            grads[m] = jnp.stack([part[k * size : (k + 1) * size] for part in (low, high)])
    probe_grad = jnp.stack([grads[m] for m in range(modes)])
    return (object_grad, probe_grad)


def solution(mesh):
    return jax.shard_map(
        shards,
        mesh=mesh,
        in_specs=(
            P("scene", "row", "col"),
            P(("scene", "mode"), None, None, None),
            P(("scene", "row"), "col", None, None, None),
            P(("scene", "row"), "col", None, None),
            P(("scene", "row"), "col"),
        ),
        out_specs=(P(("scene", "mode"), "row", "col"), P(("scene", "mode"), None, None, None)),
        check_vma=False,
    )
```

time: 143 us -> 106 us (0.74)
  waiting for transfers between devices: 64.1 us -> 29.1 us
  local copies, waits for them, and re-layouts: 21.4 us -> 0.28 us
  starting transfers between devices: 38.6 us -> 51 us
  Pallas kernels: 14.2 us -> 19.6 us
  other arithmetic: 2.43 us -> 4.18 us
    ppermute x31 -> x30, waiting for transfers between devices: 64.1 us -> 29.1 us  [the longest x23 20.6 us: swap(): return lax.ppermute(value, AXES, crossed(turn)[0])]
    unnamed x38 -> x10, local copies, waits for them, and re-layouts: 14.5 us -> 0.02 us
    ppermute x31 -> x30, starting transfers between devices: 38.6 us -> 51 us  [the longest x23 36.7 us: swap(): return lax.ppermute(value, AXES, crossed(turn)[0])]
    pallas_call x3 -> x5, Pallas kernels: 11.8 us -> 17.2 us  [the longest x1 8.2 us: backward(): pl.pallas_call(functools.partial(backward_kernel, size, slots, chunks, sc...]
    slice x2 -> x0, local copies, waits for them, and re-layouts: 3.49 us -> none  [the longest x1 1.86 us: shards(): from_below = lax.ppermute(field[:margin], 'row', upward)]
    add x9 -> x12, other arithmetic: 0.27 us -> 2.18 us  [the longest x8 2.11 us: summed(): value = keep + got]
    dynamic_slice x1 -> x0, local copies, waits for them, and re-layouts: 1.85 us -> none  [shards(): edge = lax.dynamic_slice(field, (0, start), (tile, margin))]
  transfers between devices with their start and end apart: 31 -> 30, of which waited for: 20 -> 16; matrix products, arithmetic and copies ran while one was open for 5% -> 3% of each run, Pallas kernels for 1% -> 3%
where the time goes in v2:
time: 106 us
  starting transfers between devices  51 us (48%)
  waiting for transfers between devices  29.1 us (27%)
  Pallas kernels  19.6 us (18%)
  other arithmetic  4.18 us (4%)
  between operations  1.64 us (2%)
    ppermute x23, starting transfers between devices, swap(): return lax.ppermute(value, AXES, crossed(turn)[0])  36.7 us
    ppermute x23, waiting for transfers between devices, swap(): return lax.ppermute(value, AXES, crossed(turn)[0])  20.6 us
    pallas_call x1, Pallas kernels, backward(): pl.pallas_call(functools.partial(backward_kernel, size, slots, chunks, sc...  8.2 us
    ppermute x1, starting transfers between devices, shards(): from_above = lax.ppermute(bottom, 'row', downward)  5.57 us
    pallas_call x1, Pallas kernels, forward(): pl.pallas_call(functools.partial(forward_kernel, size, slots, modes), in_...  4.33 us
    ppermute x1, waiting for transfers between devices, shards(): from_below = lax.ppermute(top, 'row', upward)  2.36 us
    pallas_call x1, Pallas kernels, cut_patches(): pl.pallas_call(functools.partial(cut_kernel, size, margin, tile, slots),...  2.26 us
    ppermute x1, waiting for transfers between devices, shards(): corners.append(lax.ppermute(jnp.stack(ends), 'col', shift))  2.23 us
  transfers between devices with their start and end apart: 30, of which 16 were waited for; matrix products, arithmetic and copies ran while one was open for 3% of the time, Pallas kernels for 3%

profile of v2, /device:TPU:0, one launch (start us, length us, event | category | flops | bytes accessed | tf_op | source)
XLA Modules:
  0.0 105.8 jit_solution(159817718567954278)
XLA Ops:
  0.6 1.2 %edges.1 = (f32[128,512]{1,0:T(8,128)S(1)}, f32[128,512]{1,0:T(8,128)S(1)}, f32[512,128]{1,0:T(8,128)S(1)}) custom-call(f32[2,512,512]{2,1,0:T(8,128)} %field.3), custom_call_target="tpu_custom_call" | custom-call | tf_op jit(solution)/shard_map/edges/pallas_call | solution.py:91
  1.8 1.3 %collective-permute-start.1 = (f32[128,512]{1,0:T(8,128)S(1)}, f32[128,512]{1,0:T(8,128)S(1)}, u32[]{:S(2)}, u32[]{:S(2)}) collective-permute-start(f32[128,512]{1,0:T(8,128)S(1)} %get-tuple-element.51), channel_id=1, source_target_pairs={{4,0},{8,4},{12,8},{5,1},{9,5},{13,9},{6,2},{10,6},{14,10},{7,3},{... | collective-permute-start | bytes 786440 | tf_op jit(solution)/shard_map/ppermute | solution.py:500
  3.1 5.6 %collective-permute-start = (f32[128,512]{1,0:T(8,128)S(1)}, f32[128,512]{1,0:T(8,128)S(1)}, u32[]{:S(2)}, u32[]{:S(2)}) collective-permute-start(f32[128,512]{1,0:T(8,128)S(1)} %get-tuple-element.50), channel_id=1, source_target_pairs={{0,4},{4,8},{8,12},{1,5},{5,9},{9,13},{2,6},{6,10},{10,14},{3,7},{... | collective-permute-start | bytes 786440 | tf_op jit(solution)/shard_map/ppermute | solution.py:499
  8.7 2.0 %collective-permute-start.2 = (f32[512,128]{1,0:T(8,128)S(1)}, f32[512,128]{1,0:T(8,128)S(1)}, u32[]{:S(2)}, u32[]{:S(2)}) collective-permute-start(f32[512,128]{1,0:T(8,128)S(1)} %get-tuple-element.52), channel_id=1, source_target_pairs={{0,2},{2,0},{1,3},{3,1},{4,6},{6,4},{5,7},{7,5},{8,10},{10,8},{9,1... | collective-permute-start | bytes 786440 | tf_op jit(solution)/shard_map/ppermute | solution.py:503
  10.7 2.4 %collective-permute-done.1.down = f32[128,512]{1,0:T(8,128)S(1)} collective-permute-done((f32[128,512]{1,0:T(8,128)S(1)}, f32[128,512]{1,0:T(8,128)S(1)}, u32[]{:S(2)}, u32[]{:S(2)}) %collective-permute-start.1) | collective-permute-done | bytes 262176 | tf_op jit(solution)/shard_map/ppermute | solution.py:500
  13.0 1.2 %collective-permute-done.up = f32[128,512]{1,0:T(8,128)S(1)} collective-permute-done((f32[128,512]{1,0:T(8,128)S(1)}, f32[128,512]{1,0:T(8,128)S(1)}, u32[]{:S(2)}, u32[]{:S(2)}) %collective-permute-start) | collective-permute-done | bytes 262176 | tf_op jit(solution)/shard_map/ppermute | solution.py:499
  14.2 1.7 %collective-permute-start.3 = (f32[2,128,128]{2,1,0:T(8,128)S(1)}, f32[2,128,128]{2,1,0:T(8,128)S(1)}, u32[]{:S(2)}, u32[]{:S(2)}) collective-permute-start(f32[2,128,128]{2,1,0:T(8,128)S(1)} %pad_maximum_fusion.5), channel_id=1, source_target_pairs={{0,2},{2,0},{1,3},{3,1},{4,6},{6,4},{5,7},{7,5},{8,10},{10,8},{9,1... | collective-permute-start | bytes 393224 | tf_op jit(solution)/shard_map/ppermute | solution.py:506
  16.0 0.1 reshape_squeeze.3.offsets
  16.0 1.0 collective-permute-done.2.left.right
  17.1 2.2 %collective-permute-done.3.corners_left.corners_right = f32[2,128,128]{2,1,0:T(8,128)S(1)} collective-permute-done((f32[2,128,128]{2,1,0:T(8,128)S(1)}, f32[2,128,128]{2,1,0:T(8,128)S(1)}, u32[]{:S(2)}, u32[]{:S(2)}) %collective-permute-start.3) | collective-permute-done | bytes 131104 | tf_op jit(solution)/shard_map/ppermute | solution.py:506
  19.3 2.3 %cut.1.mine = f32[2,256,256]{2,1,0:T(8,128)S(1)} custom-call(s32[4]{0:T(128)S(1)} %reshape_squeeze.3.offsets, f32[2,512,512]{2,1,0:T(8,128)} %field.3, f32[128,512]{1,0:T(8,128)S(1)} %collective-permute-done.up, f32[128,512]{1,0:T(8,128)S(1)} %collective-permute-done.1.down, f32[512,128]{1,0:T(8,128)S(1)} %collective-permute-done.2.left.right, ...), custom_call_target="tpu_custom_call" | custom-call | tf_op jit(solution)/shard_map/cut/pallas_call | solution.py:148
  21.6 0.1 collective-permute-start.4
  21.7 1.2 %stage.1.tables = bf16[2,512,512]{2,1,0:T(8,128)(2,1)S(1)} custom-call(bf16[2,512,512]{2,1,0:T(8,128)(2,1)} %constant.27.clone.source.tables), custom_call_target="tpu_custom_call" | custom-call | tf_op jit(solution)/shard_map/stage/pallas_call | solution.py:180
  22.9 0.7 collective-permute-done.4.other
  23.6 4.3 %forward.1 = (f32[4,2,256,512]{3,2,1,0:T(8,128)}, f32[2,256,256]{2,1,0:T(8,128)}) custom-call(f32[2,256,256]{2,1,0:T(8,128)S(1)} %cut.1.mine, f32[2,256,256]{2,1,0:T(8,128)S(1)} %collective-permute-done.4.other, f32[4,2,256,256]{3,2,1,0:T(8,128)S(1)} %copy-done, bf16[2,512,512]{2,1,0:T(8,128)(2,1)S(1)} %stage.1.tables), custom_call_target="tpu_custom_call" | custom-call | tf_op jit(solution)/shard_map/forward/pallas_call | solution.py:220
  27.9 0.2 collective-permute-start.5
  28.8 0.1 stack.81.live
  28.9 1.4 %collective-permute-done.5.power_other = f32[2,256,256]{2,1,0:T(8,128)} collective-permute-done((f32[2,256,256]{2,1,0:T(8,128)}, f32[2,256,256]{2,1,0:T(8,128)}, u32[]{:S(2)}, u32[]{:S(2)}) %collective-permute-start.5) | collective-permute-done | bytes 524320 | tf_op jit(solution)/shard_map/ppermute | solution.py:423
  30.2 8.2 %backward.1 = (f32[256,256]{1,0:T(8,128)}, f32[256,256]{1,0:T(8,128)}, f32[256,256]{1,0:T(8,128)}, f32[256,256]{1,0:T(8,128)}, f32[256,256]{1,0:T(8,128)}, /*ind...) custom-call(s32[5]{0:T(128)S(1)} %stack.81.live, ...), custom_call_target="tpu_custom_call" | custom-call | tf_op jit(solution)/shard_map/backward/pallas_call | solution.py:300
  38.4 0.0 copy-start.1
  38.5 1.7 %collective-permute-start.7 = (f32[256,256]{1,0:T(8,128)}, f32[256,256]{1,0:T(8,128)S(1)}, u32[]{:S(2)}, u32[]{:S(2)}) collective-permute-start(f32[256,256]{1,0:T(8,128)} %get-tuple-element.61), channel_id=1, source_target_pairs={{0,2},{1,3},{2,0},{3,1},{4,6},{5,7},{6,4},{7,5},{8,10},{9,11},{10,... | collective-permute-start | bytes 786440 | tf_op jit(solution)/shard_map/ppermute | solution.py:423
  40.2 0.0 collective-permute-start.6
  40.2 2.4 %collective-permute-start.9 = (f32[256,256]{1,0:T(8,128)}, f32[256,256]{1,0:T(8,128)S(1)}, u32[]{:S(2)}, u32[]{:S(2)}) collective-permute-start(f32[256,256]{1,0:T(8,128)} %get-tuple-element.60), channel_id=1, source_target_pairs={{0,4},{1,5},{2,6},{3,7},{4,0},{5,1},{6,2},{7,3},{8,12},{9,13},{10,... | collective-permute-start | bytes 786440 | tf_op jit(solution)/shard_map/ppermute | solution.py:423
  42.6 4.5 %collective-permute-done.7 = f32[256,256]{1,0:T(8,128)S(1)} collective-permute-done((f32[256,256]{1,0:T(8,128)}, f32[256,256]{1,0:T(8,128)S(1)}, u32[]{:S(2)}, u32[]{:S(2)}) %collective-permute-start.7) | collective-permute-done | bytes 262176 | tf_op jit(solution)/shard_map/ppermute | solution.py:423
  47.1 1.0 add.54
  48.1 2.5 %collective-permute-start.8 = (f32[128,256]{1,0:T(8,128)S(1)}, f32[128,256]{1,0:T(8,128)S(1)}, u32[]{:S(2)}, u32[]{:S(2)}) collective-permute-start(f32[128,256]{1,0:T(8,128)S(1)} %constant_dynamic-slice_fusion.3), channel_id=1, source_target_pairs={{0,4},{1,5},{2,6},{3,7},{4,0},{5,1},{6,2},{7,3},{8,12},{9,13},{10,... | collective-permute-start | bytes 393224 | tf_op jit(solution)/shard_map/ppermute | solution.py:423
  50.6 1.6 %collective-permute-start.12 = (f32[256,256]{1,0:T(8,128)}, f32[256,256]{1,0:T(8,128)S(1)}, u32[]{:S(2)}, u32[]{:S(2)}) collective-permute-start(f32[256,256]{1,0:T(8,128)} %get-tuple-element.62), channel_id=1, source_target_pairs={{0,2},{1,3},{2,0},{3,1},{4,6},{5,7},{6,4},{7,5},{8,10},{9,11},{10,... | collective-permute-start | bytes 786440 | tf_op jit(solution)/shard_map/ppermute | solution.py:423
  52.3 0.1 pad_add_fusion.info
  52.3 0.4 collective-permute-start.14
  52.7 1.0 add.62
  53.7 0.0 collective-permute-done.8
  53.7 3.1 %collective-permute-start.11 = (f32[128,256]{1,0:T(8,128)S(1)}, f32[128,256]{1,0:T(8,128)S(1)}, u32[]{:S(2)}, u32[]{:S(2)}) collective-permute-start(f32[128,256]{1,0:T(8,128)S(1)} %dynamic-slice_add_fusion.3), channel_id=1, source_target_pairs={{0,8},{1,9},{2,10},{3,11},{4,12},{5,13},{6,14},{7,15},{8,0},{9,1},... | collective-permute-start | bytes 393224 | tf_op jit(solution)/shard_map/ppermute | solution.py:423
  56.8 0.0 collective-permute-done.6.other
  56.8 3.2 %collective-permute-done.12 = f32[256,256]{1,0:T(8,128)S(1)} collective-permute-done((f32[256,256]{1,0:T(8,128)}, f32[256,256]{1,0:T(8,128)S(1)}, u32[]{:S(2)}, u32[]{:S(2)}) %collective-permute-start.12) | collective-permute-done | bytes 262176 | tf_op jit(solution)/shard_map/ppermute | solution.py:423
  60.1 0.1 collective-permute-start.13
  60.3 1.7 %collective-permute-start.18 = (f32[128,256]{1,0:T(8,128)S(1)}, f32[128,256]{1,0:T(8,128)S(1)}, u32[]{:S(2)}, u32[]{:S(2)}) collective-permute-start(f32[128,256]{1,0:T(8,128)S(1)} %constant_dynamic-slice_fusion), channel_id=1, source_target_pairs={{0,2},{1,3},{2,0},{3,1},{4,6},{5,7},{6,4},{7,5},{8,10},{9,11},{10,... | collective-permute-start | bytes 393224 | tf_op jit(solution)/shard_map/ppermute | solution.py:423
  62.0 1.2 %place.1 = (f32[768,512]{1,0:T(8,128)S(1)}, f32[1,768,128]{2,1,0:T(8,128)S(1)}) custom-call(s32[5]{0:T(128)S(1)} %pad_add_fusion.info, f32[2,256,256]{2,1,0:T(8,128)S(1)} %copy-done.1, f32[2,256,256]{2,1,0:T(8,128)S(1)} %collective-permute-done.6.other), custom_call_target="tpu_custom_call" | custom-call | tf_op jit(solution)/shard_map/place/pallas_call | solution.py:342
  63.2 0.5 collective-permute-start.10
  63.7 2.0 %collective-permute-done.14 = f32[256,256]{1,0:T(8,128)S(1)} collective-permute-done((f32[256,256]{1,0:T(8,128)}, f32[256,256]{1,0:T(8,128)S(1)}, u32[]{:S(2)}, u32[]{:S(2)}) %collective-permute-start.14) | collective-permute-done | bytes 262176 | tf_op jit(solution)/shard_map/ppermute | solution.py:423
  65.7 0.1 collective-permute-start.17
  65.9 2.0 %collective-permute-start.15 = (f32[128,256]{1,0:T(8,128)S(1)}, f32[128,256]{1,0:T(8,128)S(1)}, u32[]{:S(2)}, u32[]{:S(2)}) collective-permute-start(f32[128,256]{1,0:T(8,128)S(1)} %add.59), channel_id=1, source_target_pairs={{0,4},{1,5},{2,6},{3,7},{4,0},{5,1},{6,2},{7,3},{8,12},{9,13},{10,... | collective-permute-start | bytes 393224 | tf_op jit(solution)/shard_map/ppermute | solution.py:423
  68.0 2.8 %collective-permute-start.16 = (f32[128,256]{1,0:T(8,128)S(1)}, f32[128,256]{1,0:T(8,128)S(1)}, u32[]{:S(2)}, u32[]{:S(2)}) collective-permute-start(f32[128,256]{1,0:T(8,128)S(1)} %dynamic-slice_add_fusion.2), channel_id=1, source_target_pairs={{0,8},{1,9},{2,10},{3,11},{4,12},{5,13},{6,14},{7,15},{8,0},{9,1},... | collective-permute-start | bytes 393224 | tf_op jit(solution)/shard_map/ppermute | solution.py:423
  70.8 0.0 collective-permute-done.17
  70.8 4.2 %collective-permute-start.23 = (f32[128,256]{1,0:T(8,128)S(1)}, f32[128,256]{1,0:T(8,128)S(1)}, u32[]{:S(2)}, u32[]{:S(2)}) collective-permute-start(f32[128,256]{1,0:T(8,128)S(1)} %dynamic-slice_add_fusion), channel_id=1, source_target_pairs={{0,8},{1,9},{2,10},{3,11},{4,12},{5,13},{6,14},{7,15},{8,0},{9,1},... | collective-permute-start | bytes 393224 | tf_op jit(solution)/shard_map/ppermute | solution.py:423
  75.0 1.2 %collective-permute-done.16 = f32[128,256]{1,0:T(8,128)S(1)} collective-permute-done((f32[128,256]{1,0:T(8,128)S(1)}, f32[128,256]{1,0:T(8,128)S(1)}, u32[]{:S(2)}, u32[]{:S(2)}) %collective-permute-start.16) | collective-permute-done | bytes 131104 | tf_op jit(solution)/shard_map/ppermute | solution.py:423
  76.2 4.5 %collective-permute-start.22 = (f32[128,256]{1,0:T(8,128)S(1)}, f32[128,256]{1,0:T(8,128)S(1)}, u32[]{:S(2)}, u32[]{:S(2)}) collective-permute-start(f32[128,256]{1,0:T(8,128)S(1)} %add.65), channel_id=1, source_target_pairs={{0,4},{1,5},{2,6},{3,7},{4,0},{5,1},{6,2},{7,3},{8,12},{9,13},{10,... | collective-permute-start | bytes 393224 | tf_op jit(solution)/shard_map/ppermute | solution.py:423
  80.8 1.3 %collective-permute-start.21 = (f32[128,256]{1,0:T(8,128)S(1)}, f32[128,256]{1,0:T(8,128)S(1)}, u32[]{:S(2)}, u32[]{:S(2)}) collective-permute-start(f32[128,256]{1,0:T(8,128)S(1)} %dynamic-slice_add_fusion.1), channel_id=1, source_target_pairs={{0,8},{1,9},{2,10},{3,11},{4,12},{5,13},{6,14},{7,15},{8,0},{9,1},... | collective-permute-start | bytes 393224 | tf_op jit(solution)/shard_map/ppermute | solution.py:423
  82.1 0.2 merge.1
  82.3 1.9 %collective-permute-start.19 = (f32[128,512]{1,0:T(8,128)S(1)}, f32[128,512]{1,0:T(8,128)S(1)}, u32[]{:S(2)}, u32[]{:S(2)}) collective-permute-start(f32[128,512]{1,0:T(8,128)S(1)} %get-tuple-element.85), channel_id=1, source_target_pairs={{0,4},{4,8},{8,12},{1,5},{5,9},{9,13},{2,6},{6,10},{10,14},{3,7},{... | collective-permute-start | bytes 786440 | tf_op jit(solution)/shard_map/ppermute | solution.py:540
  84.2 1.3 %collective-permute-start.20 = (f32[128,512]{1,0:T(8,128)S(1)}, f32[128,512]{1,0:T(8,128)S(1)}, u32[]{:S(2)}, u32[]{:S(2)}) collective-permute-start(f32[128,512]{1,0:T(8,128)S(1)} %get-tuple-element.86), channel_id=1, source_target_pairs={{4,0},{8,4},{12,8},{5,1},{9,5},{13,9},{6,2},{10,6},{14,10},{7,3},{... | collective-permute-start | bytes 786440 | tf_op jit(solution)/shard_map/ppermute | solution.py:540
  85.6 1.6 %collective-permute-start.24 = (f32[128,256]{1,0:T(8,128)S(1)}, f32[128,256]{1,0:T(8,128)S(1)}, u32[]{:S(2)}, u32[]{:S(2)}) collective-permute-start(f32[128,256]{1,0:T(8,128)S(1)} %add.68), channel_id=1, source_target_pairs={{0,2},{1,3},{2,0},{3,1},{4,6},{5,7},{6,4},{7,5},{8,10},{9,11},{10,... | collective-permute-start | bytes 393224 | tf_op jit(solution)/shard_map/ppermute | solution.py:423
  87.2 1.1 %collective-permute-done.21 = f32[128,256]{1,0:T(8,128)S(1)} collective-permute-done((f32[128,256]{1,0:T(8,128)S(1)}, f32[128,256]{1,0:T(8,128)S(1)}, u32[]{:S(2)}, u32[]{:S(2)}) %collective-permute-start.21) | collective-permute-done | bytes 131104 | tf_op jit(solution)/shard_map/ppermute | solution.py:423
  88.3 1.7 %collective-permute-start.27 = (f32[128,256]{1,0:T(8,128)S(1)}, f32[128,256]{1,0:T(8,128)S(1)}, u32[]{:S(2)}, u32[]{:S(2)}) collective-permute-start(f32[128,256]{1,0:T(8,128)S(1)} %add.69), channel_id=1, source_target_pairs={{0,4},{1,5},{2,6},{3,7},{4,0},{5,1},{6,2},{7,3},{8,12},{9,13},{10,... | collective-permute-start | bytes 393224 | tf_op jit(solution)/shard_map/ppermute | solution.py:423
  90.1 0.9 collective-permute-start.28
  91.0 1.3 %collective-permute-start.26 = (f32[256,256]{1,0:T(8,128)S(1)}, f32[256,256]{1,0:T(8,128)S(1)}, u32[]{:S(2)}, u32[]{:S(2)}) collective-permute-start(f32[256,256]{1,0:T(8,128)S(1)} %pad_maximum_fusion.2), channel_id=1, source_target_pairs={{0,2},{1,3},{2,0},{3,1},{4,6},{5,7},{6,4},{7,5},{8,10},{9,11},{10,... | collective-permute-start | bytes 786440 | tf_op jit(solution)/shard_map/ppermute | solution.py:423
  92.3 1.7 %collective-permute-done.20.below = f32[128,512]{1,0:T(8,128)S(1)} collective-permute-done((f32[128,512]{1,0:T(8,128)S(1)}, f32[128,512]{1,0:T(8,128)S(1)}, u32[]{:S(2)}, u32[]{:S(2)}) %collective-permute-start.20) | collective-permute-done | bytes 262176 | tf_op jit(solution)/shard_map/ppermute | solution.py:540
  94.0 1.1 %finish.1 = f32[1,512,512]{2,1,0:T(8,128)} custom-call(f32[512,512]{1,0:T(8,128)S(1)} %get-tuple-element.84.middle, f32[128,512]{1,0:T(8,128)S(1)} %collective-permute-done.19.above, f32[128,512]{1,0:T(8,128)S(1)} %collective-permute-done.20.below), custom_call_target="tpu_custom_call" | custom-call | tf_op jit(solution)/shard_map/finish/pallas_call | solution.py:399
  95.1 0.8 collective-permute-start.25
  95.9 1.9 %collective-permute-done.28 = f32[256,256]{1,0:T(8,128)S(1)} collective-permute-done((f32[256,256]{1,0:T(8,128)S(1)}, f32[256,256]{1,0:T(8,128)S(1)}, u32[]{:S(2)}, u32[]{:S(2)}) %collective-permute-start.28) | collective-permute-done | bytes 262176 | tf_op jit(solution)/shard_map/ppermute | solution.py:423
  97.8 1.5 %collective-permute-start.29 = (f32[256,256]{1,0:T(8,128)S(1)}, f32[256,256]{1,0:T(8,128)S(1)}, u32[]{:S(2)}, u32[]{:S(2)}) collective-permute-start(f32[256,256]{1,0:T(8,128)S(1)} %pad_maximum_fusion.4), channel_id=1, source_target_pairs={{0,2},{1,3},{2,0},{3,1},{4,6},{5,7},{6,4},{7,5},{8,10},{9,11},{10,... | collective-permute-start | bytes 786440 | tf_op jit(solution)/shard_map/ppermute | solution.py:423
  99.4 1.2 %collective-permute-done.26 = f32[256,256]{1,0:T(8,128)S(1)} collective-permute-done((f32[256,256]{1,0:T(8,128)S(1)}, f32[256,256]{1,0:T(8,128)S(1)}, u32[]{:S(2)}, u32[]{:S(2)}) %collective-permute-start.26) | collective-permute-done | bytes 262176 | tf_op jit(solution)/shard_map/ppermute | solution.py:423
  100.7 0.9 collective-permute-done.25
  101.6 2.6 %collective-permute-done.29 = f32[256,256]{1,0:T(8,128)S(1)} collective-permute-done((f32[256,256]{1,0:T(8,128)S(1)}, f32[256,256]{1,0:T(8,128)S(1)}, u32[]{:S(2)}, u32[]{:S(2)}) %collective-permute-start.29) | collective-permute-done | bytes 262176 | tf_op jit(solution)/shard_map/ppermute | solution.py:423
  104.3 1.5 %pad_maximum_fusion = f32[4,2,256,256]{3,2,1,0:T(8,128)} fusion(f32[1,2,256,256]{3,2,1,0:T(8,128)S(1)} %maximum_bitcast_fusion.3, f32[1,2,256,256]{3,2,1,0:T(8,128)S(1)} %maximum_bitcast_fusion.2, f32[1,2,256,256]{3,2,1,0:T(8,128)S(1)} %maximum_bitcast_fusion.1, f32[1,2,256,256]{3,2,1,0:T(8,128)S(1)} %maximum_bitcast_fusion), kind=kLoop, calls=%fused_computation | loop fusion | flops 1572864 | bytes 4194304 | tf_op jit(solution)/shard_map/stack | solution.py:551
  (52 shorter events, 0.8 us)
Async XLA Ops:
  0.6 15.3 %copy-start.4 = (s32[1,1,2,2]{3,2,1,0:T(2,128)S(1)}, s32[1,1,2,2]{3,2,1,0:T(2,128)}, u32[]{:S(2)}) copy-start(s32[1,1,2,2]{3,2,1,0:T(2,128)} %param.9) | copy-start | bytes 52
  1.8 11.2 %collective-permute-start.1 = (f32[128,512]{1,0:T(8,128)S(1)}, f32[128,512]{1,0:T(8,128)S(1)}, u32[]{:S(2)}, u32[]{:S(2)}) collective-permute-start(f32[128,512]{1,0:T(8,128)S(1)} %get-tuple-element.51), channel_id=1, source_target_pairs={{4,0},{8,4},{12,8},{5,1},{9,5},{13,9},{6,2},{10,6},{14,10},{7,3},{... | collective-permute-start | bytes 786440 | tf_op jit(solution)/shard_map/ppermute | solution.py:500
  3.1 11.1 %collective-permute-start = (f32[128,512]{1,0:T(8,128)S(1)}, f32[128,512]{1,0:T(8,128)S(1)}, u32[]{:S(2)}, u32[]{:S(2)}) collective-permute-start(f32[128,512]{1,0:T(8,128)S(1)} %get-tuple-element.50), channel_id=1, source_target_pairs={{0,4},{4,8},{8,12},{1,5},{5,9},{9,13},{2,6},{6,10},{10,14},{3,7},{... | collective-permute-start | bytes 786440 | tf_op jit(solution)/shard_map/ppermute | solution.py:499
  8.7 8.4 %collective-permute-start.2 = (f32[512,128]{1,0:T(8,128)S(1)}, f32[512,128]{1,0:T(8,128)S(1)}, u32[]{:S(2)}, u32[]{:S(2)}) collective-permute-start(f32[512,128]{1,0:T(8,128)S(1)} %get-tuple-element.52), channel_id=1, source_target_pairs={{0,2},{2,0},{1,3},{3,1},{4,6},{6,4},{5,7},{7,5},{8,10},{10,8},{9,1... | collective-permute-start | bytes 786440 | tf_op jit(solution)/shard_map/ppermute | solution.py:503
  14.2 5.1 %collective-permute-start.3 = (f32[2,128,128]{2,1,0:T(8,128)S(1)}, f32[2,128,128]{2,1,0:T(8,128)S(1)}, u32[]{:S(2)}, u32[]{:S(2)}) collective-permute-start(f32[2,128,128]{2,1,0:T(8,128)S(1)} %pad_maximum_fusion.5), channel_id=1, source_target_pairs={{0,2},{2,0},{1,3},{3,1},{4,6},{6,4},{5,7},{7,5},{8,10},{10,8},{9,1... | collective-permute-start | bytes 393224 | tf_op jit(solution)/shard_map/ppermute | solution.py:506
  16.0 7.5 %copy-start = (f32[4,2,256,256]{3,2,1,0:T(8,128)S(1)}, f32[4,2,256,256]{3,2,1,0:T(8,128)}, u32[]{:S(2)}) copy-start(f32[4,2,256,256]{3,2,1,0:T(8,128)} %probes.3) | copy-start | bytes 6291460
  21.6 2.0 %collective-permute-start.4 = (f32[2,256,256]{2,1,0:T(8,128)S(1)}, f32[2,256,256]{2,1,0:T(8,128)S(1)}, u32[]{:S(2)}, u32[]{:S(2)}) collective-permute-start(f32[2,256,256]{2,1,0:T(8,128)S(1)} %cut.1.mine), channel_id=1, source_target_pairs={{0,1},{1,0},{2,3},{3,2},{4,5},{5,4},{6,7},{7,6},{8,9},{9,8},{10,11... | collective-permute-start | bytes 1572872 | tf_op jit(solution)/shard_map/ppermute | solution.py:423
  27.9 2.3 %collective-permute-start.5 = (f32[2,256,256]{2,1,0:T(8,128)}, f32[2,256,256]{2,1,0:T(8,128)}, u32[]{:S(2)}, u32[]{:S(2)}) collective-permute-start(f32[2,256,256]{2,1,0:T(8,128)} %get-tuple-element.54.power), channel_id=1, source_target_pairs={{0,1},{1,0},{2,3},{3,2},{4,5},{5,4},{6,7},{7,6},{8,9},{9,8},{10,11... | collective-permute-start | bytes 1572872 | tf_op jit(solution)/shard_map/ppermute | solution.py:423
  38.4 21.6 %copy-start.3 = (f32[256,256]{1,0:T(8,128)S(1)}, f32[256,256]{1,0:T(8,128)}, u32[]{:S(2)}) copy-start(f32[256,256]{1,0:T(8,128)} %get-tuple-element.72) | copy-start | bytes 786436
  38.4 23.6 %copy-start.1 = (f32[2,256,256]{2,1,0:T(8,128)S(1)}, f32[2,256,256]{2,1,0:T(8,128)}, u32[]{:S(2)}) copy-start(f32[2,256,256]{2,1,0:T(8,128)} %get-tuple-element.55.mine) | copy-start | bytes 1572868
  38.5 8.6 %collective-permute-start.7 = (f32[256,256]{1,0:T(8,128)}, f32[256,256]{1,0:T(8,128)S(1)}, u32[]{:S(2)}, u32[]{:S(2)}) collective-permute-start(f32[256,256]{1,0:T(8,128)} %get-tuple-element.61), channel_id=1, source_target_pairs={{0,2},{1,3},{2,0},{3,1},{4,6},{5,7},{6,4},{7,5},{8,10},{9,11},{10,... | collective-permute-start | bytes 786440 | tf_op jit(solution)/shard_map/ppermute | solution.py:423
  40.2 16.7 %collective-permute-start.6 = (f32[2,256,256]{2,1,0:T(8,128)}, f32[2,256,256]{2,1,0:T(8,128)S(1)}, u32[]{:S(2)}, u32[]{:S(2)}) collective-permute-start(f32[2,256,256]{2,1,0:T(8,128)} %get-tuple-element.64), channel_id=1, source_target_pairs={{0,1},{1,0},{2,3},{3,2},{4,5},{5,4},{6,7},{7,6},{8,9},{9,8},{10,11... | collective-permute-start | bytes 1572872 | tf_op jit(solution)/shard_map/ppermute | solution.py:423
  40.2 12.5 %collective-permute-start.9 = (f32[256,256]{1,0:T(8,128)}, f32[256,256]{1,0:T(8,128)S(1)}, u32[]{:S(2)}, u32[]{:S(2)}) collective-permute-start(f32[256,256]{1,0:T(8,128)} %get-tuple-element.60), channel_id=1, source_target_pairs={{0,4},{1,5},{2,6},{3,7},{4,0},{5,1},{6,2},{7,3},{8,12},{9,13},{10,... | collective-permute-start | bytes 786440 | tf_op jit(solution)/shard_map/ppermute | solution.py:423
  48.1 17.6 %copy-start.2 = (f32[256,256]{1,0:T(8,128)S(1)}, f32[256,256]{1,0:T(8,128)}, u32[]{:S(2)}) copy-start(f32[256,256]{1,0:T(8,128)} %get-tuple-element.77) | copy-start | bytes 786436
  48.1 5.6 %collective-permute-start.8 = (f32[128,256]{1,0:T(8,128)S(1)}, f32[128,256]{1,0:T(8,128)S(1)}, u32[]{:S(2)}, u32[]{:S(2)}) collective-permute-start(f32[128,256]{1,0:T(8,128)S(1)} %constant_dynamic-slice_fusion.3), channel_id=1, source_target_pairs={{0,4},{1,5},{2,6},{3,7},{4,0},{5,1},{6,2},{7,3},{8,12},{9,13},{10,... | collective-permute-start | bytes 393224 | tf_op jit(solution)/shard_map/ppermute | solution.py:423
  50.6 9.5 %collective-permute-start.12 = (f32[256,256]{1,0:T(8,128)}, f32[256,256]{1,0:T(8,128)S(1)}, u32[]{:S(2)}, u32[]{:S(2)}) collective-permute-start(f32[256,256]{1,0:T(8,128)} %get-tuple-element.62), channel_id=1, source_target_pairs={{0,2},{1,3},{2,0},{3,1},{4,6},{5,7},{6,4},{7,5},{8,10},{9,11},{10,... | collective-permute-start | bytes 786440 | tf_op jit(solution)/shard_map/ppermute | solution.py:423
  52.3 13.4 %collective-permute-start.14 = (f32[256,256]{1,0:T(8,128)}, f32[256,256]{1,0:T(8,128)S(1)}, u32[]{:S(2)}, u32[]{:S(2)}) collective-permute-start(f32[256,256]{1,0:T(8,128)} %get-tuple-element.63), channel_id=1, source_target_pairs={{0,2},{1,3},{2,0},{3,1},{4,6},{5,7},{6,4},{7,5},{8,10},{9,11},{10,... | collective-permute-start | bytes 786440 | tf_op jit(solution)/shard_map/ppermute | solution.py:423
  53.7 12.2 %collective-permute-start.11 = (f32[128,256]{1,0:T(8,128)S(1)}, f32[128,256]{1,0:T(8,128)S(1)}, u32[]{:S(2)}, u32[]{:S(2)}) collective-permute-start(f32[128,256]{1,0:T(8,128)S(1)} %dynamic-slice_add_fusion.3), channel_id=1, source_target_pairs={{0,8},{1,9},{2,10},{3,11},{4,12},{5,13},{6,14},{7,15},{8,0},{9,1},... | collective-permute-start | bytes 393224 | tf_op jit(solution)/shard_map/ppermute | solution.py:423
  60.1 5.8 %collective-permute-start.13 = (f32[128,256]{1,0:T(8,128)S(1)}, f32[128,256]{1,0:T(8,128)S(1)}, u32[]{:S(2)}, u32[]{:S(2)}) collective-permute-start(f32[128,256]{1,0:T(8,128)S(1)} %constant_dynamic-slice_fusion.2), channel_id=1, source_target_pairs={{0,4},{1,5},{2,6},{3,7},{4,0},{5,1},{6,2},{7,3},{8,12},{9,13},{10,... | collective-permute-start | bytes 393224 | tf_op jit(solution)/shard_map/ppermute | solution.py:423
  60.3 10.5 %collective-permute-start.18 = (f32[128,256]{1,0:T(8,128)S(1)}, f32[128,256]{1,0:T(8,128)S(1)}, u32[]{:S(2)}, u32[]{:S(2)}) collective-permute-start(f32[128,256]{1,0:T(8,128)S(1)} %constant_dynamic-slice_fusion), channel_id=1, source_target_pairs={{0,2},{1,3},{2,0},{3,1},{4,6},{5,7},{6,4},{7,5},{8,10},{9,11},{10,... | collective-permute-start | bytes 393224 | tf_op jit(solution)/shard_map/ppermute | solution.py:423
  63.2 18.9 %collective-permute-start.10 = (f32[768,128]{1,0:T(8,128)S(1)}, f32[768,128]{1,0:T(8,128)S(1)}, u32[]{:S(2)}, u32[]{:S(2)}) collective-permute-start(f32[768,128]{1,0:T(8,128)S(1)} %bitcast.36), channel_id=1, source_target_pairs={{0,2},{2,0},{1,3},{3,1},{4,6},{6,4},{5,7},{7,5},{8,10},{10,8},{9,1... | collective-permute-start | bytes 1179656 | tf_op jit(solution)/shard_map/ppermute | solution.py:538
  65.7 5.1 %collective-permute-start.17 = (f32[128,256]{1,0:T(8,128)S(1)}, f32[128,256]{1,0:T(8,128)S(1)}, u32[]{:S(2)}, u32[]{:S(2)}) collective-permute-start(f32[128,256]{1,0:T(8,128)S(1)} %constant_dynamic-slice_fusion.1), channel_id=1, source_target_pairs={{0,4},{1,5},{2,6},{3,7},{4,0},{5,1},{6,2},{7,3},{8,12},{9,13},{10,... | collective-permute-start | bytes 393224 | tf_op jit(solution)/shard_map/ppermute | solution.py:423
  65.9 16.2 %collective-permute-start.15 = (f32[128,256]{1,0:T(8,128)S(1)}, f32[128,256]{1,0:T(8,128)S(1)}, u32[]{:S(2)}, u32[]{:S(2)}) collective-permute-start(f32[128,256]{1,0:T(8,128)S(1)} %add.59), channel_id=1, source_target_pairs={{0,4},{1,5},{2,6},{3,7},{4,0},{5,1},{6,2},{7,3},{8,12},{9,13},{10,... | collective-permute-start | bytes 393224 | tf_op jit(solution)/shard_map/ppermute | solution.py:423
  68.0 8.3 %collective-permute-start.16 = (f32[128,256]{1,0:T(8,128)S(1)}, f32[128,256]{1,0:T(8,128)S(1)}, u32[]{:S(2)}, u32[]{:S(2)}) collective-permute-start(f32[128,256]{1,0:T(8,128)S(1)} %dynamic-slice_add_fusion.2), channel_id=1, source_target_pairs={{0,8},{1,9},{2,10},{3,11},{4,12},{5,13},{6,14},{7,15},{8,0},{9,1},... | collective-permute-start | bytes 393224 | tf_op jit(solution)/shard_map/ppermute | solution.py:423
  70.8 14.7 %collective-permute-start.23 = (f32[128,256]{1,0:T(8,128)S(1)}, f32[128,256]{1,0:T(8,128)S(1)}, u32[]{:S(2)}, u32[]{:S(2)}) collective-permute-start(f32[128,256]{1,0:T(8,128)S(1)} %dynamic-slice_add_fusion), channel_id=1, source_target_pairs={{0,8},{1,9},{2,10},{3,11},{4,12},{5,13},{6,14},{7,15},{8,0},{9,1},... | collective-permute-start | bytes 393224 | tf_op jit(solution)/shard_map/ppermute | solution.py:423
  76.2 11.0 %collective-permute-start.22 = (f32[128,256]{1,0:T(8,128)S(1)}, f32[128,256]{1,0:T(8,128)S(1)}, u32[]{:S(2)}, u32[]{:S(2)}) collective-permute-start(f32[128,256]{1,0:T(8,128)S(1)} %add.65), channel_id=1, source_target_pairs={{0,4},{1,5},{2,6},{3,7},{4,0},{5,1},{6,2},{7,3},{8,12},{9,13},{10,... | collective-permute-start | bytes 393224 | tf_op jit(solution)/shard_map/ppermute | solution.py:423
  80.8 7.6 %collective-permute-start.21 = (f32[128,256]{1,0:T(8,128)S(1)}, f32[128,256]{1,0:T(8,128)S(1)}, u32[]{:S(2)}, u32[]{:S(2)}) collective-permute-start(f32[128,256]{1,0:T(8,128)S(1)} %dynamic-slice_add_fusion.1), channel_id=1, source_target_pairs={{0,8},{1,9},{2,10},{3,11},{4,12},{5,13},{6,14},{7,15},{8,0},{9,1},... | collective-permute-start | bytes 393224 | tf_op jit(solution)/shard_map/ppermute | solution.py:423
  82.3 8.7 %collective-permute-start.19 = (f32[128,512]{1,0:T(8,128)S(1)}, f32[128,512]{1,0:T(8,128)S(1)}, u32[]{:S(2)}, u32[]{:S(2)}) collective-permute-start(f32[128,512]{1,0:T(8,128)S(1)} %get-tuple-element.85), channel_id=1, source_target_pairs={{0,4},{4,8},{8,12},{1,5},{5,9},{9,13},{2,6},{6,10},{10,14},{3,7},{... | collective-permute-start | bytes 786440 | tf_op jit(solution)/shard_map/ppermute | solution.py:540
  84.2 9.7 %collective-permute-start.20 = (f32[128,512]{1,0:T(8,128)S(1)}, f32[128,512]{1,0:T(8,128)S(1)}, u32[]{:S(2)}, u32[]{:S(2)}) collective-permute-start(f32[128,512]{1,0:T(8,128)S(1)} %get-tuple-element.86), channel_id=1, source_target_pairs={{4,0},{8,4},{12,8},{5,1},{9,5},{13,9},{6,2},{10,6},{14,10},{7,3},{... | collective-permute-start | bytes 786440 | tf_op jit(solution)/shard_map/ppermute | solution.py:540
  85.6 8.4 %collective-permute-start.24 = (f32[128,256]{1,0:T(8,128)S(1)}, f32[128,256]{1,0:T(8,128)S(1)}, u32[]{:S(2)}, u32[]{:S(2)}) collective-permute-start(f32[128,256]{1,0:T(8,128)S(1)} %add.68), channel_id=1, source_target_pairs={{0,2},{1,3},{2,0},{3,1},{4,6},{5,7},{6,4},{7,5},{8,10},{9,11},{10,... | collective-permute-start | bytes 393224 | tf_op jit(solution)/shard_map/ppermute | solution.py:423
  88.3 9.4 %collective-permute-start.27 = (f32[128,256]{1,0:T(8,128)S(1)}, f32[128,256]{1,0:T(8,128)S(1)}, u32[]{:S(2)}, u32[]{:S(2)}) collective-permute-start(f32[128,256]{1,0:T(8,128)S(1)} %add.69), channel_id=1, source_target_pairs={{0,4},{1,5},{2,6},{3,7},{4,0},{5,1},{6,2},{7,3},{8,12},{9,13},{10,... | collective-permute-start | bytes 393224 | tf_op jit(solution)/shard_map/ppermute | solution.py:423
  90.1 7.6 %collective-permute-start.28 = (f32[256,256]{1,0:T(8,128)S(1)}, f32[256,256]{1,0:T(8,128)S(1)}, u32[]{:S(2)}, u32[]{:S(2)}) collective-permute-start(f32[256,256]{1,0:T(8,128)S(1)} %pad_maximum_fusion.3), channel_id=1, source_target_pairs={{0,2},{1,3},{2,0},{3,1},{4,6},{5,7},{6,4},{7,5},{8,10},{9,11},{10,... | collective-permute-start | bytes 786440 | tf_op jit(solution)/shard_map/ppermute | solution.py:423
  91.0 9.5 %collective-permute-start.26 = (f32[256,256]{1,0:T(8,128)S(1)}, f32[256,256]{1,0:T(8,128)S(1)}, u32[]{:S(2)}, u32[]{:S(2)}) collective-permute-start(f32[256,256]{1,0:T(8,128)S(1)} %pad_maximum_fusion.2), channel_id=1, source_target_pairs={{0,2},{1,3},{2,0},{3,1},{4,6},{5,7},{6,4},{7,5},{8,10},{9,11},{10,... | collective-permute-start | bytes 786440 | tf_op jit(solution)/shard_map/ppermute | solution.py:423
  95.1 6.4 %collective-permute-start.25 = (f32[256,256]{1,0:T(8,128)S(1)}, f32[256,256]{1,0:T(8,128)S(1)}, u32[]{:S(2)}, u32[]{:S(2)}) collective-permute-start(f32[256,256]{1,0:T(8,128)S(1)} %pad_maximum_fusion.1), channel_id=1, source_target_pairs={{0,4},{1,5},{2,6},{3,7},{4,0},{5,1},{6,2},{7,3},{8,12},{9,13},{10,... | collective-permute-start | bytes 786440 | tf_op jit(solution)/shard_map/ppermute | solution.py:423
  97.8 6.4 %collective-permute-start.29 = (f32[256,256]{1,0:T(8,128)S(1)}, f32[256,256]{1,0:T(8,128)S(1)}, u32[]{:S(2)}, u32[]{:S(2)}) collective-permute-start(f32[256,256]{1,0:T(8,128)S(1)} %pad_maximum_fusion.4), channel_id=1, source_target_pairs={{0,2},{1,3},{2,0},{3,1},{4,6},{5,7},{6,4},{7,5},{8,10},{9,11},{10,... | collective-permute-start | bytes 786440 | tf_op jit(solution)/shard_map/ppermute | solution.py:423

commit v3 on v2

--- a/solution.py
+++ b/solution.py
@@ -14,8 +14,7 @@
 SUBLANES = 8
 MIB = 1024 * 1024
 
-CHUNKS = (("C", (0,)), ("A", (1,)), ("A", (2,)), ("A", (3,)))
-ORDER = "0123410142321032140234023103"
+CHUNKS = (("C", (0,)), ("A", (1,)), ("S", (2, 3)))
 
 f32 = jnp.float32
 bf16 = jnp.bfloat16
@@ -438,45 +437,14 @@
 
 def summed(keep, send, turns):
     sides = [crossed(turn)[1] for turn in turns]
-    send = yield send
-    got = yield swap(send, turns[0])
-    value = keep + got
+    value = keep + swap(send, turns[0])
     for turn, side in zip(turns[1:-1], sides[1:-1]):
         keep, send = halves(value, side)
-        got = yield swap(send, turn)
-        value = keep + got
-    got = yield swap(value, turns[-1])
-    value = value + got
+        value = keep + swap(send, turn)
+    value = value + swap(value, turns[-1])
     for turn, side in reversed(list(zip(turns[1:-1], sides[1:-1]))):
-        back = yield swap(value, turn)
-        value = joined(value, back, side)
-    back = yield swap(value, turns[0])
-    return (value, back)
-
-
-def woven(jobs, order):
-    waiting = [next(job) for job in jobs]
-    results = [None] * len(jobs)
-    token = None
-    for j in order:
-        got = waiting[j]
-        if token is not None:
-            got, _ = lax.optimization_barrier((got, token))
-        try:
-            waiting[j] = jobs[j].send(got)
-            token = got
-        except StopIteration as stop:
-            results[j] = stop.value
-            token = got
-    return results
-
-
-def order_of(lengths):
-    order = [int(c) for c in ORDER]
-    if [order.count(j) for j in range(len(lengths))] == lengths:
-        return order
-    steps = [(k + (j if j < len(lengths) - 1 else 1.5), j) for j, n in enumerate(lengths) for k in range(n)]
-    return [j for _, j in sorted(steps)]
+        value = joined(value, swap(value, turn), side)
+    return value, swap(value, turns[0])
 
 
 def shards(object_field, probe_modes, amplitudes, positions, counts):
@@ -523,26 +491,23 @@
         amplitudes[0, 0], power, power_other, spectrum, tables, 1.0 / math.sqrt(rows * cols),
     )
 
-    def folded():
-        if cols == 2:
-            out_starts = [jnp.where(col == 0, tile + margin, 0)]
-            in_starts = [jnp.where(col == 0, tile - margin, 0)]
-        else:
-            out_starts = [jnp.int32(tile + margin), jnp.int32(0)]
-            in_starts = [jnp.int32(0), jnp.int32(tile - margin)]
-        sent = yield object_send
-        object_other = yield swap(sent, sibling)
-        columns, outgoing = place(
-            jnp.concatenate([offsets, jnp.stack(out_starts)]), object_keep, object_other, tile, len(shifts)
-        )
-        arrived = yield [lax.ppermute(outgoing[g], "col", shift) for g, shift in enumerate(shifts)]
-        top, middle, bottom = merge(jnp.stack(in_starts), columns, arrived)
-        above, below = yield (lax.ppermute(bottom, "row", downward), lax.ppermute(top, "row", upward))
-        return finish(middle, above, below)
-
-    jobs = [summed(*parts) for parts in zip(planes[0::2], planes[1::2], plans)] + [folded()]
-    lengths = [2 * len(plan) for plan in plans] + [4]
-    *sums, object_grad = woven(jobs, order_of(lengths))
+    sums = [summed(*parts) for parts in zip(planes[0::2], planes[1::2], plans)]
+
+    if cols == 2:
+        out_starts = [jnp.where(col == 0, tile + margin, 0)]
+        in_starts = [jnp.where(col == 0, tile - margin, 0)]
+    else:
+        out_starts = [jnp.int32(tile + margin), jnp.int32(0)]
+        in_starts = [jnp.int32(0), jnp.int32(tile - margin)]
+    columns, outgoing = place(
+        jnp.concatenate([offsets, jnp.stack(out_starts)]), object_keep, swap(object_send, sibling), tile, len(shifts)
+    )
+    arrived = [lax.ppermute(outgoing[g], "col", shift) for g, shift in enumerate(shifts)]
+    top, middle, bottom = merge(jnp.stack(in_starts), columns, arrived)
+    above = lax.ppermute(bottom, "row", downward)
+    below = lax.ppermute(top, "row", upward)
+    object_grad = finish(middle, above, below)
+
     grads = {}
     for (own, back), side, (_, chunk) in zip(sums, sides, CHUNKS):
         low, high = jnp.where(side == 0, own, back), jnp.where(side == 0, back, own)

time: 106 us -> 104 us (0.981)
  starting transfers between devices: 51 us -> 37.1 us
  waiting for transfers between devices: 29.1 us -> 40 us
    ppermute x23 -> x18, starting transfers between devices: 36.7 us -> 19.8 us  [swap(): return lax.ppermute(value, AXES, crossed(turn)[0])]
    ppermute x23 -> x18, waiting for transfers between devices: 20.6 us -> 27.2 us  [swap(): return lax.ppermute(value, AXES, crossed(turn)[0])]
    ppermute x3, waiting for transfers between devices: 1.68 us -> 5.97 us  [the longest x1 4.07 us: shards(): below = lax.ppermute(top, 'row', upward)]
    ppermute x3, starting transfers between devices: 3.7 us -> 6.68 us  [the longest x1 3.92 us: shards(): above = lax.ppermute(bottom, 'row', downward)]
    add x12 -> x9, other arithmetic: 2.18 us -> 3.08 us  [the longest x3 2.04 us: summed(): value = keep + swap(send, turns[0])]
  transfers between devices with their start and end apart: 30 -> 25, of which waited for: 16 -> 17; matrix products, arithmetic and copies ran while one was open for 3% -> 4% of each run, Pallas kernels for 3% -> 4%
where the time goes in v3:
time: 104 us
  waiting for transfers between devices  40 us (38%)
  starting transfers between devices  37.1 us (36%)
  Pallas kernels  19.8 us (19%)
  other arithmetic  5.17 us (5%)
  between operations  1.61 us (2%)
    ppermute x18, waiting for transfers between devices, swap(): return lax.ppermute(value, AXES, crossed(turn)[0])  27.2 us
    ppermute x18, starting transfers between devices, swap(): return lax.ppermute(value, AXES, crossed(turn)[0])  19.8 us
    pallas_call x1, Pallas kernels, backward(): pl.pallas_call(functools.partial(backward_kernel, size, slots, chunks, sc...  8.27 us
    ppermute x1, starting transfers between devices, shards(): from_above = lax.ppermute(bottom, 'row', downward)  5.57 us
    pallas_call x1, Pallas kernels, forward(): pl.pallas_call(functools.partial(forward_kernel, size, slots, modes), in_...  4.45 us
    ppermute x1, waiting for transfers between devices, shards(): below = lax.ppermute(top, 'row', upward)  4.07 us
    ppermute x1, starting transfers between devices, shards(): above = lax.ppermute(bottom, 'row', downward)  3.92 us
    ppermute x1, waiting for transfers between devices, shards(): from_below = lax.ppermute(top, 'row', upward)  2.36 us
  transfers between devices with their start and end apart: 25, of which 17 were waited for; matrix products, arithmetic and copies ran while one was open for 4% of the time, Pallas kernels for 4%

profile of v3, /device:TPU:0, one launch (start us, length us, event | category | flops | bytes accessed | tf_op | source)
XLA Modules:
  0.0 103.9 jit_solution(7818683378791247654)
XLA Ops:
  0.6 1.2 %edges.1 = (f32[128,512]{1,0:T(8,128)S(1)}, f32[128,512]{1,0:T(8,128)S(1)}, f32[512,128]{1,0:T(8,128)S(1)}) custom-call(f32[2,512,512]{2,1,0:T(8,128)} %field.3), custom_call_target="tpu_custom_call" | custom-call | tf_op jit(solution)/shard_map/edges/pallas_call | solution.py:90
  1.8 1.3 %collective-permute-start.1 = (f32[128,512]{1,0:T(8,128)S(1)}, f32[128,512]{1,0:T(8,128)S(1)}, u32[]{:S(2)}, u32[]{:S(2)}) collective-permute-start(f32[128,512]{1,0:T(8,128)S(1)} %get-tuple-element.21), channel_id=1, source_target_pairs={{4,0},{8,4},{12,8},{5,1},{9,5},{13,9},{6,2},{10,6},{14,10},{7,3},{... | collective-permute-start | bytes 786440 | tf_op jit(solution)/shard_map/ppermute | solution.py:468
  3.1 5.6 %collective-permute-start = (f32[128,512]{1,0:T(8,128)S(1)}, f32[128,512]{1,0:T(8,128)S(1)}, u32[]{:S(2)}, u32[]{:S(2)}) collective-permute-start(f32[128,512]{1,0:T(8,128)S(1)} %get-tuple-element.20), channel_id=1, source_target_pairs={{0,4},{4,8},{8,12},{1,5},{5,9},{9,13},{2,6},{6,10},{10,14},{3,7},{... | collective-permute-start | bytes 786440 | tf_op jit(solution)/shard_map/ppermute | solution.py:467
  8.7 2.0 %collective-permute-start.2 = (f32[512,128]{1,0:T(8,128)S(1)}, f32[512,128]{1,0:T(8,128)S(1)}, u32[]{:S(2)}, u32[]{:S(2)}) collective-permute-start(f32[512,128]{1,0:T(8,128)S(1)} %get-tuple-element.22), channel_id=1, source_target_pairs={{0,2},{2,0},{1,3},{3,1},{4,6},{6,4},{5,7},{7,5},{8,10},{10,8},{9,1... | collective-permute-start | bytes 786440 | tf_op jit(solution)/shard_map/ppermute | solution.py:471
  10.7 2.4 %collective-permute-done.1.down = f32[128,512]{1,0:T(8,128)S(1)} collective-permute-done((f32[128,512]{1,0:T(8,128)S(1)}, f32[128,512]{1,0:T(8,128)S(1)}, u32[]{:S(2)}, u32[]{:S(2)}) %collective-permute-start.1) | collective-permute-done | bytes 262176 | tf_op jit(solution)/shard_map/ppermute | solution.py:468
  13.0 1.2 %collective-permute-done.up = f32[128,512]{1,0:T(8,128)S(1)} collective-permute-done((f32[128,512]{1,0:T(8,128)S(1)}, f32[128,512]{1,0:T(8,128)S(1)}, u32[]{:S(2)}, u32[]{:S(2)}) %collective-permute-start) | collective-permute-done | bytes 262176 | tf_op jit(solution)/shard_map/ppermute | solution.py:467
  14.2 1.7 %collective-permute-start.3 = (f32[2,128,128]{2,1,0:T(8,128)S(1)}, f32[2,128,128]{2,1,0:T(8,128)S(1)}, u32[]{:S(2)}, u32[]{:S(2)}) collective-permute-start(f32[2,128,128]{2,1,0:T(8,128)S(1)} %pad_maximum_fusion.4), channel_id=1, source_target_pairs={{0,2},{2,0},{1,3},{3,1},{4,6},{6,4},{5,7},{7,5},{8,10},{10,8},{9,1... | collective-permute-start | bytes 393224 | tf_op jit(solution)/shard_map/ppermute | solution.py:474
  16.0 0.1 reshape_squeeze.3.offsets
  16.0 1.0 %collective-permute-done.2.left.right = f32[512,128]{1,0:T(8,128)S(1)} collective-permute-done((f32[512,128]{1,0:T(8,128)S(1)}, f32[512,128]{1,0:T(8,128)S(1)}, u32[]{:S(2)}, u32[]{:S(2)}) %collective-permute-start.2) | collective-permute-done | bytes 262176 | tf_op jit(solution)/shard_map/ppermute | solution.py:471
  17.1 2.2 %collective-permute-done.3.corners_left.corners_right = f32[2,128,128]{2,1,0:T(8,128)S(1)} collective-permute-done((f32[2,128,128]{2,1,0:T(8,128)S(1)}, f32[2,128,128]{2,1,0:T(8,128)S(1)}, u32[]{:S(2)}, u32[]{:S(2)}) %collective-permute-start.3) | collective-permute-done | bytes 131104 | tf_op jit(solution)/shard_map/ppermute | solution.py:474
  19.3 2.3 %cut.1.mine = f32[2,256,256]{2,1,0:T(8,128)S(1)} custom-call(s32[4]{0:T(128)S(1)} %reshape_squeeze.3.offsets, f32[2,512,512]{2,1,0:T(8,128)} %field.3, f32[128,512]{1,0:T(8,128)S(1)} %collective-permute-done.up, f32[128,512]{1,0:T(8,128)S(1)} %collective-permute-done.1.down, f32[512,128]{1,0:T(8,128)S(1)} %collective-permute-done.2.left.right, ...), custom_call_target="tpu_custom_call" | custom-call | tf_op jit(solution)/shard_map/cut/pallas_call | solution.py:147
  21.6 0.1 collective-permute-start.4
  21.7 1.2 %stage.1.tables = bf16[2,512,512]{2,1,0:T(8,128)(2,1)S(1)} custom-call(bf16[2,512,512]{2,1,0:T(8,128)(2,1)} %constant.28.clone.source.tables), custom_call_target="tpu_custom_call" | custom-call | tf_op jit(solution)/shard_map/stage/pallas_call | solution.py:179
  22.9 0.7 collective-permute-done.4.other
  23.6 4.5 %forward.1 = (f32[4,2,256,512]{3,2,1,0:T(8,128)}, f32[2,256,256]{2,1,0:T(8,128)}) custom-call(f32[2,256,256]{2,1,0:T(8,128)S(1)} %cut.1.mine, f32[2,256,256]{2,1,0:T(8,128)S(1)} %collective-permute-done.4.other, f32[4,2,256,256]{3,2,1,0:T(8,128)S(1)} %copy-done, bf16[2,512,512]{2,1,0:T(8,128)(2,1)S(1)} %stage.1.tables), custom_call_target="tpu_custom_call" | custom-call | tf_op jit(solution)/shard_map/forward/pallas_call | solution.py:219
  28.0 0.2 collective-permute-start.5
  28.9 0.1 pad_add_fusion.1.live
  29.0 1.4 %collective-permute-done.5.power_other = f32[2,256,256]{2,1,0:T(8,128)} collective-permute-done((f32[2,256,256]{2,1,0:T(8,128)}, f32[2,256,256]{2,1,0:T(8,128)}, u32[]{:S(2)}, u32[]{:S(2)}) %collective-permute-start.5) | collective-permute-done | bytes 524320 | tf_op jit(solution)/shard_map/ppermute | solution.py:422
  30.3 8.3 %backward.1 = (f32[256,256]{1,0:T(8,128)}, f32[256,256]{1,0:T(8,128)}, f32[256,256]{1,0:T(8,128)}, f32[256,256]{1,0:T(8,128)}, f32[512,256]{1,0:T(8,128)}, /*ind...) custom-call(s32[4]{0:T(128)S(1)} %pad_add_fusion.1.live, ...), custom_call_target="tpu_custom_call" | custom-call | tf_op jit(solution)/shard_map/backward/pallas_call | solution.py:299
  38.6 0.0 copy-start.2
  38.6 2.5 %collective-permute-start.10 = (f32[256,256]{1,0:T(8,128)}, f32[256,256]{1,0:T(8,128)S(1)}, u32[]{:S(2)}, u32[]{:S(2)}) collective-permute-start(f32[256,256]{1,0:T(8,128)} %get-tuple-element.33), channel_id=1, source_target_pairs={{0,4},{1,5},{2,6},{3,7},{4,0},{5,1},{6,2},{7,3},{8,12},{9,13},{10,... | collective-permute-start | bytes 786440 | tf_op jit(solution)/shard_map/ppermute | solution.py:422
  41.1 1.6 %collective-permute-start.15 = (f32[256,256]{1,0:T(8,128)}, f32[256,256]{1,0:T(8,128)S(1)}, u32[]{:S(2)}, u32[]{:S(2)}) collective-permute-start(f32[256,256]{1,0:T(8,128)} %get-tuple-element.35), channel_id=1, source_target_pairs={{0,2},{1,3},{2,0},{3,1},{4,6},{5,7},{6,4},{7,5},{8,10},{9,11},{10,... | collective-permute-start | bytes 786440 | tf_op jit(solution)/shard_map/ppermute | solution.py:422
  42.8 0.4 collective-permute-start.20
  43.2 5.3 %collective-permute-done.10 = f32[256,256]{1,0:T(8,128)S(1)} collective-permute-done((f32[256,256]{1,0:T(8,128)}, f32[256,256]{1,0:T(8,128)S(1)}, u32[]{:S(2)}, u32[]{:S(2)}) %collective-permute-start.10) | collective-permute-done | bytes 262176 | tf_op jit(solution)/shard_map/ppermute | solution.py:422
  48.4 1.0 add.47
  49.5 1.7 %collective-permute-start.11 = (f32[128,256]{1,0:T(8,128)S(1)}, f32[128,256]{1,0:T(8,128)S(1)}, u32[]{:S(2)}, u32[]{:S(2)}) collective-permute-start(f32[128,256]{1,0:T(8,128)S(1)} %constant_dynamic-slice_fusion.2), channel_id=1, source_target_pairs={{0,2},{1,3},{2,0},{3,1},{4,6},{5,7},{6,4},{7,5},{8,10},{9,11},{10,... | collective-permute-start | bytes 393224 | tf_op jit(solution)/shard_map/ppermute | solution.py:422
  51.2 0.0 collective-permute-start.6
  51.2 0.0 collective-permute-done.15
  51.2 1.0 add.52
  52.2 2.1 %collective-permute-start.16 = (f32[128,256]{1,0:T(8,128)S(1)}, f32[128,256]{1,0:T(8,128)S(1)}, u32[]{:S(2)}, u32[]{:S(2)}) collective-permute-start(f32[128,256]{1,0:T(8,128)S(1)} %constant_dynamic-slice_fusion.1), channel_id=1, source_target_pairs={{0,4},{1,5},{2,6},{3,7},{4,0},{5,1},{6,2},{7,3},{8,12},{9,13},{10,... | collective-permute-start | bytes 393224 | tf_op jit(solution)/shard_map/ppermute | solution.py:422
  54.3 3.5 %collective-permute-done.11 = f32[128,256]{1,0:T(8,128)S(1)} collective-permute-done((f32[128,256]{1,0:T(8,128)S(1)}, f32[128,256]{1,0:T(8,128)S(1)}, u32[]{:S(2)}, u32[]{:S(2)}) %collective-permute-start.11) | collective-permute-done | bytes 131104 | tf_op jit(solution)/shard_map/ppermute | solution.py:422
  57.9 3.3 %collective-permute-start.12 = (f32[128,256]{1,0:T(8,128)S(1)}, f32[128,256]{1,0:T(8,128)}, u32[]{:S(2)}, u32[]{:S(2)}) collective-permute-start(f32[128,256]{1,0:T(8,128)S(1)} %dynamic-slice_add_fusion.2), channel_id=1, source_target_pairs={{0,8},{1,9},{2,10},{3,11},{4,12},{5,13},{6,14},{7,15},{8,0},{9,1},... | collective-permute-start | bytes 393224 | tf_op jit(solution)/shard_map/ppermute | solution.py:422
  61.2 0.0 collective-permute-done.20
  61.2 0.1 add.57
  61.3 0.1 collective-permute-start.21
  61.4 0.3 collective-permute-start.17
  61.7 0.1 pad_add_fusion.info
  61.8 1.2 %place.1 = (f32[768,512]{1,0:T(8,128)S(1)}, f32[1,768,128]{2,1,0:T(8,128)S(1)}) custom-call(s32[5]{0:T(128)S(1)} %pad_add_fusion.info, f32[2,256,256]{2,1,0:T(8,128)S(1)} %copy-done.1, f32[2,256,256]{2,1,0:T(8,128)S(1)} %collective-permute-done.6.other), custom_call_target="tpu_custom_call" | custom-call | tf_op jit(solution)/shard_map/place/pallas_call | solution.py:341
  63.0 1.5 %collective-permute-start.7 = (f32[768,128]{1,0:T(8,128)S(1)}, f32[768,128]{1,0:T(8,128)S(1)}, u32[]{:S(2)}, u32[]{:S(2)}) collective-permute-start(f32[768,128]{1,0:T(8,128)S(1)} %bitcast.37), channel_id=1, source_target_pairs={{0,2},{2,0},{1,3},{3,1},{4,6},{6,4},{5,7},{7,5},{8,10},{10,8},{9,1... | collective-permute-start | bytes 1179656 | tf_op jit(solution)/shard_map/ppermute | solution.py:505
  64.5 3.5 %collective-permute-done.12 = f32[128,256]{1,0:T(8,128)} collective-permute-done((f32[128,256]{1,0:T(8,128)S(1)}, f32[128,256]{1,0:T(8,128)}, u32[]{:S(2)}, u32[]{:S(2)}) %collective-permute-start.12) | collective-permute-done | bytes 131104 | tf_op jit(solution)/shard_map/ppermute | solution.py:422
  67.9 0.9 add.51
  68.9 0.6 collective-permute-start.13
  69.4 1.3 %collective-permute-done.17 = f32[128,256]{1,0:T(8,128)S(1)} collective-permute-done((f32[128,256]{1,0:T(8,128)S(1)}, f32[128,256]{1,0:T(8,128)S(1)}, u32[]{:S(2)}, u32[]{:S(2)}) %collective-permute-start.17) | collective-permute-done | bytes 131104 | tf_op jit(solution)/shard_map/ppermute | solution.py:422
  70.8 0.1 collective-permute-start.18
  70.9 1.6 %collective-permute-done.21 = f32[256,256]{1,0:T(8,128)S(1)} collective-permute-done((f32[256,256]{1,0:T(8,128)S(1)}, f32[256,256]{1,0:T(8,128)S(1)}, u32[]{:S(2)}, u32[]{:S(2)}) %collective-permute-start.21) | collective-permute-done | bytes 262176 | tf_op jit(solution)/shard_map/ppermute | solution.py:422
  72.5 1.7 %collective-permute-start.22 = (f32[256,256]{1,0:T(8,128)S(1)}, f32[256,256]{1,0:T(8,128)S(1)}, u32[]{:S(2)}, u32[]{:S(2)}) collective-permute-start(f32[256,256]{1,0:T(8,128)S(1)} %dynamic-slice_add_fusion), channel_id=1, source_target_pairs={{0,8},{1,9},{2,10},{3,11},{4,12},{5,13},{6,14},{7,15},{8,0},{9,1},... | collective-permute-start | bytes 786440 | tf_op jit(solution)/shard_map/ppermute | solution.py:422
  74.2 1.8 %collective-permute-done.13 = f32[128,256]{1,0:T(8,128)S(1)} collective-permute-done((f32[128,256]{1,0:T(8,128)S(1)}, f32[128,256]{1,0:T(8,128)S(1)}, u32[]{:S(2)}, u32[]{:S(2)}) %collective-permute-start.13) | collective-permute-done | bytes 131104 | tf_op jit(solution)/shard_map/ppermute | solution.py:422
  76.0 2.3 %collective-permute-start.14 = (f32[256,256]{1,0:T(8,128)S(1)}, f32[256,256]{1,0:T(8,128)S(1)}, u32[]{:S(2)}, u32[]{:S(2)}) collective-permute-start(f32[256,256]{1,0:T(8,128)S(1)} %pad_maximum_fusion.2), channel_id=1, source_target_pairs={{0,4},{1,5},{2,6},{3,7},{4,0},{5,1},{6,2},{7,3},{8,12},{9,13},{10,... | collective-permute-start | bytes 786440 | tf_op jit(solution)/shard_map/ppermute | solution.py:422
  78.3 5.6 %collective-permute-done.22 = f32[256,256]{1,0:T(8,128)S(1)} collective-permute-done((f32[256,256]{1,0:T(8,128)S(1)}, f32[256,256]{1,0:T(8,128)S(1)}, u32[]{:S(2)}, u32[]{:S(2)}) %collective-permute-start.22) | collective-permute-done | bytes 262176 | tf_op jit(solution)/shard_map/ppermute | solution.py:422
  84.0 0.2 collective-permute-start.23
  84.3 1.1 %collective-permute-start.19 = (f32[256,256]{1,0:T(8,128)S(1)}, f32[256,256]{1,0:T(8,128)S(1)}, u32[]{:S(2)}, u32[]{:S(2)}) collective-permute-start(f32[256,256]{1,0:T(8,128)S(1)} %pad_maximum_fusion.3), channel_id=1, source_target_pairs={{0,2},{1,3},{2,0},{3,1},{4,6},{5,7},{6,4},{7,5},{8,10},{9,11},{10,... | collective-permute-start | bytes 786440 | tf_op jit(solution)/shard_map/ppermute | solution.py:422
  85.4 0.2 merge.1
  85.6 3.9 %collective-permute-start.8 = (f32[128,512]{1,0:T(8,128)S(1)}, f32[128,512]{1,0:T(8,128)S(1)}, u32[]{:S(2)}, u32[]{:S(2)}) collective-permute-start(f32[128,512]{1,0:T(8,128)S(1)} %get-tuple-element.30), channel_id=1, source_target_pairs={{0,4},{4,8},{8,12},{1,5},{5,9},{9,13},{2,6},{6,10},{10,14},{3,7},{... | collective-permute-start | bytes 786440 | tf_op jit(solution)/shard_map/ppermute | solution.py:507
  89.5 1.3 %collective-permute-start.9 = (f32[128,512]{1,0:T(8,128)S(1)}, f32[128,512]{1,0:T(8,128)S(1)}, u32[]{:S(2)}, u32[]{:S(2)}) collective-permute-start(f32[128,512]{1,0:T(8,128)S(1)} %get-tuple-element.31), channel_id=1, source_target_pairs={{4,0},{8,4},{12,8},{5,1},{9,5},{13,9},{6,2},{10,6},{14,10},{7,3},{... | collective-permute-start | bytes 786440 | tf_op jit(solution)/shard_map/ppermute | solution.py:508
  90.8 2.1 %collective-permute-done.23 = f32[256,256]{1,0:T(8,128)S(1)} collective-permute-done((f32[256,256]{1,0:T(8,128)S(1)}, f32[256,256]{1,0:T(8,128)S(1)}, u32[]{:S(2)}, u32[]{:S(2)}) %collective-permute-start.23) | collective-permute-done | bytes 262176 | tf_op jit(solution)/shard_map/ppermute | solution.py:422
  93.0 1.5 %collective-permute-start.24 = (f32[512,256]{1,0:T(8,128)S(1)}, f32[512,256]{1,0:T(8,128)S(1)}, u32[]{:S(2)}, u32[]{:S(2)}) collective-permute-start(f32[512,256]{1,0:T(8,128)S(1)} %pad_maximum_fusion.1), channel_id=1, source_target_pairs={{0,2},{1,5},{2,0},{3,7},{4,6},{5,1},{6,4},{7,3},{8,10},{9,13},{10,... | collective-permute-start | bytes 1572872 | tf_op jit(solution)/shard_map/ppermute | solution.py:422
  94.6 0.1 maximum_bitcast_fusion
  94.7 1.9 %collective-permute-done.8.above = f32[128,512]{1,0:T(8,128)S(1)} collective-permute-done((f32[128,512]{1,0:T(8,128)S(1)}, f32[128,512]{1,0:T(8,128)S(1)}, u32[]{:S(2)}, u32[]{:S(2)}) %collective-permute-start.8) | collective-permute-done | bytes 262176 | tf_op jit(solution)/shard_map/ppermute | solution.py:507
  96.6 4.1 %collective-permute-done.9.below = f32[128,512]{1,0:T(8,128)S(1)} collective-permute-done((f32[128,512]{1,0:T(8,128)S(1)}, f32[128,512]{1,0:T(8,128)S(1)}, u32[]{:S(2)}, u32[]{:S(2)}) %collective-permute-start.9) | collective-permute-done | bytes 262176 | tf_op jit(solution)/shard_map/ppermute | solution.py:508
  100.6 1.1 %finish.1 = f32[1,512,512]{2,1,0:T(8,128)} custom-call(f32[512,512]{1,0:T(8,128)S(1)} %get-tuple-element.29.middle, f32[128,512]{1,0:T(8,128)S(1)} %collective-permute-done.8.above, f32[128,512]{1,0:T(8,128)S(1)} %collective-permute-done.9.below), custom_call_target="tpu_custom_call" | custom-call | tf_op jit(solution)/shard_map/finish/pallas_call | solution.py:398
  101.7 0.5 collective-permute-done.24
  102.2 0.1 broadcast_select_fusion.1
  102.3 0.1 slice_bitcast_fusion.2
  102.5 1.5 %pad_maximum_fusion = f32[4,2,256,256]{3,2,1,0:T(8,128)} fusion(f32[1,2,256,256]{3,2,1,0:T(8,128)S(1)} %maximum_bitcast_fusion.3, f32[1,2,256,256]{3,2,1,0:T(8,128)S(1)} %maximum_bitcast_fusion.2, f32[1,2,256,256]{3,2,1,0:T(8,128)S(1)} %get-tuple-element.57, f32[1,2,256,256]{3,2,1,0:T(8,128)S(1)} %get-tuple-element.56), kind=kLoop, calls=%fused_computation | loop fusion | flops 1572864 | bytes 4194304 | tf_op jit(solution)/shard_map/stack | solution.py:516
  (34 shorter events, 0.5 us)
Async XLA Ops:
  0.6 15.3 %copy-start.3 = (s32[1,1,2,2]{3,2,1,0:T(2,128)S(1)}, s32[1,1,2,2]{3,2,1,0:T(2,128)}, u32[]{:S(2)}) copy-start(s32[1,1,2,2]{3,2,1,0:T(2,128)} %param.9) | copy-start | bytes 52
  1.8 11.2 %collective-permute-start.1 = (f32[128,512]{1,0:T(8,128)S(1)}, f32[128,512]{1,0:T(8,128)S(1)}, u32[]{:S(2)}, u32[]{:S(2)}) collective-permute-start(f32[128,512]{1,0:T(8,128)S(1)} %get-tuple-element.21), channel_id=1, source_target_pairs={{4,0},{8,4},{12,8},{5,1},{9,5},{13,9},{6,2},{10,6},{14,10},{7,3},{... | collective-permute-start | bytes 786440 | tf_op jit(solution)/shard_map/ppermute | solution.py:468
  3.1 11.1 %collective-permute-start = (f32[128,512]{1,0:T(8,128)S(1)}, f32[128,512]{1,0:T(8,128)S(1)}, u32[]{:S(2)}, u32[]{:S(2)}) collective-permute-start(f32[128,512]{1,0:T(8,128)S(1)} %get-tuple-element.20), channel_id=1, source_target_pairs={{0,4},{4,8},{8,12},{1,5},{5,9},{9,13},{2,6},{6,10},{10,14},{3,7},{... | collective-permute-start | bytes 786440 | tf_op jit(solution)/shard_map/ppermute | solution.py:467
  8.7 8.4 %collective-permute-start.2 = (f32[512,128]{1,0:T(8,128)S(1)}, f32[512,128]{1,0:T(8,128)S(1)}, u32[]{:S(2)}, u32[]{:S(2)}) collective-permute-start(f32[512,128]{1,0:T(8,128)S(1)} %get-tuple-element.22), channel_id=1, source_target_pairs={{0,2},{2,0},{1,3},{3,1},{4,6},{6,4},{5,7},{7,5},{8,10},{10,8},{9,1... | collective-permute-start | bytes 786440 | tf_op jit(solution)/shard_map/ppermute | solution.py:471
  14.2 5.1 %collective-permute-start.3 = (f32[2,128,128]{2,1,0:T(8,128)S(1)}, f32[2,128,128]{2,1,0:T(8,128)S(1)}, u32[]{:S(2)}, u32[]{:S(2)}) collective-permute-start(f32[2,128,128]{2,1,0:T(8,128)S(1)} %pad_maximum_fusion.4), channel_id=1, source_target_pairs={{0,2},{2,0},{1,3},{3,1},{4,6},{6,4},{5,7},{7,5},{8,10},{10,8},{9,1... | collective-permute-start | bytes 393224 | tf_op jit(solution)/shard_map/ppermute | solution.py:474
  16.0 7.5 %copy-start = (f32[4,2,256,256]{3,2,1,0:T(8,128)S(1)}, f32[4,2,256,256]{3,2,1,0:T(8,128)}, u32[]{:S(2)}) copy-start(f32[4,2,256,256]{3,2,1,0:T(8,128)} %probes.3) | copy-start | bytes 6291460
  21.6 2.0 %collective-permute-start.4 = (f32[2,256,256]{2,1,0:T(8,128)S(1)}, f32[2,256,256]{2,1,0:T(8,128)S(1)}, u32[]{:S(2)}, u32[]{:S(2)}) collective-permute-start(f32[2,256,256]{2,1,0:T(8,128)S(1)} %cut.1.mine), channel_id=1, source_target_pairs={{0,1},{1,0},{2,3},{3,2},{4,5},{5,4},{6,7},{7,6},{8,9},{9,8},{10,11... | collective-permute-start | bytes 1572872 | tf_op jit(solution)/shard_map/ppermute | solution.py:422
  28.0 2.3 %collective-permute-start.5 = (f32[2,256,256]{2,1,0:T(8,128)}, f32[2,256,256]{2,1,0:T(8,128)}, u32[]{:S(2)}, u32[]{:S(2)}) collective-permute-start(f32[2,256,256]{2,1,0:T(8,128)} %get-tuple-element.24.power), channel_id=1, source_target_pairs={{0,1},{1,0},{2,3},{3,2},{4,5},{5,4},{6,7},{7,6},{8,9},{9,8},{10,11... | collective-permute-start | bytes 1572872 | tf_op jit(solution)/shard_map/ppermute | solution.py:422
  38.6 22.6 %copy-start.2 = (f32[512,256]{1,0:T(8,128)S(1)}, f32[512,256]{1,0:T(8,128)}, u32[]{:S(2)}) copy-start(f32[512,256]{1,0:T(8,128)} %get-tuple-element.36) | copy-start | bytes 1572868
  38.6 9.8 %collective-permute-start.10 = (f32[256,256]{1,0:T(8,128)}, f32[256,256]{1,0:T(8,128)S(1)}, u32[]{:S(2)}, u32[]{:S(2)}) collective-permute-start(f32[256,256]{1,0:T(8,128)} %get-tuple-element.33), channel_id=1, source_target_pairs={{0,4},{1,5},{2,6},{3,7},{4,0},{5,1},{6,2},{7,3},{8,12},{9,13},{10,... | collective-permute-start | bytes 786440 | tf_op jit(solution)/shard_map/ppermute | solution.py:422
  41.1 10.0 %collective-permute-start.15 = (f32[256,256]{1,0:T(8,128)}, f32[256,256]{1,0:T(8,128)S(1)}, u32[]{:S(2)}, u32[]{:S(2)}) collective-permute-start(f32[256,256]{1,0:T(8,128)} %get-tuple-element.35), channel_id=1, source_target_pairs={{0,2},{1,3},{2,0},{3,1},{4,6},{5,7},{6,4},{7,5},{8,10},{9,11},{10,... | collective-permute-start | bytes 786440 | tf_op jit(solution)/shard_map/ppermute | solution.py:422
  42.8 18.4 %collective-permute-start.20 = (f32[512,256]{1,0:T(8,128)}, f32[512,256]{1,0:T(8,128)S(1)}, u32[]{:S(2)}, u32[]{:S(2)}) collective-permute-start(f32[512,256]{1,0:T(8,128)} %get-tuple-element.37), channel_id=1, source_target_pairs={{0,2},{1,5},{2,0},{3,7},{4,6},{5,1},{6,4},{7,3},{8,10},{9,13},{10,... | collective-permute-start | bytes 1572872 | tf_op jit(solution)/shard_map/ppermute | solution.py:422
  49.4 12.4 %copy-start.1 = (f32[2,256,256]{2,1,0:T(8,128)S(1)}, f32[2,256,256]{2,1,0:T(8,128)}, u32[]{:S(2)}) copy-start(f32[2,256,256]{2,1,0:T(8,128)} %get-tuple-element.25.mine) | copy-start | bytes 1572868
  49.5 8.4 %collective-permute-start.11 = (f32[128,256]{1,0:T(8,128)S(1)}, f32[128,256]{1,0:T(8,128)S(1)}, u32[]{:S(2)}, u32[]{:S(2)}) collective-permute-start(f32[128,256]{1,0:T(8,128)S(1)} %constant_dynamic-slice_fusion.2), channel_id=1, source_target_pairs={{0,2},{1,3},{2,0},{3,1},{4,6},{5,7},{6,4},{7,5},{8,10},{9,11},{10,... | collective-permute-start | bytes 393224 | tf_op jit(solution)/shard_map/ppermute | solution.py:422
  51.2 10.6 %collective-permute-start.6 = (f32[2,256,256]{2,1,0:T(8,128)}, f32[2,256,256]{2,1,0:T(8,128)S(1)}, u32[]{:S(2)}, u32[]{:S(2)}) collective-permute-start(f32[2,256,256]{2,1,0:T(8,128)} %get-tuple-element.26), channel_id=1, source_target_pairs={{0,1},{1,0},{2,3},{3,2},{4,5},{5,4},{6,7},{7,6},{8,9},{9,8},{10,11... | collective-permute-start | bytes 1572872 | tf_op jit(solution)/shard_map/ppermute | solution.py:422
  52.2 9.2 %collective-permute-start.16 = (f32[128,256]{1,0:T(8,128)S(1)}, f32[128,256]{1,0:T(8,128)S(1)}, u32[]{:S(2)}, u32[]{:S(2)}) collective-permute-start(f32[128,256]{1,0:T(8,128)S(1)} %constant_dynamic-slice_fusion.1), channel_id=1, source_target_pairs={{0,4},{1,5},{2,6},{3,7},{4,0},{5,1},{6,2},{7,3},{8,12},{9,13},{10,... | collective-permute-start | bytes 393224 | tf_op jit(solution)/shard_map/ppermute | solution.py:422
  57.9 10.1 %collective-permute-start.12 = (f32[128,256]{1,0:T(8,128)S(1)}, f32[128,256]{1,0:T(8,128)}, u32[]{:S(2)}, u32[]{:S(2)}) collective-permute-start(f32[128,256]{1,0:T(8,128)S(1)} %dynamic-slice_add_fusion.2), channel_id=1, source_target_pairs={{0,8},{1,9},{2,10},{3,11},{4,12},{5,13},{6,14},{7,15},{8,0},{9,1},... | collective-permute-start | bytes 393224 | tf_op jit(solution)/shard_map/ppermute | solution.py:422
  61.3 11.2 %collective-permute-start.21 = (f32[256,256]{1,0:T(8,128)S(1)}, f32[256,256]{1,0:T(8,128)S(1)}, u32[]{:S(2)}, u32[]{:S(2)}) collective-permute-start(f32[256,256]{1,0:T(8,128)S(1)} %constant_dynamic-slice_fusion), channel_id=1, source_target_pairs={{0,4},{1,3},{2,6},{3,1},{4,0},{5,7},{6,2},{7,5},{8,12},{9,11},{10,... | collective-permute-start | bytes 786440 | tf_op jit(solution)/shard_map/ppermute | solution.py:422
  61.4 9.4 %collective-permute-start.17 = (f32[128,256]{1,0:T(8,128)S(1)}, f32[128,256]{1,0:T(8,128)S(1)}, u32[]{:S(2)}, u32[]{:S(2)}) collective-permute-start(f32[128,256]{1,0:T(8,128)S(1)} %dynamic-slice_add_fusion.1), channel_id=1, source_target_pairs={{0,8},{1,9},{2,10},{3,11},{4,12},{5,13},{6,14},{7,15},{8,0},{9,1},... | collective-permute-start | bytes 393224 | tf_op jit(solution)/shard_map/ppermute | solution.py:422
  63.0 22.4 %collective-permute-start.7 = (f32[768,128]{1,0:T(8,128)S(1)}, f32[768,128]{1,0:T(8,128)S(1)}, u32[]{:S(2)}, u32[]{:S(2)}) collective-permute-start(f32[768,128]{1,0:T(8,128)S(1)} %bitcast.37), channel_id=1, source_target_pairs={{0,2},{2,0},{1,3},{3,1},{4,6},{6,4},{5,7},{7,5},{8,10},{10,8},{9,1... | collective-permute-start | bytes 1179656 | tf_op jit(solution)/shard_map/ppermute | solution.py:505
  68.9 7.1 %collective-permute-start.13 = (f32[128,256]{1,0:T(8,128)S(1)}, f32[128,256]{1,0:T(8,128)S(1)}, u32[]{:S(2)}, u32[]{:S(2)}) collective-permute-start(f32[128,256]{1,0:T(8,128)S(1)} %add.51), channel_id=1, source_target_pairs={{0,2},{1,3},{2,0},{3,1},{4,6},{5,7},{6,4},{7,5},{8,10},{9,11},{10,... | collective-permute-start | bytes 393224 | tf_op jit(solution)/shard_map/ppermute | solution.py:422
  70.8 13.4 %collective-permute-start.18 = (f32[128,256]{1,0:T(8,128)S(1)}, f32[128,256]{1,0:T(8,128)S(1)}, u32[]{:S(2)}, u32[]{:S(2)}) collective-permute-start(f32[128,256]{1,0:T(8,128)S(1)} %add.56), channel_id=1, source_target_pairs={{0,4},{1,5},{2,6},{3,7},{4,0},{5,1},{6,2},{7,3},{8,12},{9,13},{10,... | collective-permute-start | bytes 393224 | tf_op jit(solution)/shard_map/ppermute | solution.py:422
  72.5 11.5 %collective-permute-start.22 = (f32[256,256]{1,0:T(8,128)S(1)}, f32[256,256]{1,0:T(8,128)S(1)}, u32[]{:S(2)}, u32[]{:S(2)}) collective-permute-start(f32[256,256]{1,0:T(8,128)S(1)} %dynamic-slice_add_fusion), channel_id=1, source_target_pairs={{0,8},{1,9},{2,10},{3,11},{4,12},{5,13},{6,14},{7,15},{8,0},{9,1},... | collective-permute-start | bytes 786440 | tf_op jit(solution)/shard_map/ppermute | solution.py:422
  76.0 18.5 %collective-permute-start.14 = (f32[256,256]{1,0:T(8,128)S(1)}, f32[256,256]{1,0:T(8,128)S(1)}, u32[]{:S(2)}, u32[]{:S(2)}) collective-permute-start(f32[256,256]{1,0:T(8,128)S(1)} %pad_maximum_fusion.2), channel_id=1, source_target_pairs={{0,4},{1,5},{2,6},{3,7},{4,0},{5,1},{6,2},{7,3},{8,12},{9,13},{10,... | collective-permute-start | bytes 786440 | tf_op jit(solution)/shard_map/ppermute | solution.py:422
  84.0 8.9 %collective-permute-start.23 = (f32[256,256]{1,0:T(8,128)S(1)}, f32[256,256]{1,0:T(8,128)S(1)}, u32[]{:S(2)}, u32[]{:S(2)}) collective-permute-start(f32[256,256]{1,0:T(8,128)S(1)} %add.61), channel_id=1, source_target_pairs={{0,4},{1,3},{2,6},{3,1},{4,0},{5,7},{6,2},{7,5},{8,12},{9,11},{10,... | collective-permute-start | bytes 786440 | tf_op jit(solution)/shard_map/ppermute | solution.py:422
  84.3 10.3 %collective-permute-start.19 = (f32[256,256]{1,0:T(8,128)S(1)}, f32[256,256]{1,0:T(8,128)S(1)}, u32[]{:S(2)}, u32[]{:S(2)}) collective-permute-start(f32[256,256]{1,0:T(8,128)S(1)} %pad_maximum_fusion.3), channel_id=1, source_target_pairs={{0,2},{1,3},{2,0},{3,1},{4,6},{5,7},{6,4},{7,5},{8,10},{9,11},{10,... | collective-permute-start | bytes 786440 | tf_op jit(solution)/shard_map/ppermute | solution.py:422
  85.6 11.0 %collective-permute-start.8 = (f32[128,512]{1,0:T(8,128)S(1)}, f32[128,512]{1,0:T(8,128)S(1)}, u32[]{:S(2)}, u32[]{:S(2)}) collective-permute-start(f32[128,512]{1,0:T(8,128)S(1)} %get-tuple-element.30), channel_id=1, source_target_pairs={{0,4},{4,8},{8,12},{1,5},{5,9},{9,13},{2,6},{6,10},{10,14},{3,7},{... | collective-permute-start | bytes 786440 | tf_op jit(solution)/shard_map/ppermute | solution.py:507
  89.5 11.1 %collective-permute-start.9 = (f32[128,512]{1,0:T(8,128)S(1)}, f32[128,512]{1,0:T(8,128)S(1)}, u32[]{:S(2)}, u32[]{:S(2)}) collective-permute-start(f32[128,512]{1,0:T(8,128)S(1)} %get-tuple-element.31), channel_id=1, source_target_pairs={{4,0},{8,4},{12,8},{5,1},{9,5},{13,9},{6,2},{10,6},{14,10},{7,3},{... | collective-permute-start | bytes 786440 | tf_op jit(solution)/shard_map/ppermute | solution.py:508
  93.0 9.2 %collective-permute-start.24 = (f32[512,256]{1,0:T(8,128)S(1)}, f32[512,256]{1,0:T(8,128)S(1)}, u32[]{:S(2)}, u32[]{:S(2)}) collective-permute-start(f32[512,256]{1,0:T(8,128)S(1)} %pad_maximum_fusion.1), channel_id=1, source_target_pairs={{0,2},{1,5},{2,0},{3,7},{4,6},{5,1},{6,4},{7,3},{8,10},{9,13},{10,... | collective-permute-start | bytes 1572872 | tf_op jit(solution)/shard_map/ppermute | solution.py:422
